TPU v7x, 32 devices: a whole 2x2x4 slice. The times are simulated.
32 devices in a mesh: section: 4 (over z), dp: 4 (over x, core), space: 2 (over y).
Axes of the slice: x: 2, y: 2, z: 4, core: 2. Of those that a mesh axis runs over, the one named last changes fastest.
Arguments:
- inputs: bfloat16 [4, 2, 4, 2, 8, 8, 256], P('section', None, 'dp', 'space'), may hold values from -6 to 6
- preacts: bfloat16 [4, 2, 4, 2, 8, 8, 256], P('section', None, 'dp', 'space'), may hold values from -6 to 6
- out_grad: bfloat16 [2, 4, 2, 8, 8, 256], P(None, 'dp', 'space'), may hold values from -6 to 6
- conv_w: bfloat16 [4, 27, 256, 256], P('section'), may hold values from -0.078125 to 0.078125
- proj_w: bfloat16 [4, 256, 256], P('section'), may hold values from -0.1875 to 0.1875
Outputs:
- section_grads: bfloat16 [4, 2, 4, 2, 8, 8, 256], P('section', None, 'dp', 'space')
- grad_conv: float32 [4, 256, 27, 256], P('section', 'dp')
- grad_proj: float32 [4, 256, 256], P('section', 'dp')
All inputs are finite; a program needn't handle non-finite values.
Results may differ from a plain program's by a relative error of at most 0.029.
Values may be sent and summed in bfloat16 or wider, within the bound.
No kernel may reach another device: no remote copies, remote signals or barrier semaphores. Data moves between devices by JAX's collectives and lax.ppermute only.
A program may use at most 64 MiB of HBM per device.

v0:
```python
import jax
import jax.numpy as jnp
from jax import lax
from jax.sharding import PartitionSpec as P


def extended(cells, sides, width):
    for axis, dim in sides:
        count = lax.axis_size(axis)
        ends = count - 1
        head = lax.slice_in_dim(cells, 0, width, axis=dim)
        tail = lax.slice_in_dim(cells, cells.shape[dim] - width, cells.shape[dim], axis=dim)
        cells = jnp.concatenate(
            [
                lax.ppermute(tail, axis, [(i, (i + 1) % count) for i in range(ends)]),
                cells,
                lax.ppermute(head, axis, [((i + 1) % count, i) for i in range(ends)]),
            ],
            axis=dim,
        )
    return cells


def passed_along(block, axis, distance):
    devices = range(lax.axis_size(axis))
    route = [(i - distance, i) for i in devices if i - distance in devices]
    return lax.ppermute(block, axis, route)


def tap_offsets():
    return [
        (depth_off, row_off, col_off)
        for depth_off in (-1, 0, 1)
        for row_off in (-1, 0, 1)
        for col_off in (-1, 0, 1)
    ]


def shards(inputs, preacts, out_grad, conv_w, proj_w):
    section_count = lax.axis_size("section")
    section_id = lax.axis_index("section")
    micro_count = inputs.shape[1]
    depth_dev = inputs.shape[3]
    height = inputs.shape[4]
    plane_width = inputs.shape[5]
    channels = inputs.shape[6]
    row_count = depth_dev * height * plane_width
    scale_term = 1.0 / (micro_count * lax.axis_size("dp"))
    offsets = tap_offsets()
    tap_count = len(offsets)
    acts = inputs[0, :, 0]
    pre_acts = preacts[0, :, 0]
    seeds = out_grad[:, 0]
    conv_weight = conv_w[0]
    proj_weight = proj_w[0]
    acts_rim = extended(acts, (("space", 1),), 1)
    acts_ext = jnp.pad(acts_rim, ((0, 0), (0, 0), (1, 1), (1, 1), (0, 0)))
    hidden_all = jnp.maximum(pre_acts, jnp.zeros((), jnp.bfloat16)).reshape(
        micro_count, row_count, channels
    )
    contract_rows = (((0,), (0,)), ((), ()))
    contract_cols = (((1,), (1,)), ((), ()))
    grad_keep_init = jnp.zeros((micro_count, row_count, channels), jnp.bfloat16)
    seed_keep_init = jnp.zeros((micro_count, row_count, channels), jnp.bfloat16)
    outgoing_init = jnp.zeros((depth_dev, height, plane_width, channels), jnp.bfloat16)
    section_init = jnp.zeros((micro_count, depth_dev, height, plane_width, channels), jnp.bfloat16)

    def advance(step_index, carry):
        outgoing, section_out, grad_keep, seed_keep = carry
        incoming = passed_along(outgoing, "section", -1)
        micro_index = step_index - (section_count - 1 - section_id)
        active = (micro_index >= 0) & (micro_index < micro_count)
        safe_index = jnp.clip(micro_index, 0, micro_count - 1)
        seed_now = lax.dynamic_index_in_dim(seeds, safe_index, 0, keepdims=False)
        grad_out = jnp.where(section_id == section_count - 1, seed_now, incoming)
        grad_out_flat = grad_out.reshape(row_count, channels)
        pre_now = lax.dynamic_index_in_dim(pre_acts, safe_index, 0, keepdims=False).reshape(
            row_count, channels
        )

        def open_branch():
            grad_hidden = lax.dot_general(
                grad_out_flat, proj_weight, contract_cols, preferred_element_type=jnp.float32
            )
            masked = jnp.where(pre_now > 0, grad_hidden, jnp.zeros((), jnp.float32))
            return masked.astype(jnp.bfloat16).reshape(depth_dev, height, plane_width, channels)

        def skip_open():
            return jnp.zeros((depth_dev, height, plane_width, channels), jnp.bfloat16)

        grad_pre = lax.cond(active, open_branch, skip_open)
        grad_rim = extended(grad_pre, (("space", 0),), 1)
        grad_ext = jnp.pad(grad_rim, ((0, 0), (1, 1), (1, 1), (0, 0)))
        grad_flat = grad_pre.reshape(row_count, channels)

        def close_branch():
            total = grad_out_flat.astype(jnp.float32)
            for index, (depth_off, row_off, col_off) in enumerate(offsets):
                moved = grad_ext[
                    1 - depth_off : 1 - depth_off + depth_dev,
                    1 - row_off : 1 - row_off + height,
                    1 - col_off : 1 - col_off + plane_width,
                ]
                total = total + lax.dot_general(
                    moved.reshape(row_count, channels),
                    conv_weight[index],
                    contract_cols,
                    preferred_element_type=jnp.float32,
                )
            grad_in = total.astype(jnp.bfloat16).reshape(depth_dev, height, plane_width, channels)
            new_out = lax.dynamic_update_index_in_dim(section_out, grad_in, safe_index, 0)
            new_grad_keep = lax.dynamic_update_index_in_dim(grad_keep, grad_flat, safe_index, 0)
            new_seed_keep = lax.dynamic_update_index_in_dim(seed_keep, grad_out_flat, safe_index, 0)
            return (grad_in, new_out, new_grad_keep, new_seed_keep)

        def skip_close():
            return (jnp.zeros_like(outgoing), section_out, grad_keep, seed_keep)

        return lax.cond(active, close_branch, skip_close)

    init = (outgoing_init, section_init, grad_keep_init, seed_keep_init)
    final = lax.fori_loop(0, section_count + micro_count - 1, advance, init)
    section_out = final[1]
    grad_keep = final[2].reshape(micro_count * row_count, channels)
    seed_keep = final[3].reshape(micro_count * row_count, channels)
    shard_rows = channels // lax.axis_size("dp")
    columns = []
    for depth_off, row_off, col_off in offsets:
        columns.append(
            acts_ext[
                :,
                1 + depth_off : 1 + depth_off + depth_dev,
                1 + row_off : 1 + row_off + height,
                1 + col_off : 1 + col_off + plane_width,
            ]
        )
    unfolded = jnp.stack(columns, axis=-1).reshape(micro_count * row_count, channels * tap_count)
    conv_full = (
        lax.dot_general(unfolded, grad_keep, contract_rows, preferred_element_type=jnp.float32)
        * scale_term
    )
    conv_full = conv_full.reshape(channels, tap_count * channels)
    proj_full = (
        lax.dot_general(
            hidden_all.reshape(micro_count * row_count, channels),
            seed_keep,
            contract_rows,
            preferred_element_type=jnp.float32,
        )
        * scale_term
    )
    conv_shard, proj_shard = (
        lax.psum_scatter(
            conv_full.astype(jnp.bfloat16), "dp", scatter_dimension=0, tiled=True
        ).astype(jnp.float32),
        lax.psum_scatter(
            proj_full.astype(jnp.bfloat16), "dp", scatter_dimension=0, tiled=True
        ).astype(jnp.float32),
    )
    conv_sum, proj_sum = (
        lax.psum(conv_shard.astype(jnp.bfloat16), "space").astype(jnp.float32),
        lax.psum(proj_shard.astype(jnp.bfloat16), "space").astype(jnp.float32),
    )
    grad_conv = conv_sum.reshape(shard_rows, tap_count, channels)[None]
    grad_proj = proj_sum[None]
    section_grads = section_out[None, :, None]
    return (section_grads, grad_conv, grad_proj)


def solution(mesh):
    placed = (
        P("section", None, "dp", "space", None, None, None),
        P("section", None, "dp", "space", None, None, None),
        P(None, "dp", "space", None, None, None),
        P("section", None, None, None),
        P("section", None, None),
    )
    return jax.shard_map(
        shards,
        mesh=mesh,
        in_specs=placed,
        out_specs=(
            P("section", None, "dp", "space", None, None, None),
            P("section", "dp", None, None),
            P("section", "dp", None),
        ),
        check_vma=False,
    )
```

profile of v0, /device:TPU:0, one launch (start us, length us, event | category | flops | bytes accessed | tf_op | source)
XLA Modules:
  0.0 322.1 jit_solution(12988815061634251787)
XLA Ops:
  7.2 4.9 %collective-permute-start.3 = (bf16[2,1,8,8,256]{4,3,2,0,1:T(8,128)(2,1)}, bf16[2,1,8,8,256]{4,3,2,0,1:T(8,128)(2,1)S(1)}, u32[]{:S(2)}, u32[]{:S(2)}) collective-permute-start(bf16[2,1,8,8,256]{4,3,2,0,1:T(8,128)(2,1)} %bitcast.315), channel_id=1, source_target_pairs={{0,1},{2,3},{4,5},{6,7},{8,9},{10,11},{12,13},{14,15},{16,17},{18,... | collective-permute-start | bytes 196616 | tf_op jit(solution)/shard_map/ppermute | solution.py:15
  12.1 1.3 collective-permute-start.4
  14.3 4.2 %collective-permute-done.4 = bf16[2,1,8,8,256]{4,3,2,0,1:T(8,128)(2,1)S(1)} collective-permute-done((bf16[2,1,8,8,256]{4,3,2,0,1:T(8,128)(2,1)}, bf16[2,1,8,8,256]{4,3,2,0,1:T(8,128)(2,1)S(1)}, u32[]{:S(2)}, u32[]{:S(2)}) %collective-permute-start.4) | collective-permute-done | bytes 65568 | tf_op jit(solution)/shard_map/ppermute | solution.py:17
  20.1 6.3 %copy.8 = bf16[2,1,8,8,256,27]{5,4,3,2,0,1:T(8,128)(2,1)} copy(bf16[2,1,8,8,256,27]{4,3,2,0,5,1:T(8,128)(2,1)S(1)} %fusion.143) | data formatting | bytes 3538944 | tf_op jit(solution)/shard_map/stack | solution.py:137
  26.4 11.8 %reshape.172 = bf16[128,6912]{1,0:T(8,128)(2,1)} reshape(bf16[2,1,8,8,256,27]{5,4,3,2,0,1:T(8,128)(2,1)} %copy.8) | data formatting | bytes 3538944 | tf_op jit(solution)/shard_map/reshape | solution.py:137
  38.9 161.0 %while.21 = (s32[]{:T(128)}, bf16[1,8,8,256]{3,2,1,0:T(8,128)(2,1)}, bf16[2,1,8,8,256]{4,3,2,1,0:T(8,128)(2,1)S(1)}, bf16[2,64,256]{2,1,0:T(8,128)(2,1)S(1)}, bf...) while((s32[]{:T(128)}, ...), condition=%wide.region_5.6_spmd, body=%wide.region_0.5_spmd.sunk | while | flops 235520000 | bytes 24773168 | solution.py:122
  38.9 1.3 collective-permute-start
  40.2 4.7 %collective-permute-done = bf16[1,8,8,256]{3,2,1,0:T(8,128)(2,1)S(1)} collective-permute-done((bf16[1,8,8,256]{3,2,1,0:T(8,128)(2,1)}, bf16[1,8,8,256]{3,2,1,0:T(8,128)(2,1)S(1)}, u32[]{:S(2)}, u32[]{:S(2)}) %collective-permute-start) | collective-permute-done | bytes 32800 | tf_op jit(solution)/shard_map/while/body/eval_jaxpr/ppermute | solution.py:27
  45.5 1.3 collective-permute-start.1
  46.8 4.5 %collective-permute-start.2 = (bf16[1,8,8,256]{3,2,1,0:T(8,128)(2,1)}, bf16[1,8,8,256]{3,2,1,0:T(8,128)(2,1)S(1)}, u32[]{:S(2)}, u32[]{:S(2)}) collective-permute-start(bf16[1,8,8,256]{3,2,1,0:T(8,128)(2,1)} %get-tuple-element.470), channel_id=1, source_target_pairs={{0,1},{2,3},{4,5},{6,7},{8,9},{10,11},{12,13},{14,15},{16,17},{18,... | collective-permute-start | bytes 98312 | tf_op jit(solution)/shard_map/while/body/eval_jaxpr/ppermute | solution.py:15
  51.6 1.7 collective-permute-done.2
  54.7 1.3 collective-permute-start
  56.0 4.7 %collective-permute-done = bf16[1,8,8,256]{3,2,1,0:T(8,128)(2,1)S(1)} collective-permute-done((bf16[1,8,8,256]{3,2,1,0:T(8,128)(2,1)}, bf16[1,8,8,256]{3,2,1,0:T(8,128)(2,1)S(1)}, u32[]{:S(2)}, u32[]{:S(2)}) %collective-permute-start) | collective-permute-done | bytes 32800 | tf_op jit(solution)/shard_map/while/body/eval_jaxpr/ppermute | solution.py:27
  61.3 1.3 collective-permute-start.1
  62.6 4.5 %collective-permute-start.2 = (bf16[1,8,8,256]{3,2,1,0:T(8,128)(2,1)}, bf16[1,8,8,256]{3,2,1,0:T(8,128)(2,1)S(1)}, u32[]{:S(2)}, u32[]{:S(2)}) collective-permute-start(bf16[1,8,8,256]{3,2,1,0:T(8,128)(2,1)} %get-tuple-element.470), channel_id=1, source_target_pairs={{0,1},{2,3},{4,5},{6,7},{8,9},{10,11},{12,13},{14,15},{16,17},{18,... | collective-permute-start | bytes 98312 | tf_op jit(solution)/shard_map/while/body/eval_jaxpr/ppermute | solution.py:15
  67.3 1.7 collective-permute-done.2
  70.5 1.3 collective-permute-start
  71.8 4.7 %collective-permute-done = bf16[1,8,8,256]{3,2,1,0:T(8,128)(2,1)S(1)} collective-permute-done((bf16[1,8,8,256]{3,2,1,0:T(8,128)(2,1)}, bf16[1,8,8,256]{3,2,1,0:T(8,128)(2,1)S(1)}, u32[]{:S(2)}, u32[]{:S(2)}) %collective-permute-start) | collective-permute-done | bytes 32800 | tf_op jit(solution)/shard_map/while/body/eval_jaxpr/ppermute | solution.py:27
  77.1 1.3 collective-permute-start.1
  78.4 4.5 %collective-permute-start.2 = (bf16[1,8,8,256]{3,2,1,0:T(8,128)(2,1)}, bf16[1,8,8,256]{3,2,1,0:T(8,128)(2,1)S(1)}, u32[]{:S(2)}, u32[]{:S(2)}) collective-permute-start(bf16[1,8,8,256]{3,2,1,0:T(8,128)(2,1)} %get-tuple-element.470), channel_id=1, source_target_pairs={{0,1},{2,3},{4,5},{6,7},{8,9},{10,11},{12,13},{14,15},{16,17},{18,... | collective-permute-start | bytes 98312 | tf_op jit(solution)/shard_map/while/body/eval_jaxpr/ppermute | solution.py:15
  83.1 1.7 collective-permute-done.2
  86.3 1.3 collective-permute-start
  87.6 52.4 %collective-permute-done = bf16[1,8,8,256]{3,2,1,0:T(8,128)(2,1)S(1)} collective-permute-done((bf16[1,8,8,256]{3,2,1,0:T(8,128)(2,1)}, bf16[1,8,8,256]{3,2,1,0:T(8,128)(2,1)S(1)}, u32[]{:S(2)}, u32[]{:S(2)}) %collective-permute-start) | collective-permute-done | bytes 32800 | tf_op jit(solution)/shard_map/while/body/eval_jaxpr/ppermute | solution.py:27
  140.0 1.6 conditional.4
  141.6 1.3 collective-permute-start.1
  142.9 4.5 %collective-permute-start.2 = (bf16[1,8,8,256]{3,2,1,0:T(8,128)(2,1)}, bf16[1,8,8,256]{3,2,1,0:T(8,128)(2,1)S(1)}, u32[]{:S(2)}, u32[]{:S(2)}) collective-permute-start(bf16[1,8,8,256]{3,2,1,0:T(8,128)(2,1)} %get-tuple-element.470), channel_id=1, source_target_pairs={{0,1},{2,3},{4,5},{6,7},{8,9},{10,11},{12,13},{14,15},{16,17},{18,... | collective-permute-start | bytes 98312 | tf_op jit(solution)/shard_map/while/body/eval_jaxpr/ppermute | solution.py:15
  147.6 1.7 collective-permute-done.2
  150.1 16.8 %conditional.5 = (bf16[1,8,8,256]{3,2,1,0:T(8,128)(2,1)}, bf16[2,1,8,8,256]{4,3,2,1,0:T(8,128)(2,1)S(1)}, bf16[2,64,256]{2,1,0:T(8,128)(2,1)S(1)}, bf16[2,64,256]{2,1,0:T(8,128)(2,1)S(1)}) conditional(s32[]{:T(128)} %convert_element_type.57, (bf16[2,1,8,8,256]{4,3,2,1,0:T(8,128)(2,1)S(1)}, bf16[2,64,256]{2,1,0:T(8,128)(2,1)S(1)}, ...), branch_computations={%region_3.3_spmd, %region_4.4_spmd} | conditional | flops 226967552 | bytes 23789670 | solution.py:119
  150.1 1.2 convolution_add_fusion.26
  165.1 1.7 bitcast_dynamic-update-slice_fusion.2
  166.9 1.3 collective-permute-start
  168.2 4.7 %collective-permute-done = bf16[1,8,8,256]{3,2,1,0:T(8,128)(2,1)S(1)} collective-permute-done((bf16[1,8,8,256]{3,2,1,0:T(8,128)(2,1)}, bf16[1,8,8,256]{3,2,1,0:T(8,128)(2,1)S(1)}, u32[]{:S(2)}, u32[]{:S(2)}) %collective-permute-start) | collective-permute-done | bytes 32800 | tf_op jit(solution)/shard_map/while/body/eval_jaxpr/ppermute | solution.py:27
  172.9 1.6 conditional.4
  174.5 1.3 collective-permute-start.1
  175.8 4.5 %collective-permute-start.2 = (bf16[1,8,8,256]{3,2,1,0:T(8,128)(2,1)}, bf16[1,8,8,256]{3,2,1,0:T(8,128)(2,1)S(1)}, u32[]{:S(2)}, u32[]{:S(2)}) collective-permute-start(bf16[1,8,8,256]{3,2,1,0:T(8,128)(2,1)} %get-tuple-element.470), channel_id=1, source_target_pairs={{0,1},{2,3},{4,5},{6,7},{8,9},{10,11},{12,13},{14,15},{16,17},{18,... | collective-permute-start | bytes 98312 | tf_op jit(solution)/shard_map/while/body/eval_jaxpr/ppermute | solution.py:15
  180.5 1.7 collective-permute-done.2
  183.0 16.8 %conditional.5 = (bf16[1,8,8,256]{3,2,1,0:T(8,128)(2,1)}, bf16[2,1,8,8,256]{4,3,2,1,0:T(8,128)(2,1)S(1)}, bf16[2,64,256]{2,1,0:T(8,128)(2,1)S(1)}, bf16[2,64,256]{2,1,0:T(8,128)(2,1)S(1)}) conditional(s32[]{:T(128)} %convert_element_type.57, (bf16[2,1,8,8,256]{4,3,2,1,0:T(8,128)(2,1)S(1)}, bf16[2,64,256]{2,1,0:T(8,128)(2,1)S(1)}, ...), branch_computations={%region_3.3_spmd, %region_4.4_spmd} | conditional | flops 226967552 | bytes 23789670 | solution.py:119
  183.1 1.2 convolution_add_fusion.26
  191.9 1.1 convolution_add_fusion.18
  198.1 1.7 bitcast_dynamic-update-slice_fusion.2
  200.5 2.6 fusion.135
  203.1 4.9 %convert_element_type.49 = bf16[256,6912]{1,0:T(8,128)(2,1)} reshape(bf16[6912,256]{1,0:T(8,128)(2,1)S(1)} %fusion.135) | data formatting | bytes 7077888 | tf_op jit(solution)/shard_map/convert_element_type | solution.py:154
  209.8 37.7 %reduce-scatter.3.cloned.1.call-done = bf16[64,6912]{1,0:T(8,128)(2,1)} async-done(((bf16[256,6912]{1,0:T(8,128)(2,1)}), bf16[64,6912]{1,0:T(8,128)(2,1)}) %reduce-scatter.3.cloned.1.call-update) | async-done | bytes 884752 | tf_op jit(solution)/shard_map/reduce_scatter | solution.py:153
  247.5 2.3 broadcast_in_dim_reshape.6
  249.8 19.8 %reduce-scatter.5.cloned.1.call-done = bf16[64,256]{1,0:T(8,128)(2,1)} async-done(((bf16[256,256]{1,0:T(8,128)(2,1)}), bf16[64,256]{1,0:T(8,128)(2,1)}) %reduce-scatter.5.cloned.1.call-update) | async-done | bytes 32784 | tf_op jit(solution)/shard_map/reduce_scatter | solution.py:156
  269.7 8.9 %psum.15 = bf16[1,64,256]{2,1,0:T(8,128)(2,1)S(1)} all-reduce(bf16[1,64,256]{2,1,0:T(8,128)(2,1)} %bitcast.319), channel_id=1, replica_groups=mesh['section'=4,'dp'=4,'space'=2] {'space'}, use_global_device_ids=true, to_apply=%region_9.10 | all-reduce | flops 16384 | bytes 65536 | tf_op jit(solution)/shard_map/psum | solution.py:162
  279.3 33.4 %all-reduce.4.cloned.1.call-done = bf16[1,64,27,256]{3,2,1,0:T(8,128)(2,1)} async-done(((bf16[1,64,27,256]{3,2,1,0:T(8,128)(2,1)}), bf16[1,64,27,256]{3,2,1,0:T(8,128)(2,1)}) %all-reduce.4.cloned.1.call-update) | async-done | bytes 884752 | tf_op jit(solution)/shard_map/psum | solution.py:161
  312.6 3.0 copy.9
  (149 shorter events, 48.0 us)
Async XLA Ops:
  7.2 12.6 %copy-start.8 = (bf16[1,2,1,1,8,8,256]{6,5,4,3,2,1,0:T(8,128)(2,1)S(1)}, bf16[1,2,1,1,8,8,256]{6,5,4,3,2,1,0:T(8,128)(2,1)}, u32[]{:S(2)}) copy-start(bf16[1,2,1,1,8,8,256]{6,5,4,3,2,1,0:T(8,128)(2,1)} %param.11) | copy-start | bytes 196612
  7.2 240.3 %reduce-scatter.3.cloned.1.call-start = ((), (), s32[]{:S(2)}) async-start(), calls=%async_computation.2 | async-start | bytes 4423680 | tf_op jit(solution)/shard_map/reduce_scatter | solution.py:153
  7.2 7.1 %collective-permute-start.3 = (bf16[2,1,8,8,256]{4,3,2,0,1:T(8,128)(2,1)}, bf16[2,1,8,8,256]{4,3,2,0,1:T(8,128)(2,1)S(1)}, u32[]{:S(2)}, u32[]{:S(2)}) collective-permute-start(bf16[2,1,8,8,256]{4,3,2,0,1:T(8,128)(2,1)} %bitcast.315), channel_id=1, source_target_pairs={{0,1},{2,3},{4,5},{6,7},{8,9},{10,11},{12,13},{14,15},{16,17},{18,... | collective-permute-start | bytes 196616 | tf_op jit(solution)/shard_map/ppermute | solution.py:15
  12.1 6.4 %collective-permute-start.4 = (bf16[2,1,8,8,256]{4,3,2,0,1:T(8,128)(2,1)}, bf16[2,1,8,8,256]{4,3,2,0,1:T(8,128)(2,1)S(1)}, u32[]{:S(2)}, u32[]{:S(2)}) collective-permute-start(bf16[2,1,8,8,256]{4,3,2,0,1:T(8,128)(2,1)} %bitcast.316), channel_id=1, source_target_pairs={{1,0},{3,2},{5,4},{7,6},{9,8},{11,10},{13,12},{15,14},{17,16},{19,... | collective-permute-start | bytes 196616 | tf_op jit(solution)/shard_map/ppermute | solution.py:17
  26.4 12.5 %copy-start.1 = (bf16[1,256,256]{2,1,0:T(8,128)(2,1)S(1)}, bf16[1,256,256]{2,1,0:T(8,128)(2,1)}, u32[]{:S(2)}) copy-start(bf16[1,256,256]{2,1,0:T(8,128)(2,1)} %param.15) | copy-start | bytes 393220
  26.4 12.5 %copy-start.2 = (bf16[1,2,1,1,8,8,256]{6,5,4,3,2,1,0:T(8,128)(2,1)S(1)}, bf16[1,2,1,1,8,8,256]{6,5,4,3,2,1,0:T(8,128)(2,1)}, u32[]{:S(2)}) copy-start(bf16[1,2,1,1,8,8,256]{6,5,4,3,2,1,0:T(8,128)(2,1)} %param.12) | copy-start | bytes 196612
  26.4 12.5 %copy-start.4 = (bf16[2,1,1,8,8,256]{5,4,3,2,1,0:T(8,128)(2,1)S(1)}, bf16[2,1,1,8,8,256]{5,4,3,2,1,0:T(8,128)(2,1)}, u32[]{:S(2)}) copy-start(bf16[2,1,1,8,8,256]{5,4,3,2,1,0:T(8,128)(2,1)} %param.13) | copy-start | bytes 196612
  38.9 6.0 %collective-permute-start = (bf16[1,8,8,256]{3,2,1,0:T(8,128)(2,1)}, bf16[1,8,8,256]{3,2,1,0:T(8,128)(2,1)S(1)}, u32[]{:S(2)}, u32[]{:S(2)}) collective-permute-start(bf16[1,8,8,256]{3,2,1,0:T(8,128)(2,1)} %get-tuple-element.503), channel_id=1, source_target_pairs={{8,0},{16,8},{24,16},{9,1},{17,9},{25,17},{10,2},{18,10},{26,18},{... | collective-permute-start | bytes 98312 | tf_op jit(solution)/shard_map/while/body/eval_jaxpr/ppermute | solution.py:27
  45.5 6.0 %collective-permute-start.1 = (bf16[1,8,8,256]{3,2,1,0:T(8,128)(2,1)}, bf16[1,8,8,256]{3,2,1,0:T(8,128)(2,1)S(1)}, u32[]{:S(2)}, u32[]{:S(2)}) collective-permute-start(bf16[1,8,8,256]{3,2,1,0:T(8,128)(2,1)} %get-tuple-element.470), channel_id=1, source_target_pairs={{1,0},{3,2},{5,4},{7,6},{9,8},{11,10},{13,12},{15,14},{17,16},{19,... | collective-permute-start | bytes 98312 | tf_op jit(solution)/shard_map/while/body/eval_jaxpr/ppermute | solution.py:17
  46.8 6.4 %collective-permute-start.2 = (bf16[1,8,8,256]{3,2,1,0:T(8,128)(2,1)}, bf16[1,8,8,256]{3,2,1,0:T(8,128)(2,1)S(1)}, u32[]{:S(2)}, u32[]{:S(2)}) collective-permute-start(bf16[1,8,8,256]{3,2,1,0:T(8,128)(2,1)} %get-tuple-element.470), channel_id=1, source_target_pairs={{0,1},{2,3},{4,5},{6,7},{8,9},{10,11},{12,13},{14,15},{16,17},{18,... | collective-permute-start | bytes 98312 | tf_op jit(solution)/shard_map/while/body/eval_jaxpr/ppermute | solution.py:15
  54.7 6.0 %collective-permute-start = (bf16[1,8,8,256]{3,2,1,0:T(8,128)(2,1)}, bf16[1,8,8,256]{3,2,1,0:T(8,128)(2,1)S(1)}, u32[]{:S(2)}, u32[]{:S(2)}) collective-permute-start(bf16[1,8,8,256]{3,2,1,0:T(8,128)(2,1)} %get-tuple-element.503), channel_id=1, source_target_pairs={{8,0},{16,8},{24,16},{9,1},{17,9},{25,17},{10,2},{18,10},{26,18},{... | collective-permute-start | bytes 98312 | tf_op jit(solution)/shard_map/while/body/eval_jaxpr/ppermute | solution.py:27
  61.3 6.0 %collective-permute-start.1 = (bf16[1,8,8,256]{3,2,1,0:T(8,128)(2,1)}, bf16[1,8,8,256]{3,2,1,0:T(8,128)(2,1)S(1)}, u32[]{:S(2)}, u32[]{:S(2)}) collective-permute-start(bf16[1,8,8,256]{3,2,1,0:T(8,128)(2,1)} %get-tuple-element.470), channel_id=1, source_target_pairs={{1,0},{3,2},{5,4},{7,6},{9,8},{11,10},{13,12},{15,14},{17,16},{19,... | collective-permute-start | bytes 98312 | tf_op jit(solution)/shard_map/while/body/eval_jaxpr/ppermute | solution.py:17
  62.6 6.4 %collective-permute-start.2 = (bf16[1,8,8,256]{3,2,1,0:T(8,128)(2,1)}, bf16[1,8,8,256]{3,2,1,0:T(8,128)(2,1)S(1)}, u32[]{:S(2)}, u32[]{:S(2)}) collective-permute-start(bf16[1,8,8,256]{3,2,1,0:T(8,128)(2,1)} %get-tuple-element.470), channel_id=1, source_target_pairs={{0,1},{2,3},{4,5},{6,7},{8,9},{10,11},{12,13},{14,15},{16,17},{18,... | collective-permute-start | bytes 98312 | tf_op jit(solution)/shard_map/while/body/eval_jaxpr/ppermute | solution.py:15
  70.5 6.0 %collective-permute-start = (bf16[1,8,8,256]{3,2,1,0:T(8,128)(2,1)}, bf16[1,8,8,256]{3,2,1,0:T(8,128)(2,1)S(1)}, u32[]{:S(2)}, u32[]{:S(2)}) collective-permute-start(bf16[1,8,8,256]{3,2,1,0:T(8,128)(2,1)} %get-tuple-element.503), channel_id=1, source_target_pairs={{8,0},{16,8},{24,16},{9,1},{17,9},{25,17},{10,2},{18,10},{26,18},{... | collective-permute-start | bytes 98312 | tf_op jit(solution)/shard_map/while/body/eval_jaxpr/ppermute | solution.py:27
  77.1 6.0 %collective-permute-start.1 = (bf16[1,8,8,256]{3,2,1,0:T(8,128)(2,1)}, bf16[1,8,8,256]{3,2,1,0:T(8,128)(2,1)S(1)}, u32[]{:S(2)}, u32[]{:S(2)}) collective-permute-start(bf16[1,8,8,256]{3,2,1,0:T(8,128)(2,1)} %get-tuple-element.470), channel_id=1, source_target_pairs={{1,0},{3,2},{5,4},{7,6},{9,8},{11,10},{13,12},{15,14},{17,16},{19,... | collective-permute-start | bytes 98312 | tf_op jit(solution)/shard_map/while/body/eval_jaxpr/ppermute | solution.py:17
  78.4 6.4 %collective-permute-start.2 = (bf16[1,8,8,256]{3,2,1,0:T(8,128)(2,1)}, bf16[1,8,8,256]{3,2,1,0:T(8,128)(2,1)S(1)}, u32[]{:S(2)}, u32[]{:S(2)}) collective-permute-start(bf16[1,8,8,256]{3,2,1,0:T(8,128)(2,1)} %get-tuple-element.470), channel_id=1, source_target_pairs={{0,1},{2,3},{4,5},{6,7},{8,9},{10,11},{12,13},{14,15},{16,17},{18,... | collective-permute-start | bytes 98312 | tf_op jit(solution)/shard_map/while/body/eval_jaxpr/ppermute | solution.py:15
  86.3 53.7 %collective-permute-start = (bf16[1,8,8,256]{3,2,1,0:T(8,128)(2,1)}, bf16[1,8,8,256]{3,2,1,0:T(8,128)(2,1)S(1)}, u32[]{:S(2)}, u32[]{:S(2)}) collective-permute-start(bf16[1,8,8,256]{3,2,1,0:T(8,128)(2,1)} %get-tuple-element.503), channel_id=1, source_target_pairs={{8,0},{16,8},{24,16},{9,1},{17,9},{25,17},{10,2},{18,10},{26,18},{... | collective-permute-start | bytes 98312 | tf_op jit(solution)/shard_map/while/body/eval_jaxpr/ppermute | solution.py:27
  141.6 6.0 %collective-permute-start.1 = (bf16[1,8,8,256]{3,2,1,0:T(8,128)(2,1)}, bf16[1,8,8,256]{3,2,1,0:T(8,128)(2,1)S(1)}, u32[]{:S(2)}, u32[]{:S(2)}) collective-permute-start(bf16[1,8,8,256]{3,2,1,0:T(8,128)(2,1)} %get-tuple-element.470), channel_id=1, source_target_pairs={{1,0},{3,2},{5,4},{7,6},{9,8},{11,10},{13,12},{15,14},{17,16},{19,... | collective-permute-start | bytes 98312 | tf_op jit(solution)/shard_map/while/body/eval_jaxpr/ppermute | solution.py:17
  142.9 6.4 %collective-permute-start.2 = (bf16[1,8,8,256]{3,2,1,0:T(8,128)(2,1)}, bf16[1,8,8,256]{3,2,1,0:T(8,128)(2,1)S(1)}, u32[]{:S(2)}, u32[]{:S(2)}) collective-permute-start(bf16[1,8,8,256]{3,2,1,0:T(8,128)(2,1)} %get-tuple-element.470), channel_id=1, source_target_pairs={{0,1},{2,3},{4,5},{6,7},{8,9},{10,11},{12,13},{14,15},{16,17},{18,... | collective-permute-start | bytes 98312 | tf_op jit(solution)/shard_map/while/body/eval_jaxpr/ppermute | solution.py:15
  150.1 12.2 %copy-start = (bf16[27,256,256]{2,1,0:T(8,128)(2,1)S(1)}, bf16[27,256,256]{2,1,0:T(8,128)(2,1)}, u32[]{:S(2)}) copy-start(bf16[27,256,256]{2,1,0:T(8,128)(2,1)} %get-tuple-element.335) | copy-start | bytes 10616836 | tf_op jit(solution)/shard_map/while/body/eval_jaxpr/cond
  166.9 6.0 %collective-permute-start = (bf16[1,8,8,256]{3,2,1,0:T(8,128)(2,1)}, bf16[1,8,8,256]{3,2,1,0:T(8,128)(2,1)S(1)}, u32[]{:S(2)}, u32[]{:S(2)}) collective-permute-start(bf16[1,8,8,256]{3,2,1,0:T(8,128)(2,1)} %get-tuple-element.503), channel_id=1, source_target_pairs={{8,0},{16,8},{24,16},{9,1},{17,9},{25,17},{10,2},{18,10},{26,18},{... | collective-permute-start | bytes 98312 | tf_op jit(solution)/shard_map/while/body/eval_jaxpr/ppermute | solution.py:27
  174.5 6.0 %collective-permute-start.1 = (bf16[1,8,8,256]{3,2,1,0:T(8,128)(2,1)}, bf16[1,8,8,256]{3,2,1,0:T(8,128)(2,1)S(1)}, u32[]{:S(2)}, u32[]{:S(2)}) collective-permute-start(bf16[1,8,8,256]{3,2,1,0:T(8,128)(2,1)} %get-tuple-element.470), channel_id=1, source_target_pairs={{1,0},{3,2},{5,4},{7,6},{9,8},{11,10},{13,12},{15,14},{17,16},{19,... | collective-permute-start | bytes 98312 | tf_op jit(solution)/shard_map/while/body/eval_jaxpr/ppermute | solution.py:17
  175.8 6.4 %collective-permute-start.2 = (bf16[1,8,8,256]{3,2,1,0:T(8,128)(2,1)}, bf16[1,8,8,256]{3,2,1,0:T(8,128)(2,1)S(1)}, u32[]{:S(2)}, u32[]{:S(2)}) collective-permute-start(bf16[1,8,8,256]{3,2,1,0:T(8,128)(2,1)} %get-tuple-element.470), channel_id=1, source_target_pairs={{0,1},{2,3},{4,5},{6,7},{8,9},{10,11},{12,13},{14,15},{16,17},{18,... | collective-permute-start | bytes 98312 | tf_op jit(solution)/shard_map/while/body/eval_jaxpr/ppermute | solution.py:15
  183.1 12.2 %copy-start = (bf16[27,256,256]{2,1,0:T(8,128)(2,1)S(1)}, bf16[27,256,256]{2,1,0:T(8,128)(2,1)}, u32[]{:S(2)}) copy-start(bf16[27,256,256]{2,1,0:T(8,128)(2,1)} %get-tuple-element.335) | copy-start | bytes 10616836 | tf_op jit(solution)/shard_map/while/body/eval_jaxpr/cond
  199.8 0.6 copy-start.5
  199.9 0.6 copy-start.6
  199.9 0.7 copy-start.9
  208.0 0.8 copy-start.3
  208.0 0.9 copy-start.7
  208.0 61.7 %reduce-scatter.5.cloned.1.call-start = ((), (), s32[]{:S(2)}) async-start(), calls=%async_computation.4 | async-start | bytes 163840 | tf_op jit(solution)/shard_map/reduce_scatter | solution.py:156
  209.7 102.9 %all-reduce.4.cloned.1.call-start = ((), (), s32[]{:S(2)}) async-start(), calls=%async_computation.3 | async-start | bytes 2097152 | tf_op jit(solution)/shard_map/psum | solution.py:161
Sparse Core Ops, SparseCore 0:
  208.1 39.3 reduce-scatter.2
  250.0 19.5 reduce-scatter.4
  272.5 40.0 all-reduce.3
where the time goes:
time: 324 us; the launch traced here: 322 us
  waiting for transfers between devices  177 us (55%)
  starting transfers between devices  41.8 us (13%)
  matrix products  38.5 us (12%)
  local copies, waits for them, and re-layouts  36.1 us (11%)
  between operations  14.1 us (4%)
  blocking collectives  8.95 us (3%)
  other arithmetic  5.54 us (2%)
    ppermute x5, waiting for transfers between devices, passed_along(): return lax.ppermute(block, axis, route)  71.2 us
    reduce_scatter x1, waiting for transfers between devices, shards(): lax.psum_scatter(conv_full.astype(jnp.bfloat16), 'dp', scatter_dimension=...  37.7 us
    dot_general x54, matrix products, close_branch(): lax.dot_general(moved.reshape(row_count, channels), conv_weight[index], c...  33.4 us
    psum x1, waiting for transfers between devices, shards(): lax.psum(conv_shard.astype(jnp.bfloat16), 'space').astype(jnp.float32)  33.4 us
    ppermute x6, starting transfers between devices, extended(): lax.ppermute(tail, axis, [(i, (i + 1) % count) for i in range(ends)])  27.6 us
    reduce_scatter x1, waiting for transfers between devices, shards(): lax.psum_scatter(proj_full.astype(jnp.bfloat16), 'dp', scatter_dimension=...  19.8 us
    reshape x1, local copies, waits for them, and re-layouts, shards(): jnp.stack(columns, axis=-1)  11.8 us
    ppermute x6, waiting for transfers between devices, extended(): lax.ppermute(tail, axis, [(i, (i + 1) % count) for i in range(ends)])  9.53 us
  transfers between devices with their start and end apart: 20, of which 20 were waited for; matrix products, arithmetic and copies ran while one was open for 1% of the time, Pallas kernels for 0%

commit v1 on v0

v1 whole, which is shorter than its diff:
```python
import functools

import jax
import jax.numpy as jnp
from jax import lax
from jax.experimental import pallas as pl
from jax.experimental.pallas import tpu as pltpu
from jax.sharding import PartitionSpec as P

SIDE = (-1, 0, 1)
TAPS = [(depth, row, col) for depth in SIDE for row in SIDE for col in SIDE]
CONTRACT_LANES = (((1,), (1,)), ((), ()))
VMEM_LIMIT = 16 * 1024 * 1024


def peer(here, distance, count, back=False):
    if count & (count - 1) == 0:
        return here ^ distance
    return (here + (count - distance if back else distance)) % count


def moved(block, crop_distance, slab_distance):
    crops, slabs = lax.axis_size("dp"), lax.axis_size("space")
    pairs = [
        (peer(i, crop_distance, crops) * slabs + peer(j, slab_distance, slabs), i * slabs + j)
        for i in range(crops)
        for j in range(slabs)
    ]
    return lax.ppermute(block, ("dp", "space"), pairs)


def hop_pairs(count, step):
    sender = count - step
    if sender % 2 == 0 or count % 2 == 1:
        return [((i + 1) % count, i) for i in range(count)]
    return [(i ^ 1, i) for i in range(count)]


def shifts(block, extent, sign):
    depth_all, height, width = extent
    lanes = block.shape[1]
    place = lax.broadcasted_iota(jnp.int32, (1, lanes), 1)
    col, row = place % width, (place // width) % height
    depth = (place // (width * height)) % depth_all
    rolled = {}
    for tap in TAPS:
        depth_off, row_off, col_off = (sign * off for off in tap)
        amount = -((depth_off * height + row_off) * width + col_off) % lanes
        if amount not in rolled:
            rolled[amount] = pltpu.roll(block, amount, 1) if amount else block
        inside = (depth + depth_off >= 0) & (depth + depth_off < depth_all)
        inside &= (row + row_off >= 0) & (row + row_off < height)
        inside &= (col + col_off >= 0) & (col + col_off < width)
        yield jnp.where(inside, rolled[amount], 0.0).astype(jnp.bfloat16)


def pre_cotangent(grad, pre, proj):
    hidden_grad = jnp.dot(proj, grad, preferred_element_type=jnp.float32)
    return jnp.where(pre.astype(jnp.float32) > 0, hidden_grad, 0.0).astype(jnp.bfloat16)


def outgoing_kernel(seed_ref, pre_ref, *refs):
    out_refs, sems = refs[:-1], refs[-1]
    here, count = lax.axis_index("space"), lax.axis_size("space")
    copies = []
    for distance, out_ref in enumerate(out_refs, 1):
        group = out_ref.shape[1]
        span = pl.ds(peer(here, distance, count, back=True) * group, group)
        for place, source in enumerate((seed_ref, pre_ref)):
            copies.append(
                pltpu.make_async_copy(
                    source.at[span], out_ref.at[place], sems.at[distance - 1, place]
                )
            )
            copies[-1].start()
    for copy in copies:
        copy.wait()


def prepare_kernel(seed_ref, pre_ref, acts_ref, conv_ref, proj_ref, *refs):
    seed_out, pre_out, acts_out, conv_out, proj_out, acts_rows, sems = refs
    group = seed_out.shape[0]
    mine = pl.ds(lax.axis_index("space") * group, group)
    pairs = (
        (acts_ref, acts_rows),
        (seed_ref.at[mine], seed_out),
        (pre_ref.at[mine], pre_out),
        (conv_ref, conv_out),
        (proj_ref, proj_out),
    )
    copies = [
        pltpu.make_async_copy(source, target, sems.at[place])
        for place, (source, target) in enumerate(pairs)
    ]
    for copy in copies:
        copy.start()
    copies[0].wait()
    rows = acts_rows[...].reshape(-1, acts_rows.shape[-1])
    acts_out[...] = rows.astype(jnp.float32).T.astype(jnp.bfloat16)
    for copy in copies[1:]:
        copy.wait()


def first_kernel(others, extent, *refs):
    seed_ref, pre_ref, arrived_refs = refs[0], refs[1], refs[2 : 2 + others]
    conv_ref, proj_ref, grad_ref, pre_out_ref, out_ref, scratch = refs[2 + others :]
    here, count = lax.axis_index("space"), lax.axis_size("space")
    depth_dev, channels = seed_ref.shape[1], seed_ref.shape[-1]
    for distance in range(count):
        start = peer(here, distance, count) * depth_dev
        for place, own_ref in enumerate((seed_ref, pre_ref)):
            source = own_ref if distance == 0 else arrived_refs[distance - 1].at[place]
            for depth in range(depth_dev):
                scratch[place, :, start + depth] = source[:, depth].astype(jnp.float32)
    for place, target in enumerate((grad_ref, pre_out_ref)):
        target[...] = scratch[place].reshape(-1, channels).T.astype(jnp.bfloat16)
    step_kernel(0, extent, grad_ref, pre_out_ref, conv_ref, proj_ref, out_ref)


def step_kernel(step, extent, grad_ref, pre_ref, conv_ref, proj_ref, *refs):
    out_ref = refs[-1]

    @pl.when(lax.axis_index("section") == lax.axis_size("section") - 1 - step)
    def _():
        masked = pre_cotangent(grad_ref[...], pre_ref[...], proj_ref[...])
        columns = jnp.concatenate(list(shifts(masked.astype(jnp.float32), extent, -1)), axis=0)
        weights = jnp.concatenate([conv_ref[tap] for tap in range(len(TAPS))], axis=1)
        total = grad_ref[...].astype(jnp.float32) + jnp.dot(
            weights, columns, preferred_element_type=jnp.float32
        )
        out_ref[...] = total.astype(jnp.bfloat16)


def pack_kernel(pre_ref, acts_ref, *refs):
    parcel_refs, scratch = refs[:-1], refs[-1]
    place = lax.axis_index("dp")
    count = len(parcel_refs)
    channels, lanes = pre_ref.shape
    shard = channels // count
    padded = parcel_refs[0].shape[0] - channels
    scratch[...] = acts_ref[...].astype(jnp.float32)
    for distance, parcel_ref in enumerate(parcel_refs):
        target = peer(place, distance, count, back=True)
        rows = scratch[pl.ds(pl.multiple_of(target * shard, shard), shard)]
        if padded > shard:
            rows = jnp.concatenate([rows, jnp.zeros((padded - shard, lanes), jnp.float32)], axis=0)
        parcel_ref[:channels] = pre_ref[...]
        parcel_ref[channels:] = rows.astype(jnp.bfloat16)


def unfold_kernel(extent, group, shard, *refs):
    parcel_refs, unfolded_ref, scratch = refs[:-2], refs[-2], refs[-1]
    here, owners = lax.axis_index("space"), lax.axis_size("space")
    crops = len(parcel_refs) // owners
    depth_all, height, width = extent
    area = height * width
    depth_dev = depth_all // owners
    micro = group * owners
    channels = parcel_refs[0].shape[0] - scratch.shape[2]
    for crop in range(crops):
        for distance in range(owners):
            rows = parcel_refs[crop * owners + distance][channels:].astype(jnp.float32)
            start = peer(here, distance, owners) * depth_dev
            for index in range(micro):
                for depth in range(depth_dev):
                    lane = (index * depth_dev + depth) * area
                    scratch[start + depth, index] = rows[:, lane : lane + area]
        for owner in range(owners):
            pieces = [
                scratch[z, owner * group + index][:shard]
                for index in range(group)
                for z in range(depth_all)
            ]
            block = jnp.concatenate(pieces, axis=1)
            lanes = block.shape[1]
            columns = jnp.concatenate(
                [column.astype(jnp.float32) for column in shifts(block, extent, 1)], axis=0
            )
            distance = peer(owner, here, owners) if owners & (owners - 1) == 0 else lax.rem(
                owner - here + owners, owners
            )
            unfolded_ref[distance, :, crop * lanes : (crop + 1) * lanes] = columns.astype(
                jnp.bfloat16
            )


def choose_kernel(count, *refs):
    step_refs, grad_ref = refs[:count], refs[-1]
    section = lax.axis_index("section")
    for step, step_ref in enumerate(step_refs):

        @pl.when(section == count - 1 - step)
        def _(step_ref=step_ref):
            grad_ref[...] = step_ref[...]


def hand_on_kernel(count, *refs):
    out_ref = refs[-1]
    for place, block_ref in enumerate(refs[:count]):
        size = block_ref.shape[0]
        out_ref[place * size : (place + 1) * size] = block_ref[...]


def block_terms(blocks, grad_refs, parcel_refs, proj_ref, masked_ref, shard):
    here = lax.axis_index("dp")
    channels = proj_ref.shape[0]
    total = None
    for place, (ref_place, start) in enumerate(blocks):
        grad = grad_refs[ref_place][start : start + channels]
        parcel_ref = parcel_refs[place]
        lanes = grad.shape[1]
        masked_ref[:, place * lanes : (place + 1) * lanes] = pre_cotangent(
            grad, parcel_ref[:channels], proj_ref[...]
        )
        mine = parcel_ref[pl.ds(pl.multiple_of(here * shard, shard), shard)]
        hidden = jnp.maximum(mine.astype(jnp.float32), 0.0).astype(jnp.bfloat16)
        term = lax.dot_general(hidden, grad, CONTRACT_LANES, preferred_element_type=jnp.float32)
        total = term if total is None else total + term
    return total


def weights_kernel(plan, shard, has_before, final, scale_term, cuts, *refs):
    ref_count, blocks, columns = plan
    grad_refs, refs = refs[:ref_count], refs[ref_count:]
    parcel_refs, refs = refs[: len(blocks)], refs[len(blocks) :]
    unfolded_ref, proj_ref, refs = refs[0], refs[1], refs[2:]
    before_refs, refs = refs[: 2 * has_before], refs[2 * has_before :]
    copies = []
    conv_out_ref, proj_out_ref, masked_ref = refs[:3]
    scale = scale_term if final else 1.0
    proj_total = block_terms(blocks, grad_refs, parcel_refs, proj_ref, masked_ref, shard)
    if has_before:
        proj_total = before_refs[1][...] + proj_total
    proj_out_ref[...] = proj_total * scale
    lanes = grad_refs[0].shape[1]
    size = conv_out_ref.shape[0] // cuts
    for cut in range(cuts):
        span = pl.ds(cut * size, size)
        rows = jnp.concatenate(
            [
                unfolded_ref[owner, span, crop * lanes : (crop + 1) * lanes]
                for crop, owner in columns
            ],
            axis=1,
        )
        total = lax.dot_general(
            rows, masked_ref[...], CONTRACT_LANES, preferred_element_type=jnp.float32
        )
        if has_before:
            total = before_refs[0][span] + total
        if not final:
            conv_out_ref[span] = total
            continue
        rows_ref, sems = refs[3:]
        rows_ref[span] = total * scale
        copies.append(
            pltpu.make_async_copy(rows_ref.at[span], conv_out_ref.at[span], sems.at[cut])
        )
        copies[-1].start()
    for copy in copies:
        copy.wait()


def slab_kernel(extent, starts, *refs):
    owners = len(starts)
    grad_refs, refs = refs[:owners], refs[owners:]
    pre_refs, (conv_ref, proj_ref, out_ref) = refs[:owners], refs[owners:]
    here = lax.axis_index("space")
    depth_all, height, width = extent
    area = height * width
    depth_dev, channels = out_ref.shape[1], out_ref.shape[-1]
    group = out_ref.shape[0] // owners
    lanes = depth_all * area
    own_first = lax.rem((owners - here) * (depth_dev * area), lanes)

    def from_own(block):
        turned = [
            pltpu.roll(block[:, index * lanes : (index + 1) * lanes], own_first, 1)
            for index in range(group)
        ]
        return [
            [turn[:, z * area : (z + 1) * area] for turn in turned] for z in range(depth_all)
        ]

    grads, masks = [[] for _ in range(depth_all)], [[] for _ in range(depth_all)]
    for grad_ref, start, pre_ref in zip(grad_refs, starts, pre_refs):
        grad = grad_ref[start : start + channels]
        masked = pre_cotangent(grad, pre_ref[:channels], proj_ref[...])
        for target, block in ((grads, grad), (masks, masked)):
            for z, pieces in enumerate(from_own(block.astype(jnp.float32))):
                target[z] += pieces
    grads = [jnp.concatenate(pieces, axis=1) for pieces in grads]
    flat = (1, height, width)
    masks = [jnp.concatenate(pieces, axis=1) for pieces in masks]
    near_taps = len(TAPS) // len(SIDE)
    moved_planes = [list(shifts(mask, flat, -1))[near_taps : 2 * near_taps] for mask in masks]
    weights = jnp.concatenate([conv_ref[tap] for tap in range(len(TAPS))], axis=1)
    for depth in range(depth_dev):
        columns = []
        for depth_off in SIDE:
            place = here * depth_dev + depth - depth_off
            inside = (place >= 0) & (place < depth_all)
            for block in moved_planes[(depth - depth_off) % depth_all]:
                columns.append(jnp.where(inside, block, jnp.zeros_like(block)))
        total = grads[depth] + jnp.dot(
            weights, jnp.concatenate(columns, axis=0), preferred_element_type=jnp.float32
        )
        rows = total.T.astype(jnp.bfloat16)
        for distance in range(owners):
            start = peer(here, distance, owners) * group
            for index in range(group):
                first = (distance * group + index) * area
                out_ref[start + index, depth] = rows[first : first + area]


def whole(count=1):
    return [pl.BlockSpec(memory_space=pltpu.VMEM)] * count


def unread(count=1):
    return [pl.BlockSpec(memory_space=pl.ANY)] * count


def kept_in_hbm(*arrays):
    return [pltpu.with_memory_space_constraint(array, pltpu.HBM) for array in arrays]


def kernel_call(body, name, operands, outs, scratch=(), in_specs=None, out_specs=None):
    single = not isinstance(outs, (tuple, list))
    count = 1 if single else len(outs)
    specs = out_specs or whole(count)
    return pl.pallas_call(
        body,
        out_shape=outs if single else tuple(outs),
        in_specs=in_specs or whole(len(operands)),
        out_specs=specs[0] if single else tuple(specs),
        scratch_shapes=list(scratch),
        compiler_params=pltpu.CompilerParams(vmem_limit_bytes=VMEM_LIMIT),
        name=name,
    )(*operands)


def shards(inputs, preacts, out_grad, conv_w, proj_w):
    section_count = lax.axis_size("section")
    crops = lax.axis_size("dp")
    slabs = lax.axis_size("space")
    micro, _, depth_dev, height, width, channels = inputs.shape[1:]
    assert micro % slabs == 0
    group = micro // slabs
    area = height * width
    depth_all = slabs * depth_dev
    extent = (depth_all, height, width)
    lanes = group * depth_all * area
    shard = channels // crops
    padded = -(-shard // 16) * 16
    others = slabs - 1
    scale_term = 1.0 / (micro * crops)
    bfloat = jnp.bfloat16
    acts = inputs.reshape(micro, depth_dev, area, channels)
    pre_acts = preacts.reshape(acts.shape)
    seeds = out_grad.reshape(acts.shape)
    volume = jax.ShapeDtypeStruct((channels, lanes), bfloat)
    part = jax.ShapeDtypeStruct((group, depth_dev, area, channels), bfloat)
    parcel = jax.ShapeDtypeStruct((channels + padded, lanes), bfloat)
    hbm = pl.BlockSpec(memory_space=pltpu.HBM)

    arrived = kernel_call(
        outgoing_kernel,
        "outgoing",
        kept_in_hbm(seeds, pre_acts),
        [jax.ShapeDtypeStruct((2,) + part.shape, bfloat)] * others,
        scratch=[pltpu.SemaphoreType.DMA((others, 2))],
        in_specs=[hbm] * 2,
    )
    arrived = [moved(block, 0, distance) for distance, block in enumerate(arrived, 1)]
    seed_own, pre_own, acts_own, conv_weight, proj_weight = kernel_call(
        prepare_kernel,
        "prepare",
        kept_in_hbm(seeds, pre_acts, acts, conv_w[0], proj_w[0]),
        [
            part,
            part,
            volume,
            jax.ShapeDtypeStruct(conv_w.shape[1:], bfloat),
            jax.ShapeDtypeStruct(proj_w.shape[1:], bfloat),
        ],
        scratch=[pltpu.VMEM(acts.shape, bfloat), pltpu.SemaphoreType.DMA((5,))],
        in_specs=[hbm] * 5,
    )
    grad_first, pre_all, result = kernel_call(
        functools.partial(first_kernel, others, extent),
        "first_block",
        [seed_own, pre_own, *arrived, conv_weight, proj_weight],
        [volume] * 3,
        scratch=[pltpu.VMEM((2, group, depth_all, area, channels), jnp.float32)],
    )

    results = [result]
    received = []
    parcels = {}
    for step in range(1, section_count):
        received.append(lax.ppermute(results[-1], "section", hop_pairs(section_count, step)))
        if not parcels:
            sent = kernel_call(
                pack_kernel,
                "pack",
                [pre_all, acts_own],
                [parcel] * crops,
                scratch=[pltpu.VMEM(volume.shape, jnp.float32)],
            )
            parcels = {
                (crop, slab): moved(sent[crop], crop, slab) if crop or slab else sent[0]
                for crop in range(crops)
                for slab in range(slabs)
            }
        if step == section_count - 1:
            break
        earlier = [parcels[crop, 0] for crop in range(crops if step > 1 else 1)]
        results.append(
            kernel_call(
                functools.partial(step_kernel, step, extent),
                "block",
                [received[-1], pre_all, conv_weight, proj_weight, *earlier],
                volume,
                in_specs=whole(4) + unread(len(earlier)),
            )
        )

    taps = len(TAPS)
    unfolded = kernel_call(
        functools.partial(unfold_kernel, extent, group, shard),
        "unfold",
        [parcels[crop, slab] for crop in range(crops) for slab in range(slabs)],
        jax.ShapeDtypeStruct((slabs, taps * shard, crops * lanes), bfloat),
        scratch=[pltpu.VMEM((depth_all, micro, padded, area), jnp.float32)],
    )
    grad_own = kernel_call(
        functools.partial(choose_kernel, section_count),
        "choose",
        [grad_first, *received, unfolded],
        volume,
        in_specs=whole(section_count) + unread(),
    )

    conv_shape = jax.ShapeDtypeStruct((taps * shard, channels), jnp.float32)
    proj_shape = jax.ShapeDtypeStruct((shard, channels), jnp.float32)
    cuts = len(SIDE) if (taps // len(SIDE) * shard) % 16 == 0 else 1

    def weight_sums(arrays, blocks, columns, before, final):
        plan = (len(arrays), blocks, columns)
        operands = [*arrays, *[parcels[column] for column in columns]]
        operands += [unfolded, proj_weight, *before]
        scratch = [pltpu.VMEM((channels, len(columns) * lanes), bfloat)]
        out_specs = whole(2)
        if final:
            scratch += [pltpu.VMEM(conv_shape.shape, jnp.float32), pltpu.SemaphoreType.DMA((cuts,))]
            out_specs = [hbm] + whole()
        return kernel_call(
            functools.partial(
                weights_kernel, plan, shard, bool(before), final, scale_term, cuts if final else 1
            ),
            "weight_grads" if final else "part_weight_grads",
            operands,
            [conv_shape, proj_shape],
            scratch=scratch,
            out_specs=out_specs,
        )

    near = crops // 2
    if near < 2 or crops & (crops - 1):
        columns = [(crop, slab) for crop in range(crops) for slab in range(slabs)]
        arrays = [moved(grad_own, *column) if any(column) else grad_own for column in columns]
        blocks = [(place, 0) for place in range(len(columns))]
        conv_rows, proj_rows = weight_sums(arrays, blocks, columns, (), True)
        slab_grads = [(arrays[columns.index((0, slab))], 0) for slab in range(slabs)]
    else:
        across = [moved(grad_own, near, slab) for slab in range(slabs)]
        beside = [moved(grad_own, 0, slab) for slab in range(1, slabs)]
        columns = [(crop, 0) for crop in range(near)]
        arrays = [grad_own] + [moved(grad_own, crop, 0) for crop in range(1, near)]
        blocks = [(place, 0) for place in range(near)]
        sums = weight_sums(arrays, blocks, columns, (), False)
        middle = beside + across
        handed = kernel_call(
            functools.partial(hand_on_kernel, len(middle)),
            "hand_on",
            [*middle, sums[1]],
            jax.ShapeDtypeStruct((len(middle) * channels, lanes), bfloat),
            in_specs=whole(len(middle)) + unread(),
        )
        places = [(0, slab) for slab in range(1, slabs)] + [(near, slab) for slab in range(slabs)]
        columns = [(crop + place, slab) for crop in range(near) for place, slab in places]
        arrays = [handed] + [moved(handed, crop, 0) for crop in range(1, near)]
        blocks = [
            (array, place * channels) for array in range(near) for place in range(len(places))
        ]
        conv_rows, proj_rows = weight_sums(arrays, blocks, columns, sums, True)
        slab_grads = [(grad_own, 0)] + [(handed, place * channels) for place in range(others)]

    section_out = kernel_call(
        functools.partial(slab_kernel, extent, [start for _, start in slab_grads]),
        "own_slab",
        [block for block, _ in slab_grads]
        + [parcels[0, slab] for slab in range(slabs)]
        + [conv_weight, proj_weight],
        jax.ShapeDtypeStruct(acts.shape, bfloat),
    )

    section_grads = section_out.reshape(inputs.shape)
    grad_conv = conv_rows.reshape(taps, shard, channels).swapaxes(0, 1)[None]
    return section_grads, grad_conv, proj_rows[None]


def solution(mesh):
    placed = (
        P("section", None, "dp", "space", None, None, None),
        P("section", None, "dp", "space", None, None, None),
        P(None, "dp", "space", None, None, None),
        P("section", None, None, None),
        P("section", None, None),
    )
    return jax.shard_map(
        shards,
        mesh=mesh,
        in_specs=placed,
        out_specs=(
            P("section", None, "dp", "space", None, None, None),
            P("section", "dp", None, None),
            P("section", "dp", None),
        ),
        check_vma=False,
    )
```

time: 324 us -> 40.5 us (0.12)
  waiting for transfers between devices: 177 us -> 8.59 us
  matrix products: 38.5 us -> 0 us
  local copies, waits for them, and re-layouts: 36.1 us -> 0 us
  starting transfers between devices: 41.8 us -> 20.6 us
  between operations: 14.1 us -> 0.72 us
  Pallas kernels: 0 us -> 10.3 us
  blocking collectives: 8.95 us -> 0 us
  other arithmetic: 5.54 us -> 0 us
    ppermute x17 -> x16, waiting for transfers between devices: 85.8 us -> 8.59 us  [the longest x13 8.34 us: moved(): return lax.ppermute(block, ('dp', 'space'), pairs)]
    reduce_scatter x2 -> x0, waiting for transfers between devices: 57.5 us -> none  [the longest x1 37.7 us: shards(): lax.psum_scatter(conv_full.astype(jnp.bfloat16), 'dp', scatter_dimension=...]
    dot_general x58 -> x0, matrix products: 38.5 us -> none  [the longest x54 33.4 us: close_branch(): lax.dot_general(moved.reshape(row_count, channels), conv_weight[index], c...]
    psum x1 -> x0, waiting for transfers between devices: 33.4 us -> none  [shards(): lax.psum(conv_shard.astype(jnp.bfloat16), 'space').astype(jnp.float32)]
    ppermute x17 -> x16, starting transfers between devices: 41.7 us -> 20.6 us  [the longest x13 13.1 us: moved(): return lax.ppermute(block, ('dp', 'space'), pairs)]
    another operation x13 -> x0, local copies, waits for them, and re-layouts: 13 us -> none  [the longest x2 6.29 us: shards(): jnp.stack(columns, axis=-1)]
    reshape x4 -> x0, local copies, waits for them, and re-layouts: 11.8 us -> none  [the longest x1 11.8 us: shards(): jnp.stack(columns, axis=-1)]
    pallas_call x0 -> x12, Pallas kernels: none -> 10.3 us  [kernel_call(): pl.pallas_call(body, out_shape=outs if single else tuple(outs), in_specs=...]
  transfers between devices with their start and end apart: 20 -> 16, of which waited for: 20 -> 7; matrix products, arithmetic and copies ran while one was open for 1% -> 0% of each run, Pallas kernels for 0% -> 16%
where the time goes in v1:
time: 40.5 us; the launch traced here: 40.3 us
  starting transfers between devices  20.6 us (51%)
  Pallas kernels  10.3 us (25%)
  waiting for transfers between devices  8.59 us (21%)
  between operations  0.72 us (2%)
    ppermute x13, starting transfers between devices, moved(): return lax.ppermute(block, ('dp', 'space'), pairs)  13.1 us
    pallas_call x12, Pallas kernels, kernel_call(): pl.pallas_call(body, out_shape=outs if single else tuple(outs), in_specs=...  10.3 us
    ppermute x13, waiting for transfers between devices, moved(): return lax.ppermute(block, ('dp', 'space'), pairs)  8.34 us
    ppermute x3, starting transfers between devices, shards(): lax.ppermute(results[-1], 'section', hop_pairs(section_count, step))  7.55 us
  transfers between devices with their start and end apart: 16, of which 7 were waited for; matrix products, arithmetic and copies ran while one was open for 0% of the time, Pallas kernels for 16%

profile of v1, /device:TPU:0, one launch (start us, length us, event | category | flops | bytes accessed | tf_op | source)
XLA Modules:
  0.0 40.3 jit_solution(15400366856863446664)
XLA Ops:
  0.6 0.8 %outgoing.1 = bf16[2,1,1,64,256]{4,3,2,1,0:T(8,128)(2,1)S(1)} custom-call(bf16[2,1,64,256]{3,2,1,0:T(8,128)(2,1)} %bitcast.15, bf16[2,1,64,256]{3,2,1,0:T(8,128)(2,1)} %bitcast.17), custom_call_target="tpu_custom_call" | custom-call | tf_op jit(solution)/shard_map/outgoing/pallas_call | solution.py:332
  1.4 3.0 %collective-permute-start = (bf16[2,1,1,64,256]{4,3,2,1,0:T(8,128)(2,1)S(1)}, bf16[2,1,1,64,256]{4,3,2,1,0:T(8,128)(2,1)S(1)}, u32[]{:S(2)}, u32[]{:S(2)}) collective-permute-start(bf16[2,1,1,64,256]{4,3,2,1,0:T(8,128)(2,1)S(1)} %outgoing.1), channel_id=1, source_target_pairs={{1,0},{0,1},{3,2},{2,3},{5,4},{4,5},{7,6},{6,7},{9,8},{8,9},{11,10... | collective-permute-start | bytes 196616 | tf_op jit(solution)/shard_map/ppermute | solution.py:29
  4.5 2.1 %prepare.1 = (bf16[1,1,64,256]{3,2,1,0:T(8,128)(2,1)S(1)}, bf16[1,1,64,256]{3,2,1,0:T(8,128)(2,1)S(1)}, bf16[256,128]{1,0:T(8,128)(2,1)S(1)}, bf16[27,256,256]{2,1,0:T(8,128)(2,1)S(1)}, bf16[256,256]{1,0:T(8,128)(2,1)S(1)}) custom-call(bf16[2,1,64,256]{3,2,1,0:T(8,128)(2,1)} %bitcast.16, bf16[2,1,64,256]{3,2,1,0:T(8,128)(2,1)} %bitcast.18, ...), custom_call_target="tpu_custom_call" | custom-call | tf_op jit(solution)/shard_map/prepare/pallas_call | solution.py:332
  6.6 0.1 collective-permute-done.refs_2_
  6.7 0.1 first_block.1
  6.8 2.1 %collective-permute-start.1 = (bf16[256,128]{1,0:T(8,128)(2,1)S(1)}, bf16[256,128]{1,0:T(8,128)(2,1)S(1)}, u32[]{:S(2)}, u32[]{:S(2)}) collective-permute-start(bf16[256,128]{1,0:T(8,128)(2,1)S(1)} %get-tuple-element.24), channel_id=1, source_target_pairs={{8,0},{0,8},{24,16},{16,24},{9,1},{1,9},{25,17},{17,25},{10,2},{2,... | collective-permute-start | bytes 196616 | tf_op jit(solution)/shard_map/ppermute | solution.py:402
  9.0 0.1 collective-permute-start.3
  9.1 1.6 %collective-permute-start.4 = (bf16[320,128]{1,0:T(8,128)(2,1)S(1)}, bf16[320,128]{1,0:T(8,128)(2,1)S(1)}, u32[]{:S(2)}, u32[]{:S(2)}) collective-permute-start(bf16[320,128]{1,0:T(8,128)(2,1)S(1)} %get-tuple-element.29), channel_id=1, source_target_pairs={{4,0},{5,1},{6,2},{7,3},{0,4},{1,5},{2,6},{3,7},{12,8},{13,9},{14,... | collective-permute-start | bytes 245768 | tf_op jit(solution)/shard_map/ppermute | solution.py:29
  10.7 0.3 collective-permute-start.5
  11.0 0.3 collective-permute-done.1.grad_ref.refs_1_
  11.2 5.4 %collective-permute-start.2 = (bf16[256,128]{1,0:T(8,128)(2,1)S(1)}, bf16[256,128]{1,0:T(8,128)(2,1)S(1)}, u32[]{:S(2)}, u32[]{:S(2)}) collective-permute-start(bf16[256,128]{1,0:T(8,128)(2,1)S(1)} %block.2), channel_id=1, source_target_pairs={{8,0},{16,8},{24,16},{0,24},{9,1},{17,9},{25,17},{1,25},{10,2},{18... | collective-permute-start | bytes 196616 | tf_op jit(solution)/shard_map/ppermute | solution.py:402
  16.6 0.0 collective-permute-start.8
  16.6 0.0 collective-permute-done.3.refs_1_.refs_2_.refs_3_
  16.6 2.4 %collective-permute-start.9 = (bf16[320,128]{1,0:T(8,128)(2,1)S(1)}, bf16[320,128]{1,0:T(8,128)(2,1)S(1)}, u32[]{:S(2)}, u32[]{:S(2)}) collective-permute-start(bf16[320,128]{1,0:T(8,128)(2,1)S(1)} %get-tuple-element.29), channel_id=1, source_target_pairs={{5,0},{4,1},{7,2},{6,3},{1,4},{0,5},{3,6},{2,7},{13,8},{12,9},{15,... | collective-permute-start | bytes 245768 | tf_op jit(solution)/shard_map/ppermute | solution.py:29
  19.1 0.0 collective-permute-done.4.refs_2_.refs_4_.refs_3_
  19.1 1.4 %collective-permute-start.10 = (bf16[320,128]{1,0:T(8,128)(2,1)S(1)}, bf16[320,128]{1,0:T(8,128)(2,1)S(1)}, u32[]{:S(2)}, u32[]{:S(2)}) collective-permute-start(bf16[320,128]{1,0:T(8,128)(2,1)S(1)} %get-tuple-element.30), channel_id=1, source_target_pairs={{7,0},{6,1},{5,2},{4,3},{3,4},{2,5},{1,6},{0,7},{15,8},{14,9},{13,... | collective-permute-start | bytes 245768 | tf_op jit(solution)/shard_map/ppermute | solution.py:29
  20.5 0.0 collective-permute-done.5.refs_3_.refs_6_
  20.5 0.5 %collective-permute-start.7 = (bf16[320,128]{1,0:T(8,128)(2,1)S(1)}, bf16[320,128]{1,0:T(8,128)(2,1)S(1)}, u32[]{:S(2)}, u32[]{:S(2)}) collective-permute-start(bf16[320,128]{1,0:T(8,128)(2,1)S(1)} %get-tuple-element.27.refs_0_.refs_2_), channel_id=1, source_target_pairs={{1,0},{0,1},{3,2},{2,3},{5,4},{4,5},{7,6},{6,7},{9,8},{8,9},{11,10... | collective-permute-start | bytes 245768 | tf_op jit(solution)/shard_map/ppermute | solution.py:29
  21.0 0.0 collective-permute-done.2.grad_ref.refs_2_
  21.0 0.0 collective-permute-start.6
  21.1 3.8 %collective-permute-done.8.refs_3_.refs_5_ = bf16[320,128]{1,0:T(8,128)(2,1)S(1)} collective-permute-done((bf16[320,128]{1,0:T(8,128)(2,1)S(1)}, bf16[320,128]{1,0:T(8,128)(2,1)S(1)}, u32[]{:S(2)}, u32[]{:S(2)}) %collective-permute-start.8) | collective-permute-done | bytes 81952 | tf_op jit(solution)/shard_map/ppermute | solution.py:29
  24.8 0.0 collective-permute-done.9.refs_5_.refs_4_
  24.8 0.0 collective-permute-done.10.refs_7_
  24.8 1.8 %collective-permute-done.7.refs_1_.refs_3_.refs_2_ = bf16[320,128]{1,0:T(8,128)(2,1)S(1)} collective-permute-done((bf16[320,128]{1,0:T(8,128)(2,1)S(1)}, bf16[320,128]{1,0:T(8,128)(2,1)S(1)}, u32[]{:S(2)}, u32[]{:S(2)}) %collective-permute-start.7) | collective-permute-done | bytes 81952 | tf_op jit(solution)/shard_map/ppermute | solution.py:29
  26.7 1.5 %unfold.1.refs_4_.refs_8_ = bf16[2,1728,512]{2,1,0:T(8,128)(2,1)S(1)} custom-call(bf16[320,128]{1,0:T(8,128)(2,1)S(1)} %get-tuple-element.27.refs_0_.refs_2_, bf16[320,128]{1,0:T(8,128)(2,1)S(1)} %collective-permute-done.7.refs_1_.refs_3_.refs_2_, bf16[320,128]{1,0:T(8,128)(2,1)S(1)} %collective-permute-done.3.refs_1_.refs_2_.refs_3_, ...), custom_call_target="tpu_custom_call" | custom-call | tf_op jit(solution)/shard_map/unfold/pallas_call | solution.py:332
  28.2 0.0 collective-permute-done.6.refs_3_
  28.2 0.1 collective-permute-start.14
  28.3 1.9 %collective-permute-start.13 = (bf16[256,128]{1,0:T(8,128)(2,1)S(1)}, bf16[256,128]{1,0:T(8,128)(2,1)S(1)}, u32[]{:S(2)}, u32[]{:S(2)}) collective-permute-start(bf16[256,128]{1,0:T(8,128)(2,1)S(1)} %choose.1.refs_0_), channel_id=1, source_target_pairs={{5,0},{4,1},{7,2},{6,3},{1,4},{0,5},{3,6},{2,7},{13,8},{12,9},{15,... | collective-permute-start | bytes 196616 | tf_op jit(solution)/shard_map/ppermute | solution.py:29
  30.2 0.5 %collective-permute-start.12 = (bf16[256,128]{1,0:T(8,128)(2,1)S(1)}, bf16[256,128]{1,0:T(8,128)(2,1)S(1)}, u32[]{:S(2)}, u32[]{:S(2)}) collective-permute-start(bf16[256,128]{1,0:T(8,128)(2,1)S(1)} %choose.1.refs_0_), channel_id=1, source_target_pairs={{4,0},{5,1},{6,2},{7,3},{0,4},{1,5},{2,6},{3,7},{12,8},{13,9},{14,... | collective-permute-start | bytes 196616 | tf_op jit(solution)/shard_map/ppermute | solution.py:29
  30.7 1.1 %collective-permute-start.11 = (bf16[256,128]{1,0:T(8,128)(2,1)S(1)}, bf16[256,128]{1,0:T(8,128)(2,1)S(1)}, u32[]{:S(2)}, u32[]{:S(2)}) collective-permute-start(bf16[256,128]{1,0:T(8,128)(2,1)S(1)} %choose.1.refs_0_), channel_id=1, source_target_pairs={{1,0},{0,1},{3,2},{2,3},{5,4},{4,5},{7,6},{6,7},{9,8},{8,9},{11,10... | collective-permute-start | bytes 196616 | tf_op jit(solution)/shard_map/ppermute | solution.py:29
  31.9 0.0 collective-permute-done.14.refs_1_
  31.9 0.6 %part_weight_grads.1 = (f32[1728,256]{1,0:T(8,128)S(1)}, f32[64,256]{1,0:T(8,128)S(1)}) custom-call(bf16[256,128]{1,0:T(8,128)(2,1)S(1)} %choose.1.refs_0_, bf16[256,128]{1,0:T(8,128)(2,1)S(1)} %collective-permute-done.14.refs_1_, bf16[320,128]{1,0:T(8,128)(2,1)S(1)} %get-tuple-element.27.refs_0_.refs_2_, ...), custom_call_target="tpu_custom_call" | custom-call | tf_op jit(solution)/shard_map/part_weight_grads/pallas_call | solution.py:332
  32.5 1.4 %collective-permute-done.13.refs_2_ = bf16[256,128]{1,0:T(8,128)(2,1)S(1)} collective-permute-done((bf16[256,128]{1,0:T(8,128)(2,1)S(1)}, bf16[256,128]{1,0:T(8,128)(2,1)S(1)}, u32[]{:S(2)}, u32[]{:S(2)}) %collective-permute-start.13) | collective-permute-done | bytes 65568 | tf_op jit(solution)/shard_map/ppermute | solution.py:29
  34.0 0.6 %collective-permute-done.12.refs_1_ = bf16[256,128]{1,0:T(8,128)(2,1)S(1)} collective-permute-done((bf16[256,128]{1,0:T(8,128)(2,1)S(1)}, bf16[256,128]{1,0:T(8,128)(2,1)S(1)}, u32[]{:S(2)}, u32[]{:S(2)}) %collective-permute-start.12) | collective-permute-done | bytes 65568 | tf_op jit(solution)/shard_map/ppermute | solution.py:29
  34.6 0.6 %collective-permute-done.11.refs_0_ = bf16[256,128]{1,0:T(8,128)(2,1)S(1)} collective-permute-done((bf16[256,128]{1,0:T(8,128)(2,1)S(1)}, bf16[256,128]{1,0:T(8,128)(2,1)S(1)}, u32[]{:S(2)}, u32[]{:S(2)}) %collective-permute-start.11) | collective-permute-done | bytes 65568 | tf_op jit(solution)/shard_map/ppermute | solution.py:29
  35.1 0.1 collective-permute-start.15
  35.2 2.2 %own_slab.1 = bf16[2,1,64,256]{3,2,1,0:T(8,128)(2,1)} custom-call(bf16[256,128]{1,0:T(8,128)(2,1)S(1)} %choose.1.refs_0_, bf16[768,128]{1,0:T(8,128)(2,1)S(1)} %hand_on.1.refs_1_.refs_0_, bf16[320,128]{1,0:T(8,128)(2,1)S(1)} %get-tuple-element.27.refs_0_.refs_2_, bf16[320,128]{1,0:T(8,128)(2,1)S(1)} %collective-permute-done.7.refs_1_.refs_3_.refs_2_, ...), custom_call_target="tpu_custom_call" | custom-call | tf_op jit(solution)/shard_map/own_slab/pallas_call | solution.py:332
  37.4 0.0 collective-permute-done.15.refs_1_
  37.4 2.9 %weight_grads.1 = (f32[1728,256]{1,0:T(8,128)}, f32[64,256]{1,0:T(8,128)}) custom-call(bf16[768,128]{1,0:T(8,128)(2,1)S(1)} %hand_on.1.refs_1_.refs_0_, bf16[768,128]{1,0:T(8,128)(2,1)S(1)} %collective-permute-done.15.refs_1_, bf16[320,128]{1,0:T(8,128)(2,1)S(1)} %collective-permute-done.7.refs_1_.refs_3_.refs_2_, ...), custom_call_target="tpu_custom_call" | custom-call | tf_op jit(solution)/shard_map/weight_grads/pallas_call | solution.py:332
  (5 shorter events, 0.1 us)
Async XLA Ops:
  1.4 5.3 %collective-permute-start = (bf16[2,1,1,64,256]{4,3,2,1,0:T(8,128)(2,1)S(1)}, bf16[2,1,1,64,256]{4,3,2,1,0:T(8,128)(2,1)S(1)}, u32[]{:S(2)}, u32[]{:S(2)}) collective-permute-start(bf16[2,1,1,64,256]{4,3,2,1,0:T(8,128)(2,1)S(1)} %outgoing.1), channel_id=1, source_target_pairs={{1,0},{0,1},{3,2},{2,3},{5,4},{4,5},{7,6},{6,7},{9,8},{8,9},{11,10... | collective-permute-start | bytes 196616 | tf_op jit(solution)/shard_map/ppermute | solution.py:29
  6.8 4.4 %collective-permute-start.1 = (bf16[256,128]{1,0:T(8,128)(2,1)S(1)}, bf16[256,128]{1,0:T(8,128)(2,1)S(1)}, u32[]{:S(2)}, u32[]{:S(2)}) collective-permute-start(bf16[256,128]{1,0:T(8,128)(2,1)S(1)} %get-tuple-element.24), channel_id=1, source_target_pairs={{8,0},{0,8},{24,16},{16,24},{9,1},{1,9},{25,17},{17,25},{10,2},{2,... | collective-permute-start | bytes 196616 | tf_op jit(solution)/shard_map/ppermute | solution.py:402
  9.0 7.6 %collective-permute-start.3 = (bf16[320,128]{1,0:T(8,128)(2,1)S(1)}, bf16[320,128]{1,0:T(8,128)(2,1)S(1)}, u32[]{:S(2)}, u32[]{:S(2)}) collective-permute-start(bf16[320,128]{1,0:T(8,128)(2,1)S(1)} %get-tuple-element.28), channel_id=1, source_target_pairs={{2,0},{3,1},{0,2},{1,3},{6,4},{7,5},{4,6},{5,7},{10,8},{11,9},{8,1... | collective-permute-start | bytes 245768 | tf_op jit(solution)/shard_map/ppermute | solution.py:29
  9.1 10.0 %collective-permute-start.4 = (bf16[320,128]{1,0:T(8,128)(2,1)S(1)}, bf16[320,128]{1,0:T(8,128)(2,1)S(1)}, u32[]{:S(2)}, u32[]{:S(2)}) collective-permute-start(bf16[320,128]{1,0:T(8,128)(2,1)S(1)} %get-tuple-element.29), channel_id=1, source_target_pairs={{4,0},{5,1},{6,2},{7,3},{0,4},{1,5},{2,6},{3,7},{12,8},{13,9},{14,... | collective-permute-start | bytes 245768 | tf_op jit(solution)/shard_map/ppermute | solution.py:29
  10.7 9.9 %collective-permute-start.5 = (bf16[320,128]{1,0:T(8,128)(2,1)S(1)}, bf16[320,128]{1,0:T(8,128)(2,1)S(1)}, u32[]{:S(2)}, u32[]{:S(2)}) collective-permute-start(bf16[320,128]{1,0:T(8,128)(2,1)S(1)} %get-tuple-element.30), channel_id=1, source_target_pairs={{6,0},{7,1},{4,2},{5,3},{2,4},{3,5},{0,6},{1,7},{14,8},{15,9},{12,... | collective-permute-start | bytes 245768 | tf_op jit(solution)/shard_map/ppermute | solution.py:29
  11.2 9.8 %collective-permute-start.2 = (bf16[256,128]{1,0:T(8,128)(2,1)S(1)}, bf16[256,128]{1,0:T(8,128)(2,1)S(1)}, u32[]{:S(2)}, u32[]{:S(2)}) collective-permute-start(bf16[256,128]{1,0:T(8,128)(2,1)S(1)} %block.2), channel_id=1, source_target_pairs={{8,0},{16,8},{24,16},{0,24},{9,1},{17,9},{25,17},{1,25},{10,2},{18... | collective-permute-start | bytes 196616 | tf_op jit(solution)/shard_map/ppermute | solution.py:402
  16.6 8.2 %collective-permute-start.8 = (bf16[320,128]{1,0:T(8,128)(2,1)S(1)}, bf16[320,128]{1,0:T(8,128)(2,1)S(1)}, u32[]{:S(2)}, u32[]{:S(2)}) collective-permute-start(bf16[320,128]{1,0:T(8,128)(2,1)S(1)} %get-tuple-element.28), channel_id=1, source_target_pairs={{3,0},{2,1},{1,2},{0,3},{7,4},{6,5},{5,6},{4,7},{11,8},{10,9},{9,1... | collective-permute-start | bytes 245768 | tf_op jit(solution)/shard_map/ppermute | solution.py:29
  16.6 8.2 %collective-permute-start.9 = (bf16[320,128]{1,0:T(8,128)(2,1)S(1)}, bf16[320,128]{1,0:T(8,128)(2,1)S(1)}, u32[]{:S(2)}, u32[]{:S(2)}) collective-permute-start(bf16[320,128]{1,0:T(8,128)(2,1)S(1)} %get-tuple-element.29), channel_id=1, source_target_pairs={{5,0},{4,1},{7,2},{6,3},{1,4},{0,5},{3,6},{2,7},{13,8},{12,9},{15,... | collective-permute-start | bytes 245768 | tf_op jit(solution)/shard_map/ppermute | solution.py:29
  19.1 5.7 %collective-permute-start.10 = (bf16[320,128]{1,0:T(8,128)(2,1)S(1)}, bf16[320,128]{1,0:T(8,128)(2,1)S(1)}, u32[]{:S(2)}, u32[]{:S(2)}) collective-permute-start(bf16[320,128]{1,0:T(8,128)(2,1)S(1)} %get-tuple-element.30), channel_id=1, source_target_pairs={{7,0},{6,1},{5,2},{4,3},{3,4},{2,5},{1,6},{0,7},{15,8},{14,9},{13,... | collective-permute-start | bytes 245768 | tf_op jit(solution)/shard_map/ppermute | solution.py:29
  20.5 6.1 %collective-permute-start.7 = (bf16[320,128]{1,0:T(8,128)(2,1)S(1)}, bf16[320,128]{1,0:T(8,128)(2,1)S(1)}, u32[]{:S(2)}, u32[]{:S(2)}) collective-permute-start(bf16[320,128]{1,0:T(8,128)(2,1)S(1)} %get-tuple-element.27.refs_0_.refs_2_), channel_id=1, source_target_pairs={{1,0},{0,1},{3,2},{2,3},{5,4},{4,5},{7,6},{6,7},{9,8},{8,9},{11,10... | collective-permute-start | bytes 245768 | tf_op jit(solution)/shard_map/ppermute | solution.py:29
  21.0 7.1 %collective-permute-start.6 = (bf16[256,128]{1,0:T(8,128)(2,1)S(1)}, bf16[256,128]{1,0:T(8,128)(2,1)S(1)}, u32[]{:S(2)}, u32[]{:S(2)}) collective-permute-start(bf16[256,128]{1,0:T(8,128)(2,1)S(1)} %block.3), channel_id=1, source_target_pairs={{8,0},{0,8},{24,16},{16,24},{9,1},{1,9},{25,17},{17,25},{10,2},{2,... | collective-permute-start | bytes 196616 | tf_op jit(solution)/shard_map/ppermute | solution.py:402
  28.2 3.6 %collective-permute-start.14 = (bf16[256,128]{1,0:T(8,128)(2,1)S(1)}, bf16[256,128]{1,0:T(8,128)(2,1)S(1)}, u32[]{:S(2)}, u32[]{:S(2)}) collective-permute-start(bf16[256,128]{1,0:T(8,128)(2,1)S(1)} %choose.1.refs_0_), channel_id=1, source_target_pairs={{2,0},{3,1},{0,2},{1,3},{6,4},{7,5},{4,6},{5,7},{10,8},{11,9},{8,1... | collective-permute-start | bytes 196616 | tf_op jit(solution)/shard_map/ppermute | solution.py:29
  28.3 5.6 %collective-permute-start.13 = (bf16[256,128]{1,0:T(8,128)(2,1)S(1)}, bf16[256,128]{1,0:T(8,128)(2,1)S(1)}, u32[]{:S(2)}, u32[]{:S(2)}) collective-permute-start(bf16[256,128]{1,0:T(8,128)(2,1)S(1)} %choose.1.refs_0_), channel_id=1, source_target_pairs={{5,0},{4,1},{7,2},{6,3},{1,4},{0,5},{3,6},{2,7},{13,8},{12,9},{15,... | collective-permute-start | bytes 196616 | tf_op jit(solution)/shard_map/ppermute | solution.py:29
  30.2 4.4 %collective-permute-start.12 = (bf16[256,128]{1,0:T(8,128)(2,1)S(1)}, bf16[256,128]{1,0:T(8,128)(2,1)S(1)}, u32[]{:S(2)}, u32[]{:S(2)}) collective-permute-start(bf16[256,128]{1,0:T(8,128)(2,1)S(1)} %choose.1.refs_0_), channel_id=1, source_target_pairs={{4,0},{5,1},{6,2},{7,3},{0,4},{1,5},{2,6},{3,7},{12,8},{13,9},{14,... | collective-permute-start | bytes 196616 | tf_op jit(solution)/shard_map/ppermute | solution.py:29
  30.7 4.4 %collective-permute-start.11 = (bf16[256,128]{1,0:T(8,128)(2,1)S(1)}, bf16[256,128]{1,0:T(8,128)(2,1)S(1)}, u32[]{:S(2)}, u32[]{:S(2)}) collective-permute-start(bf16[256,128]{1,0:T(8,128)(2,1)S(1)} %choose.1.refs_0_), channel_id=1, source_target_pairs={{1,0},{0,1},{3,2},{2,3},{5,4},{4,5},{7,6},{6,7},{9,8},{8,9},{11,10... | collective-permute-start | bytes 196616 | tf_op jit(solution)/shard_map/ppermute | solution.py:29
  35.1 2.3 %collective-permute-start.15 = (bf16[768,128]{1,0:T(8,128)(2,1)S(1)}, bf16[768,128]{1,0:T(8,128)(2,1)S(1)}, u32[]{:S(2)}, u32[]{:S(2)}) collective-permute-start(bf16[768,128]{1,0:T(8,128)(2,1)S(1)} %hand_on.1.refs_1_.refs_0_), channel_id=1, source_target_pairs={{2,0},{3,1},{0,2},{1,3},{6,4},{7,5},{4,6},{5,7},{10,8},{11,9},{8,1... | collective-permute-start | bytes 589832 | tf_op jit(solution)/shard_map/ppermute | solution.py:29

commit v2 on v1

--- a/solution.py
+++ b/solution.py
@@ -62,15 +62,18 @@
 def outgoing_kernel(seed_ref, pre_ref, *refs):
     out_refs, sems = refs[:-1], refs[-1]
     here, count = lax.axis_index("space"), lax.axis_size("space")
+    micro = pre_ref.shape[0]
+    group = micro // count
     copies = []
     for distance, out_ref in enumerate(out_refs, 1):
-        group = out_ref.shape[1]
         span = pl.ds(peer(here, distance, count, back=True) * group, group)
-        for place, source in enumerate((seed_ref, pre_ref)):
+        pairs = (
+            (seed_ref.at[span], out_ref.at[pl.ds(0, group)]),
+            (pre_ref, out_ref.at[pl.ds(group, micro)]),
+        )
+        for place, (source, target) in enumerate(pairs):
             copies.append(
-                pltpu.make_async_copy(
-                    source.at[span], out_ref.at[place], sems.at[distance - 1, place]
-                )
+                pltpu.make_async_copy(source, target, sems.at[distance - 1, place])
             )
             copies[-1].start()
     for copy in copies:
@@ -84,7 +87,7 @@
     pairs = (
         (acts_ref, acts_rows),
         (seed_ref.at[mine], seed_out),
-        (pre_ref.at[mine], pre_out),
+        (pre_ref, pre_out),
         (conv_ref, conv_out),
         (proj_ref, proj_out),
     )
@@ -103,17 +106,26 @@
 
 def first_kernel(others, extent, *refs):
     seed_ref, pre_ref, arrived_refs = refs[0], refs[1], refs[2 : 2 + others]
-    conv_ref, proj_ref, grad_ref, pre_out_ref, out_ref, scratch = refs[2 + others :]
+    conv_ref, proj_ref, grad_ref, pre_out_ref, out_ref, seed_scratch, pre_scratch = refs[
+        2 + others :
+    ]
     here, count = lax.axis_index("space"), lax.axis_size("space")
-    depth_dev, channels = seed_ref.shape[1], seed_ref.shape[-1]
+    group, depth_dev = seed_ref.shape[:2]
+    channels = seed_ref.shape[-1]
     for distance in range(count):
         start = peer(here, distance, count) * depth_dev
-        for place, own_ref in enumerate((seed_ref, pre_ref)):
-            source = own_ref if distance == 0 else arrived_refs[distance - 1].at[place]
-            for depth in range(depth_dev):
-                scratch[place, :, start + depth] = source[:, depth].astype(jnp.float32)
-    for place, target in enumerate((grad_ref, pre_out_ref)):
-        target[...] = scratch[place].reshape(-1, channels).T.astype(jnp.bfloat16)
+        arrived = arrived_refs[distance - 1]
+        seeds = seed_ref if distance == 0 else arrived.at[pl.ds(0, group)]
+        pres = pre_ref if distance == 0 else arrived.at[pl.ds(group, group * count)]
+        for depth in range(depth_dev):
+            seed_scratch[:, start + depth] = seeds[:, depth].astype(jnp.float32)
+            pre_scratch[:, start + depth] = pres[:, depth].astype(jnp.float32)
+    grad_ref[...] = seed_scratch[...].reshape(-1, channels).T.astype(jnp.bfloat16)
+    for distance in range(count):
+        span = pl.ds(peer(here, distance, count) * group, group)
+        pre_out_ref[distance * channels : (distance + 1) * channels] = (
+            pre_scratch[span].reshape(-1, channels).T.astype(jnp.bfloat16)
+        )
     step_kernel(0, extent, grad_ref, pre_out_ref, conv_ref, proj_ref, out_ref)
 
 
@@ -122,7 +134,8 @@
 
     @pl.when(lax.axis_index("section") == lax.axis_size("section") - 1 - step)
     def _():
-        masked = pre_cotangent(grad_ref[...], pre_ref[...], proj_ref[...])
+        channels = grad_ref.shape[0]
+        masked = pre_cotangent(grad_ref[...], pre_ref[:channels], proj_ref[...])
         columns = jnp.concatenate(list(shifts(masked.astype(jnp.float32), extent, -1)), axis=0)
         weights = jnp.concatenate([conv_ref[tap] for tap in range(len(TAPS))], axis=1)
         total = grad_ref[...].astype(jnp.float32) + jnp.dot(
@@ -135,31 +148,39 @@
     parcel_refs, scratch = refs[:-1], refs[-1]
     place = lax.axis_index("dp")
     count = len(parcel_refs)
-    channels, lanes = pre_ref.shape
-    shard = channels // count
-    padded = parcel_refs[0].shape[0] - channels
+    size, lanes = pre_ref.shape
+    shard = acts_ref.shape[0] // count
+    padded = parcel_refs[0].shape[0] - size
     scratch[...] = acts_ref[...].astype(jnp.float32)
     for distance, parcel_ref in enumerate(parcel_refs):
         target = peer(place, distance, count, back=True)
         rows = scratch[pl.ds(pl.multiple_of(target * shard, shard), shard)]
         if padded > shard:
             rows = jnp.concatenate([rows, jnp.zeros((padded - shard, lanes), jnp.float32)], axis=0)
-        parcel_ref[:channels] = pre_ref[...]
-        parcel_ref[channels:] = rows.astype(jnp.bfloat16)
+        parcel_ref[:size] = pre_ref[...]
+        parcel_ref[size:] = rows.astype(jnp.bfloat16)
+
+
+def collect_kernel(*refs):
+    parcel_refs, mine_ref = refs[:-1], refs[-1]
+    padded = mine_ref.shape[0] // len(parcel_refs)
+    for place, parcel_ref in enumerate(parcel_refs):
+        first = parcel_ref.shape[0] - padded
+        mine_ref[place * padded : (place + 1) * padded] = parcel_ref[first:]
 
 
 def unfold_kernel(extent, group, shard, *refs):
-    parcel_refs, unfolded_ref, scratch = refs[:-2], refs[-2], refs[-1]
+    slab_refs, unfolded_ref, scratch = refs[:-2], refs[-2], refs[-1]
     here, owners = lax.axis_index("space"), lax.axis_size("space")
-    crops = len(parcel_refs) // owners
     depth_all, height, width = extent
     area = height * width
     depth_dev = depth_all // owners
     micro = group * owners
-    channels = parcel_refs[0].shape[0] - scratch.shape[2]
+    size = scratch.shape[2]
+    crops = slab_refs[0].shape[0] // size
     for crop in range(crops):
-        for distance in range(owners):
-            rows = parcel_refs[crop * owners + distance][channels:].astype(jnp.float32)
+        for distance, slab_ref in enumerate(slab_refs):
+            rows = slab_ref[crop * size : (crop + 1) * size].astype(jnp.float32)
             start = peer(here, distance, owners) * depth_dev
             for index in range(micro):
                 for depth in range(depth_dev):
@@ -173,15 +194,15 @@
             ]
             block = jnp.concatenate(pieces, axis=1)
             lanes = block.shape[1]
-            columns = jnp.concatenate(
-                [column.astype(jnp.float32) for column in shifts(block, extent, 1)], axis=0
-            )
+            columns = list(shifts(block, extent, 1))
+            if shard % 16:
+                columns = [column.astype(jnp.float32) for column in columns]
             distance = peer(owner, here, owners) if owners & (owners - 1) == 0 else lax.rem(
                 owner - here + owners, owners
             )
-            unfolded_ref[distance, :, crop * lanes : (crop + 1) * lanes] = columns.astype(
-                jnp.bfloat16
-            )
+            unfolded_ref[distance, :, crop * lanes : (crop + 1) * lanes] = jnp.concatenate(
+                columns, axis=0
+            ).astype(jnp.bfloat16)
 
 
 def choose_kernel(count, *refs):
@@ -201,18 +222,19 @@
         out_ref[place * size : (place + 1) * size] = block_ref[...]
 
 
-def block_terms(blocks, grad_refs, parcel_refs, proj_ref, masked_ref, shard):
+def block_terms(blocks, columns, grad_refs, parcel_refs, proj_ref, masked_ref, shard):
     here = lax.axis_index("dp")
     channels = proj_ref.shape[0]
     total = None
     for place, (ref_place, start) in enumerate(blocks):
         grad = grad_refs[ref_place][start : start + channels]
         parcel_ref = parcel_refs[place]
+        first = columns[place][1] * channels
         lanes = grad.shape[1]
         masked_ref[:, place * lanes : (place + 1) * lanes] = pre_cotangent(
-            grad, parcel_ref[:channels], proj_ref[...]
-        )
-        mine = parcel_ref[pl.ds(pl.multiple_of(here * shard, shard), shard)]
+            grad, parcel_ref[first : first + channels], proj_ref[...]
+        )
+        mine = parcel_ref[pl.ds(pl.multiple_of(first + here * shard, shard), shard)]
         hidden = jnp.maximum(mine.astype(jnp.float32), 0.0).astype(jnp.bfloat16)
         term = lax.dot_general(hidden, grad, CONTRACT_LANES, preferred_element_type=jnp.float32)
         total = term if total is None else total + term
@@ -228,7 +250,7 @@
     copies = []
     conv_out_ref, proj_out_ref, masked_ref = refs[:3]
     scale = scale_term if final else 1.0
-    proj_total = block_terms(blocks, grad_refs, parcel_refs, proj_ref, masked_ref, shard)
+    proj_total = block_terms(blocks, columns, grad_refs, parcel_refs, proj_ref, masked_ref, shard)
     if has_before:
         proj_total = before_refs[1][...] + proj_total
     proj_out_ref[...] = proj_total * scale
@@ -264,7 +286,7 @@
 def slab_kernel(extent, starts, *refs):
     owners = len(starts)
     grad_refs, refs = refs[:owners], refs[owners:]
-    pre_refs, (conv_ref, proj_ref, out_ref) = refs[:owners], refs[owners:]
+    pre_ref, conv_ref, proj_ref, out_ref = refs
     here = lax.axis_index("space")
     depth_all, height, width = extent
     area = height * width
@@ -283,9 +305,10 @@
         ]
 
     grads, masks = [[] for _ in range(depth_all)], [[] for _ in range(depth_all)]
-    for grad_ref, start, pre_ref in zip(grad_refs, starts, pre_refs):
+    for owner, (grad_ref, start) in enumerate(zip(grad_refs, starts)):
         grad = grad_ref[start : start + channels]
-        masked = pre_cotangent(grad, pre_ref[:channels], proj_ref[...])
+        pre = pre_ref[owner * channels : (owner + 1) * channels]
+        masked = pre_cotangent(grad, pre, proj_ref[...])
         for target, block in ((grads, grad), (masks, masked)):
             for z, pieces in enumerate(from_own(block.astype(jnp.float32))):
                 target[z] += pieces
@@ -325,7 +348,7 @@
     return [pltpu.with_memory_space_constraint(array, pltpu.HBM) for array in arrays]
 
 
-def kernel_call(body, name, operands, outs, scratch=(), in_specs=None, out_specs=None):
+def kernel_call(body, name, operands, outs, scratch=(), in_specs=None, out_specs=None, cost=None):
     single = not isinstance(outs, (tuple, list))
     count = 1 if single else len(outs)
     specs = out_specs or whole(count)
@@ -337,6 +360,7 @@
         scratch_shapes=list(scratch),
         compiler_params=pltpu.CompilerParams(vmem_limit_bytes=VMEM_LIMIT),
         name=name,
+        cost_estimate=cost,
     )(*operands)
 
 
@@ -361,14 +385,15 @@
     seeds = out_grad.reshape(acts.shape)
     volume = jax.ShapeDtypeStruct((channels, lanes), bfloat)
     part = jax.ShapeDtypeStruct((group, depth_dev, area, channels), bfloat)
-    parcel = jax.ShapeDtypeStruct((channels + padded, lanes), bfloat)
+    crop_volume = jax.ShapeDtypeStruct((slabs * channels, lanes), bfloat)
+    parcel = jax.ShapeDtypeStruct((slabs * channels + padded, lanes), bfloat)
     hbm = pl.BlockSpec(memory_space=pltpu.HBM)
 
     arrived = kernel_call(
         outgoing_kernel,
         "outgoing",
         kept_in_hbm(seeds, pre_acts),
-        [jax.ShapeDtypeStruct((2,) + part.shape, bfloat)] * others,
+        [jax.ShapeDtypeStruct((group + micro,) + part.shape[1:], bfloat)] * others,
         scratch=[pltpu.SemaphoreType.DMA((others, 2))],
         in_specs=[hbm] * 2,
     )
@@ -379,7 +404,7 @@
         kept_in_hbm(seeds, pre_acts, acts, conv_w[0], proj_w[0]),
         [
             part,
-            part,
+            jax.ShapeDtypeStruct(acts.shape, bfloat),
             volume,
             jax.ShapeDtypeStruct(conv_w.shape[1:], bfloat),
             jax.ShapeDtypeStruct(proj_w.shape[1:], bfloat),
@@ -391,13 +416,19 @@
         functools.partial(first_kernel, others, extent),
         "first_block",
         [seed_own, pre_own, *arrived, conv_weight, proj_weight],
-        [volume] * 3,
-        scratch=[pltpu.VMEM((2, group, depth_all, area, channels), jnp.float32)],
-    )
-
+        [volume, crop_volume, volume],
+        scratch=[
+            pltpu.VMEM((size, depth_all, area, channels), jnp.float32) for size in (group, micro)
+        ],
+    )
+
+    block_flops = 2 * channels * lanes * channels * (len(TAPS) + 1)
+    block_cost = pl.CostEstimate(
+        flops=block_flops, bytes_accessed=conv_w.size * 2, transcendentals=0
+    )
     results = [result]
     received = []
-    parcels = {}
+    parcels = []
     for step in range(1, section_count):
         received.append(lax.ppermute(results[-1], "section", hop_pairs(section_count, step)))
         if not parcels:
@@ -408,21 +439,24 @@
                 [parcel] * crops,
                 scratch=[pltpu.VMEM(volume.shape, jnp.float32)],
             )
-            parcels = {
-                (crop, slab): moved(sent[crop], crop, slab) if crop or slab else sent[0]
-                for crop in range(crops)
-                for slab in range(slabs)
-            }
+            parcels = [sent[0]] + [moved(sent[crop], crop, 0) for crop in range(1, crops)]
+            acts_mine = kernel_call(
+                collect_kernel,
+                "collect",
+                parcels,
+                jax.ShapeDtypeStruct((crops * padded, lanes), bfloat),
+            )
         if step == section_count - 1:
             break
-        earlier = [parcels[crop, 0] for crop in range(crops if step > 1 else 1)]
+        earlier = parcels[0] if step == 1 else acts_mine
         results.append(
             kernel_call(
                 functools.partial(step_kernel, step, extent),
                 "block",
-                [received[-1], pre_all, conv_weight, proj_weight, *earlier],
+                [received[-1], pre_all, conv_weight, proj_weight, earlier],
                 volume,
-                in_specs=whole(4) + unread(len(earlier)),
+                in_specs=whole(4) + unread(),
+                cost=block_cost,
             )
         )
 
@@ -430,7 +464,7 @@
     unfolded = kernel_call(
         functools.partial(unfold_kernel, extent, group, shard),
         "unfold",
-        [parcels[crop, slab] for crop in range(crops) for slab in range(slabs)],
+        [acts_mine] + [moved(acts_mine, 0, slab) for slab in range(1, slabs)],
         jax.ShapeDtypeStruct((slabs, taps * shard, crops * lanes), bfloat),
         scratch=[pltpu.VMEM((depth_all, micro, padded, area), jnp.float32)],
     )
@@ -448,7 +482,7 @@
 
     def weight_sums(arrays, blocks, columns, before, final):
         plan = (len(arrays), blocks, columns)
-        operands = [*arrays, *[parcels[column] for column in columns]]
+        operands = [*arrays, *[parcels[crop] for crop, _ in columns]]
         operands += [unfolded, proj_weight, *before]
         scratch = [pltpu.VMEM((channels, len(columns) * lanes), bfloat)]
         out_specs = whole(2)
@@ -501,8 +535,7 @@
         functools.partial(slab_kernel, extent, [start for _, start in slab_grads]),
         "own_slab",
         [block for block, _ in slab_grads]
-        + [parcels[0, slab] for slab in range(slabs)]
-        + [conv_weight, proj_weight],
+        + [pre_all, conv_weight, proj_weight],
         jax.ShapeDtypeStruct(acts.shape, bfloat),
     )
 

time: 40.5 us -> 37.7 us (0.931); the launches traced: 40.3 us -> 37 us
  waiting for transfers between devices: 8.59 us -> 6.59 us
  starting transfers between devices: 20.6 us -> 19.2 us
    ppermute x13 -> x10, starting transfers between devices: 13.1 us -> 10.1 us  [moved(): return lax.ppermute(block, ('dp', 'space'), pairs)]
    ppermute x13 -> x10, waiting for transfers between devices: 8.34 us -> 6.09 us  [moved(): return lax.ppermute(block, ('dp', 'space'), pairs)]
    ppermute x3, starting transfers between devices: 7.55 us -> 9.08 us  [shards(): lax.ppermute(results[-1], 'section', hop_pairs(section_count, step))]
    pallas_call x12 -> x13, Pallas kernels: 10.3 us -> 10.5 us  [kernel_call(): pl.pallas_call(body, out_shape=outs if single else tuple(outs), in_specs=...]
  transfers between devices with their start and end apart: 16 -> 13, of which waited for: 7 -> 8; matrix products, arithmetic and copies ran while one was open for 0% -> 0% of each run, Pallas kernels for 16% -> 18%
where the time goes in v2:
time: 37.7 us; the launch traced here: 37 us
  starting transfers between devices  19.2 us (51%)
  Pallas kernels  10.5 us (28%)
  waiting for transfers between devices  6.59 us (17%)
  between operations  0.7 us (2%)
    pallas_call x13, Pallas kernels, kernel_call(): pl.pallas_call(body, out_shape=outs if single else tuple(outs), in_specs=...  10.5 us
    ppermute x10, starting transfers between devices, moved(): return lax.ppermute(block, ('dp', 'space'), pairs)  10.1 us
    ppermute x3, starting transfers between devices, shards(): lax.ppermute(results[-1], 'section', hop_pairs(section_count, step))  9.08 us
    ppermute x10, waiting for transfers between devices, moved(): return lax.ppermute(block, ('dp', 'space'), pairs)  6.09 us
  transfers between devices with their start and end apart: 13, of which 8 were waited for; matrix products, arithmetic and copies ran while one was open for 0% of the time, Pallas kernels for 18%

profile of v2, /device:TPU:0, one launch (start us, length us, event | category | flops | bytes accessed | tf_op | source)
XLA Modules:
  0.0 37.0 jit_solution(14363354352421476862)
XLA Ops:
  0.6 0.9 %outgoing.1 = bf16[3,1,64,256]{3,2,1,0:T(8,128)(2,1)S(1)} custom-call(bf16[2,1,64,256]{3,2,1,0:T(8,128)(2,1)} %bitcast.15, bf16[2,1,64,256]{3,2,1,0:T(8,128)(2,1)} %bitcast.17), custom_call_target="tpu_custom_call" | custom-call | tf_op jit(solution)/shard_map/outgoing/pallas_call | solution.py:355
  1.5 3.0 %collective-permute-start = (bf16[3,1,64,256]{3,2,1,0:T(8,128)(2,1)S(1)}, bf16[3,1,64,256]{3,2,1,0:T(8,128)(2,1)S(1)}, u32[]{:S(2)}, u32[]{:S(2)}) collective-permute-start(bf16[3,1,64,256]{3,2,1,0:T(8,128)(2,1)S(1)} %outgoing.1), channel_id=1, source_target_pairs={{1,0},{0,1},{3,2},{2,3},{5,4},{4,5},{7,6},{6,7},{9,8},{8,9},{11,10... | collective-permute-start | bytes 294920 | tf_op jit(solution)/shard_map/ppermute | solution.py:29
  4.6 2.1 %prepare.1 = (bf16[1,1,64,256]{3,2,1,0:T(8,128)(2,1)S(1)}, bf16[2,1,64,256]{3,2,1,0:T(8,128)(2,1)S(1)}, bf16[256,128]{1,0:T(8,128)(2,1)S(1)}, bf16[27,256,256]{2,1,0:T(8,128)(2,1)S(1)}, bf16[256,256]{1,0:T(8,128)(2,1)S(1)}) custom-call(bf16[2,1,64,256]{3,2,1,0:T(8,128)(2,1)} %bitcast.16, bf16[2,1,64,256]{3,2,1,0:T(8,128)(2,1)} %bitcast.18, ...), custom_call_target="tpu_custom_call" | custom-call | tf_op jit(solution)/shard_map/prepare/pallas_call | solution.py:355
  6.7 0.6 %collective-permute-done.refs_2_ = bf16[3,1,64,256]{3,2,1,0:T(8,128)(2,1)S(1)} collective-permute-done((bf16[3,1,64,256]{3,2,1,0:T(8,128)(2,1)S(1)}, bf16[3,1,64,256]{3,2,1,0:T(8,128)(2,1)S(1)}, u32[]{:S(2)}, u32[]{:S(2)}) %collective-permute-start) | collective-permute-done | bytes 98336 | tf_op jit(solution)/shard_map/ppermute | solution.py:29
  7.3 0.2 first_block.1
  7.5 1.9 %collective-permute-start.1 = (bf16[256,128]{1,0:T(8,128)(2,1)S(1)}, bf16[256,128]{1,0:T(8,128)(2,1)S(1)}, u32[]{:S(2)}, u32[]{:S(2)}) collective-permute-start(bf16[256,128]{1,0:T(8,128)(2,1)S(1)} %get-tuple-element.24), channel_id=1, source_target_pairs={{8,0},{0,8},{24,16},{16,24},{9,1},{1,9},{25,17},{17,25},{10,2},{2,... | collective-permute-start | bytes 196616 | tf_op jit(solution)/shard_map/ppermute | solution.py:433
  9.5 0.1 pack.1
  9.5 0.1 collective-permute-start.3
  9.6 1.6 %collective-permute-start.4 = (bf16[576,128]{1,0:T(8,128)(2,1)S(1)}, bf16[576,128]{1,0:T(8,128)(2,1)S(1)}, u32[]{:S(2)}, u32[]{:S(2)}) collective-permute-start(bf16[576,128]{1,0:T(8,128)(2,1)S(1)} %get-tuple-element.29), channel_id=1, source_target_pairs={{4,0},{5,1},{6,2},{7,3},{0,4},{1,5},{2,6},{3,7},{12,8},{13,9},{14,... | collective-permute-start | bytes 442376 | tf_op jit(solution)/shard_map/ppermute | solution.py:29
  11.2 0.3 collective-permute-start.5
  11.5 0.4 collective-permute-done.1.grad_ref.refs_1_
  11.8 5.3 %collective-permute-start.2 = (bf16[256,128]{1,0:T(8,128)(2,1)S(1)}, bf16[256,128]{1,0:T(8,128)(2,1)S(1)}, u32[]{:S(2)}, u32[]{:S(2)}) collective-permute-start(bf16[256,128]{1,0:T(8,128)(2,1)S(1)} %block.2), channel_id=1, source_target_pairs={{8,0},{16,8},{24,16},{0,24},{9,1},{17,9},{25,17},{1,25},{10,2},{18... | collective-permute-start | bytes 196616 | tf_op jit(solution)/shard_map/ppermute | solution.py:433
  17.1 0.0 collective-permute-done.3.refs_1_.refs_3_.refs_5_
  17.1 0.0 collective-permute-done.4.refs_2_.refs_3_.refs_4_
  17.1 1.5 %collective-permute-done.5.refs_3_.refs_6_.refs_7_ = bf16[576,128]{1,0:T(8,128)(2,1)S(1)} collective-permute-done((bf16[576,128]{1,0:T(8,128)(2,1)S(1)}, bf16[576,128]{1,0:T(8,128)(2,1)S(1)}, u32[]{:S(2)}, u32[]{:S(2)}) %collective-permute-start.5) | collective-permute-done | bytes 147488 | tf_op jit(solution)/shard_map/ppermute | solution.py:29
  18.6 1.5 %collective-permute-start.7 = (bf16[256,128]{1,0:T(8,128)(2,1)S(1)}, bf16[256,128]{1,0:T(8,128)(2,1)S(1)}, u32[]{:S(2)}, u32[]{:S(2)}) collective-permute-start(bf16[256,128]{1,0:T(8,128)(2,1)S(1)} %collect.1.refs_0_), channel_id=1, source_target_pairs={{1,0},{0,1},{3,2},{2,3},{5,4},{4,5},{7,6},{6,7},{9,8},{8,9},{11,10... | collective-permute-start | bytes 196616 | tf_op jit(solution)/shard_map/ppermute | solution.py:29
  20.1 0.0 collective-permute-done.2.grad_ref.refs_2_
  20.1 1.9 %collective-permute-start.6 = (bf16[256,128]{1,0:T(8,128)(2,1)S(1)}, bf16[256,128]{1,0:T(8,128)(2,1)S(1)}, u32[]{:S(2)}, u32[]{:S(2)}) collective-permute-start(bf16[256,128]{1,0:T(8,128)(2,1)S(1)} %block.3), channel_id=1, source_target_pairs={{8,0},{0,8},{24,16},{16,24},{9,1},{1,9},{25,17},{17,25},{10,2},{2,... | collective-permute-start | bytes 196616 | tf_op jit(solution)/shard_map/ppermute | solution.py:433
  22.0 0.9 %collective-permute-done.7.refs_1_ = bf16[256,128]{1,0:T(8,128)(2,1)S(1)} collective-permute-done((bf16[256,128]{1,0:T(8,128)(2,1)S(1)}, bf16[256,128]{1,0:T(8,128)(2,1)S(1)}, u32[]{:S(2)}, u32[]{:S(2)}) %collective-permute-start.7) | collective-permute-done | bytes 65568 | tf_op jit(solution)/shard_map/ppermute | solution.py:29
  22.9 1.5 %unfold.1.refs_4_.refs_8_ = bf16[2,1728,512]{2,1,0:T(8,128)(2,1)S(1)} custom-call(bf16[256,128]{1,0:T(8,128)(2,1)S(1)} %collect.1.refs_0_, bf16[256,128]{1,0:T(8,128)(2,1)S(1)} %collective-permute-done.7.refs_1_), custom_call_target="tpu_custom_call" | custom-call | tf_op jit(solution)/shard_map/unfold/pallas_call | solution.py:355
  24.4 0.1 collective-permute-done.6.refs_3_
  24.5 0.0 collective-permute-start.11
  24.6 2.5 %collective-permute-start.10 = (bf16[256,128]{1,0:T(8,128)(2,1)S(1)}, bf16[256,128]{1,0:T(8,128)(2,1)S(1)}, u32[]{:S(2)}, u32[]{:S(2)}) collective-permute-start(bf16[256,128]{1,0:T(8,128)(2,1)S(1)} %choose.1.refs_0_), channel_id=1, source_target_pairs={{5,0},{4,1},{7,2},{6,3},{1,4},{0,5},{3,6},{2,7},{13,8},{12,9},{15,... | collective-permute-start | bytes 196616 | tf_op jit(solution)/shard_map/ppermute | solution.py:29
  27.0 0.5 %collective-permute-start.9 = (bf16[256,128]{1,0:T(8,128)(2,1)S(1)}, bf16[256,128]{1,0:T(8,128)(2,1)S(1)}, u32[]{:S(2)}, u32[]{:S(2)}) collective-permute-start(bf16[256,128]{1,0:T(8,128)(2,1)S(1)} %choose.1.refs_0_), channel_id=1, source_target_pairs={{4,0},{5,1},{6,2},{7,3},{0,4},{1,5},{2,6},{3,7},{12,8},{13,9},{14,... | collective-permute-start | bytes 196616 | tf_op jit(solution)/shard_map/ppermute | solution.py:29
  27.6 0.5 %collective-permute-start.8 = (bf16[256,128]{1,0:T(8,128)(2,1)S(1)}, bf16[256,128]{1,0:T(8,128)(2,1)S(1)}, u32[]{:S(2)}, u32[]{:S(2)}) collective-permute-start(bf16[256,128]{1,0:T(8,128)(2,1)S(1)} %choose.1.refs_0_), channel_id=1, source_target_pairs={{1,0},{0,1},{3,2},{2,3},{5,4},{4,5},{7,6},{6,7},{9,8},{8,9},{11,10... | collective-permute-start | bytes 196616 | tf_op jit(solution)/shard_map/ppermute | solution.py:29
  28.1 0.0 collective-permute-done.11.refs_1_
  28.1 0.6 %part_weight_grads.1 = (f32[1728,256]{1,0:T(8,128)S(1)}, f32[64,256]{1,0:T(8,128)S(1)}) custom-call(bf16[256,128]{1,0:T(8,128)(2,1)S(1)} %choose.1.refs_0_, bf16[256,128]{1,0:T(8,128)(2,1)S(1)} %collective-permute-done.11.refs_1_, bf16[576,128]{1,0:T(8,128)(2,1)S(1)} %get-tuple-element.27.refs_0_.refs_2_, ...), custom_call_target="tpu_custom_call" | custom-call | tf_op jit(solution)/shard_map/part_weight_grads/pallas_call | solution.py:355
  28.8 1.4 %collective-permute-done.10.refs_2_ = bf16[256,128]{1,0:T(8,128)(2,1)S(1)} collective-permute-done((bf16[256,128]{1,0:T(8,128)(2,1)S(1)}, bf16[256,128]{1,0:T(8,128)(2,1)S(1)}, u32[]{:S(2)}, u32[]{:S(2)}) %collective-permute-start.10) | collective-permute-done | bytes 65568 | tf_op jit(solution)/shard_map/ppermute | solution.py:29
  30.2 1.2 %collective-permute-done.9.refs_1_ = bf16[256,128]{1,0:T(8,128)(2,1)S(1)} collective-permute-done((bf16[256,128]{1,0:T(8,128)(2,1)S(1)}, bf16[256,128]{1,0:T(8,128)(2,1)S(1)}, u32[]{:S(2)}, u32[]{:S(2)}) %collective-permute-start.9) | collective-permute-done | bytes 65568 | tf_op jit(solution)/shard_map/ppermute | solution.py:29
  31.4 0.4 %collective-permute-done.8.refs_0_ = bf16[256,128]{1,0:T(8,128)(2,1)S(1)} collective-permute-done((bf16[256,128]{1,0:T(8,128)(2,1)S(1)}, bf16[256,128]{1,0:T(8,128)(2,1)S(1)}, u32[]{:S(2)}, u32[]{:S(2)}) %collective-permute-start.8) | collective-permute-done | bytes 65568 | tf_op jit(solution)/shard_map/ppermute | solution.py:29
  31.9 0.1 collective-permute-start.12
  31.9 2.2 %own_slab.1 = bf16[2,1,64,256]{3,2,1,0:T(8,128)(2,1)} custom-call(bf16[256,128]{1,0:T(8,128)(2,1)S(1)} %choose.1.refs_0_, bf16[768,128]{1,0:T(8,128)(2,1)S(1)} %hand_on.1.refs_1_.refs_0_, bf16[512,128]{1,0:T(8,128)(2,1)S(1)} %get-tuple-element.25.pre_ref.refs_2_, bf16[27,256,256]{2,1,0:T(8,128)(2,1)S(1)} %get-tuple-element.21.refs_3_.conv_ref, ...), custom_call_target="tpu_custom_call" | custom-call | tf_op jit(solution)/shard_map/own_slab/pallas_call | solution.py:355
  34.1 0.0 collective-permute-done.12.refs_1_
  34.1 2.9 %weight_grads.1 = (f32[1728,256]{1,0:T(8,128)}, f32[64,256]{1,0:T(8,128)}) custom-call(bf16[768,128]{1,0:T(8,128)(2,1)S(1)} %hand_on.1.refs_1_.refs_0_, bf16[768,128]{1,0:T(8,128)(2,1)S(1)} %collective-permute-done.12.refs_1_, bf16[576,128]{1,0:T(8,128)(2,1)S(1)} %get-tuple-element.27.refs_0_.refs_2_, ...), custom_call_target="tpu_custom_call" | custom-call | tf_op jit(solution)/shard_map/weight_grads/pallas_call | solution.py:355
  (5 shorter events, 0.0 us)
Async XLA Ops:
  1.5 5.8 %collective-permute-start = (bf16[3,1,64,256]{3,2,1,0:T(8,128)(2,1)S(1)}, bf16[3,1,64,256]{3,2,1,0:T(8,128)(2,1)S(1)}, u32[]{:S(2)}, u32[]{:S(2)}) collective-permute-start(bf16[3,1,64,256]{3,2,1,0:T(8,128)(2,1)S(1)} %outgoing.1), channel_id=1, source_target_pairs={{1,0},{0,1},{3,2},{2,3},{5,4},{4,5},{7,6},{6,7},{9,8},{8,9},{11,10... | collective-permute-start | bytes 294920 | tf_op jit(solution)/shard_map/ppermute | solution.py:29
  7.5 4.3 %collective-permute-start.1 = (bf16[256,128]{1,0:T(8,128)(2,1)S(1)}, bf16[256,128]{1,0:T(8,128)(2,1)S(1)}, u32[]{:S(2)}, u32[]{:S(2)}) collective-permute-start(bf16[256,128]{1,0:T(8,128)(2,1)S(1)} %get-tuple-element.24), channel_id=1, source_target_pairs={{8,0},{0,8},{24,16},{16,24},{9,1},{1,9},{25,17},{17,25},{10,2},{2,... | collective-permute-start | bytes 196616 | tf_op jit(solution)/shard_map/ppermute | solution.py:433
  9.5 7.6 %collective-permute-start.3 = (bf16[576,128]{1,0:T(8,128)(2,1)S(1)}, bf16[576,128]{1,0:T(8,128)(2,1)S(1)}, u32[]{:S(2)}, u32[]{:S(2)}) collective-permute-start(bf16[576,128]{1,0:T(8,128)(2,1)S(1)} %get-tuple-element.28), channel_id=1, source_target_pairs={{2,0},{3,1},{0,2},{1,3},{6,4},{7,5},{4,6},{5,7},{10,8},{11,9},{8,1... | collective-permute-start | bytes 442376 | tf_op jit(solution)/shard_map/ppermute | solution.py:29
  9.6 7.5 %collective-permute-start.4 = (bf16[576,128]{1,0:T(8,128)(2,1)S(1)}, bf16[576,128]{1,0:T(8,128)(2,1)S(1)}, u32[]{:S(2)}, u32[]{:S(2)}) collective-permute-start(bf16[576,128]{1,0:T(8,128)(2,1)S(1)} %get-tuple-element.29), channel_id=1, source_target_pairs={{4,0},{5,1},{6,2},{7,3},{0,4},{1,5},{2,6},{3,7},{12,8},{13,9},{14,... | collective-permute-start | bytes 442376 | tf_op jit(solution)/shard_map/ppermute | solution.py:29
  11.2 7.4 %collective-permute-start.5 = (bf16[576,128]{1,0:T(8,128)(2,1)S(1)}, bf16[576,128]{1,0:T(8,128)(2,1)S(1)}, u32[]{:S(2)}, u32[]{:S(2)}) collective-permute-start(bf16[576,128]{1,0:T(8,128)(2,1)S(1)} %get-tuple-element.30), channel_id=1, source_target_pairs={{6,0},{7,1},{4,2},{5,3},{2,4},{3,5},{0,6},{1,7},{14,8},{15,9},{12,... | collective-permute-start | bytes 442376 | tf_op jit(solution)/shard_map/ppermute | solution.py:29
  11.8 8.3 %collective-permute-start.2 = (bf16[256,128]{1,0:T(8,128)(2,1)S(1)}, bf16[256,128]{1,0:T(8,128)(2,1)S(1)}, u32[]{:S(2)}, u32[]{:S(2)}) collective-permute-start(bf16[256,128]{1,0:T(8,128)(2,1)S(1)} %block.2), channel_id=1, source_target_pairs={{8,0},{16,8},{24,16},{0,24},{9,1},{17,9},{25,17},{1,25},{10,2},{18... | collective-permute-start | bytes 196616 | tf_op jit(solution)/shard_map/ppermute | solution.py:433
  18.6 4.3 %collective-permute-start.7 = (bf16[256,128]{1,0:T(8,128)(2,1)S(1)}, bf16[256,128]{1,0:T(8,128)(2,1)S(1)}, u32[]{:S(2)}, u32[]{:S(2)}) collective-permute-start(bf16[256,128]{1,0:T(8,128)(2,1)S(1)} %collect.1.refs_0_), channel_id=1, source_target_pairs={{1,0},{0,1},{3,2},{2,3},{5,4},{4,5},{7,6},{6,7},{9,8},{8,9},{11,10... | collective-permute-start | bytes 196616 | tf_op jit(solution)/shard_map/ppermute | solution.py:29
  20.1 4.4 %collective-permute-start.6 = (bf16[256,128]{1,0:T(8,128)(2,1)S(1)}, bf16[256,128]{1,0:T(8,128)(2,1)S(1)}, u32[]{:S(2)}, u32[]{:S(2)}) collective-permute-start(bf16[256,128]{1,0:T(8,128)(2,1)S(1)} %block.3), channel_id=1, source_target_pairs={{8,0},{0,8},{24,16},{16,24},{9,1},{1,9},{25,17},{17,25},{10,2},{2,... | collective-permute-start | bytes 196616 | tf_op jit(solution)/shard_map/ppermute | solution.py:433
  24.5 3.6 %collective-permute-start.11 = (bf16[256,128]{1,0:T(8,128)(2,1)S(1)}, bf16[256,128]{1,0:T(8,128)(2,1)S(1)}, u32[]{:S(2)}, u32[]{:S(2)}) collective-permute-start(bf16[256,128]{1,0:T(8,128)(2,1)S(1)} %choose.1.refs_0_), channel_id=1, source_target_pairs={{2,0},{3,1},{0,2},{1,3},{6,4},{7,5},{4,6},{5,7},{10,8},{11,9},{8,1... | collective-permute-start | bytes 196616 | tf_op jit(solution)/shard_map/ppermute | solution.py:29
  24.6 5.6 %collective-permute-start.10 = (bf16[256,128]{1,0:T(8,128)(2,1)S(1)}, bf16[256,128]{1,0:T(8,128)(2,1)S(1)}, u32[]{:S(2)}, u32[]{:S(2)}) collective-permute-start(bf16[256,128]{1,0:T(8,128)(2,1)S(1)} %choose.1.refs_0_), channel_id=1, source_target_pairs={{5,0},{4,1},{7,2},{6,3},{1,4},{0,5},{3,6},{2,7},{13,8},{12,9},{15,... | collective-permute-start | bytes 196616 | tf_op jit(solution)/shard_map/ppermute | solution.py:29
  27.0 4.4 %collective-permute-start.9 = (bf16[256,128]{1,0:T(8,128)(2,1)S(1)}, bf16[256,128]{1,0:T(8,128)(2,1)S(1)}, u32[]{:S(2)}, u32[]{:S(2)}) collective-permute-start(bf16[256,128]{1,0:T(8,128)(2,1)S(1)} %choose.1.refs_0_), channel_id=1, source_target_pairs={{4,0},{5,1},{6,2},{7,3},{0,4},{1,5},{2,6},{3,7},{12,8},{13,9},{14,... | collective-permute-start | bytes 196616 | tf_op jit(solution)/shard_map/ppermute | solution.py:29
  27.6 4.3 %collective-permute-start.8 = (bf16[256,128]{1,0:T(8,128)(2,1)S(1)}, bf16[256,128]{1,0:T(8,128)(2,1)S(1)}, u32[]{:S(2)}, u32[]{:S(2)}) collective-permute-start(bf16[256,128]{1,0:T(8,128)(2,1)S(1)} %choose.1.refs_0_), channel_id=1, source_target_pairs={{1,0},{0,1},{3,2},{2,3},{5,4},{4,5},{7,6},{6,7},{9,8},{8,9},{11,10... | collective-permute-start | bytes 196616 | tf_op jit(solution)/shard_map/ppermute | solution.py:29
  31.9 2.3 %collective-permute-start.12 = (bf16[768,128]{1,0:T(8,128)(2,1)S(1)}, bf16[768,128]{1,0:T(8,128)(2,1)S(1)}, u32[]{:S(2)}, u32[]{:S(2)}) collective-permute-start(bf16[768,128]{1,0:T(8,128)(2,1)S(1)} %hand_on.1.refs_1_.refs_0_), channel_id=1, source_target_pairs={{2,0},{3,1},{0,2},{1,3},{6,4},{7,5},{4,6},{5,7},{10,8},{11,9},{8,1... | collective-permute-start | bytes 589832 | tf_op jit(solution)/shard_map/ppermute | solution.py:29

commit v3 on v2

--- a/solution.py
+++ b/solution.py
@@ -205,8 +205,8 @@
             ).astype(jnp.bfloat16)
 
 
-def choose_kernel(count, *refs):
-    step_refs, grad_ref = refs[:count], refs[-1]
+def early_kernel(count, *refs):
+    step_refs, grad_ref = refs[:-2], refs[-1]
     section = lax.axis_index("section")
     for step, step_ref in enumerate(step_refs):
 
@@ -215,11 +215,25 @@
             grad_ref[...] = step_ref[...]
 
 
-def hand_on_kernel(count, *refs):
+def join_kernel(count, *refs):
     out_ref = refs[-1]
     for place, block_ref in enumerate(refs[:count]):
         size = block_ref.shape[0]
         out_ref[place * size : (place + 1) * size] = block_ref[...]
+
+
+def choose_kernel(*refs):
+    early_refs, out_ref = refs[:-2], refs[-1]
+
+    @pl.when(lax.axis_index("section") > 0)
+    def _():
+        for place, block_ref in enumerate(early_refs):
+            size = block_ref.shape[0]
+            out_ref[place * size : (place + 1) * size] = block_ref[...]
+
+
+def pass_kernel(block_ref, *refs):
+    refs[-1][...] = block_ref[...]
 
 
 def block_terms(blocks, columns, grad_refs, parcel_refs, proj_ref, masked_ref, shard):
@@ -348,7 +362,7 @@
     return [pltpu.with_memory_space_constraint(array, pltpu.HBM) for array in arrays]
 
 
-def kernel_call(body, name, operands, outs, scratch=(), in_specs=None, out_specs=None, cost=None):
+def kernel_call(body, name, operands, outs, scratch=(), in_specs=None, out_specs=None, **options):
     single = not isinstance(outs, (tuple, list))
     count = 1 if single else len(outs)
     specs = out_specs or whole(count)
@@ -360,7 +374,7 @@
         scratch_shapes=list(scratch),
         compiler_params=pltpu.CompilerParams(vmem_limit_bytes=VMEM_LIMIT),
         name=name,
-        cost_estimate=cost,
+        **options,
     )(*operands)
 
 
@@ -456,7 +470,7 @@
                 [received[-1], pre_all, conv_weight, proj_weight, earlier],
                 volume,
                 in_specs=whole(4) + unread(),
-                cost=block_cost,
+                cost_estimate=block_cost,
             )
         )
 
@@ -468,12 +482,41 @@
         jax.ShapeDtypeStruct((slabs, taps * shard, crops * lanes), bfloat),
         scratch=[pltpu.VMEM((depth_all, micro, padded, area), jnp.float32)],
     )
-    grad_own = kernel_call(
-        functools.partial(choose_kernel, section_count),
-        "choose",
-        [grad_first, *received, unfolded],
+    late = [received[-1]] + [
+        lax.ppermute(
+            results[-1],
+            ("section", "space"),
+            [
+                (source * slabs + peer(i, slab, slabs), target * slabs + i)
+                for source, target in hop_pairs(section_count, section_count - 1)
+                for i in range(slabs)
+            ],
+        )
+        for slab in range(1, slabs)
+    ]
+    early = kernel_call(
+        functools.partial(early_kernel, section_count),
+        "early",
+        [grad_first, *received[:-1], results[-1]],
         volume,
-        in_specs=whole(section_count) + unread(),
+        in_specs=whole(section_count - 1) + unread(),
+    )
+    early = [early] + [moved(early, 0, slab) for slab in range(1, slabs)]
+    crop_grad = kernel_call(
+        functools.partial(join_kernel, slabs),
+        "join",
+        [*late, unfolded],
+        crop_volume,
+        in_specs=whole(slabs) + unread(),
+    )
+    crop_grad = kernel_call(
+        choose_kernel, "choose", [*early, crop_grad], crop_volume, input_output_aliases={slabs: 0}
+    )
+    section_out = kernel_call(
+        functools.partial(slab_kernel, extent, [slab * channels for slab in range(slabs)]),
+        "own_slab",
+        [crop_grad] * slabs + [pre_all, conv_weight, proj_weight],
+        jax.ShapeDtypeStruct(acts.shape, bfloat),
     )
 
     conv_shape = jax.ShapeDtypeStruct((taps * shard, channels), jnp.float32)
@@ -500,44 +543,30 @@
             out_specs=out_specs,
         )
 
+    def plan_of(distances):
+        columns = [(crop, slab) for crop in distances for slab in range(slabs)]
+        blocks = [
+            (place, slab * channels) for place in range(len(distances)) for slab in range(slabs)
+        ]
+        return blocks, columns
+
     near = crops // 2
     if near < 2 or crops & (crops - 1):
-        columns = [(crop, slab) for crop in range(crops) for slab in range(slabs)]
-        arrays = [moved(grad_own, *column) if any(column) else grad_own for column in columns]
-        blocks = [(place, 0) for place in range(len(columns))]
-        conv_rows, proj_rows = weight_sums(arrays, blocks, columns, (), True)
-        slab_grads = [(arrays[columns.index((0, slab))], 0) for slab in range(slabs)]
+        arrays = [moved(crop_grad, crop, 0) if crop else crop_grad for crop in range(crops)]
+        conv_rows, proj_rows = weight_sums(arrays, *plan_of(range(crops)), (), True)
     else:
-        across = [moved(grad_own, near, slab) for slab in range(slabs)]
-        beside = [moved(grad_own, 0, slab) for slab in range(1, slabs)]
-        columns = [(crop, 0) for crop in range(near)]
-        arrays = [grad_own] + [moved(grad_own, crop, 0) for crop in range(1, near)]
-        blocks = [(place, 0) for place in range(near)]
-        sums = weight_sums(arrays, blocks, columns, (), False)
-        middle = beside + across
-        handed = kernel_call(
-            functools.partial(hand_on_kernel, len(middle)),
+        across = moved(crop_grad, near, 0)
+        arrays = [crop_grad] + [moved(crop_grad, crop, 0) for crop in range(1, near)]
+        sums = weight_sums(arrays, *plan_of(range(near)), (), False)
+        across = kernel_call(
+            pass_kernel,
             "hand_on",
-            [*middle, sums[1]],
-            jax.ShapeDtypeStruct((len(middle) * channels, lanes), bfloat),
-            in_specs=whole(len(middle)) + unread(),
-        )
-        places = [(0, slab) for slab in range(1, slabs)] + [(near, slab) for slab in range(slabs)]
-        columns = [(crop + place, slab) for crop in range(near) for place, slab in places]
-        arrays = [handed] + [moved(handed, crop, 0) for crop in range(1, near)]
-        blocks = [
-            (array, place * channels) for array in range(near) for place in range(len(places))
-        ]
-        conv_rows, proj_rows = weight_sums(arrays, blocks, columns, sums, True)
-        slab_grads = [(grad_own, 0)] + [(handed, place * channels) for place in range(others)]
-
-    section_out = kernel_call(
-        functools.partial(slab_kernel, extent, [start for _, start in slab_grads]),
-        "own_slab",
-        [block for block, _ in slab_grads]
-        + [pre_all, conv_weight, proj_weight],
-        jax.ShapeDtypeStruct(acts.shape, bfloat),
-    )
+            [across, *kept_in_hbm(section_out)],
+            crop_volume,
+            in_specs=whole() + unread(),
+        )
+        arrays = [across] + [moved(across, crop, 0) for crop in range(1, near)]
+        conv_rows, proj_rows = weight_sums(arrays, *plan_of(range(near, crops)), sums, True)
 
     section_grads = section_out.reshape(inputs.shape)
     grad_conv = conv_rows.reshape(taps, shard, channels).swapaxes(0, 1)[None]

time: 37.7 us -> 35.9 us (0.952); the launches traced: 37 us -> 35.7 us
  waiting for transfers between devices: 6.59 us -> 5.67 us
  starting transfers between devices: 19.2 us -> 18.8 us
    ppermute x10 -> x9, waiting for transfers between devices: 6.09 us -> 3.79 us  [moved(): return lax.ppermute(block, ('dp', 'space'), pairs)]
    ppermute x0 -> x1, starting transfers between devices: none -> 2.28 us  [shards(): lax.ppermute(results[-1], ('section', 'space'), [(source * slabs + peer(i...]
    ppermute x3, starting transfers between devices: 9.08 us -> 7.21 us  [shards(): lax.ppermute(results[-1], 'section', hop_pairs(section_count, step))]
    ppermute x3, waiting for transfers between devices: 0.5 us -> 1.67 us  [shards(): lax.ppermute(results[-1], 'section', hop_pairs(section_count, step))]
    ppermute x10 -> x9, starting transfers between devices: 10.1 us -> 9.32 us  [moved(): return lax.ppermute(block, ('dp', 'space'), pairs)]
    pallas_call x13 -> x15, Pallas kernels: 10.5 us -> 10.6 us  [kernel_call(): pl.pallas_call(body, out_shape=outs if single else tuple(outs), in_specs=...]
  transfers between devices with their start and end apart: 13 -> 13, of which waited for: 8 -> 7; matrix products, arithmetic and copies ran while one was open for 0% -> 0% of each run, Pallas kernels for 18% -> 19%
where the time goes in v3:
time: 35.9 us; the launch traced here: 35.7 us
  starting transfers between devices  18.8 us (52%)
  Pallas kernels  10.6 us (30%)
  waiting for transfers between devices  5.67 us (16%)
  between operations  0.72 us (2%)
    pallas_call x15, Pallas kernels, kernel_call(): pl.pallas_call(body, out_shape=outs if single else tuple(outs), in_specs=...  10.6 us
    ppermute x9, starting transfers between devices, moved(): return lax.ppermute(block, ('dp', 'space'), pairs)  9.32 us
    ppermute x3, starting transfers between devices, shards(): lax.ppermute(results[-1], 'section', hop_pairs(section_count, step))  7.21 us
    ppermute x9, waiting for transfers between devices, moved(): return lax.ppermute(block, ('dp', 'space'), pairs)  3.79 us
    ppermute x1, starting transfers between devices, shards(): lax.ppermute(results[-1], ('section', 'space'), [(source * slabs + peer(i...  2.28 us
    ppermute x3, waiting for transfers between devices, shards(): lax.ppermute(results[-1], 'section', hop_pairs(section_count, step))  1.67 us
  transfers between devices with their start and end apart: 13, of which 7 were waited for; matrix products, arithmetic and copies ran while one was open for 0% of the time, Pallas kernels for 19%

profile of v3, /device:TPU:0, one launch (start us, length us, event | category | flops | bytes accessed | tf_op | source)
XLA Modules:
  0.0 35.7 jit_solution(12010238814326185984)
XLA Ops:
  0.6 0.9 %outgoing.1 = bf16[3,1,64,256]{3,2,1,0:T(8,128)(2,1)S(1)} custom-call(bf16[2,1,64,256]{3,2,1,0:T(8,128)(2,1)} %bitcast.15, bf16[2,1,64,256]{3,2,1,0:T(8,128)(2,1)} %bitcast.17), custom_call_target="tpu_custom_call" | custom-call | tf_op jit(solution)/shard_map/outgoing/pallas_call | solution.py:369
  1.5 3.0 %collective-permute-start = (bf16[3,1,64,256]{3,2,1,0:T(8,128)(2,1)S(1)}, bf16[3,1,64,256]{3,2,1,0:T(8,128)(2,1)S(1)}, u32[]{:S(2)}, u32[]{:S(2)}) collective-permute-start(bf16[3,1,64,256]{3,2,1,0:T(8,128)(2,1)S(1)} %outgoing.1), channel_id=1, source_target_pairs={{1,0},{0,1},{3,2},{2,3},{5,4},{4,5},{7,6},{6,7},{9,8},{8,9},{11,10... | collective-permute-start | bytes 294920 | tf_op jit(solution)/shard_map/ppermute | solution.py:29
  4.6 2.1 %prepare.1 = (bf16[1,1,64,256]{3,2,1,0:T(8,128)(2,1)S(1)}, bf16[2,1,64,256]{3,2,1,0:T(8,128)(2,1)S(1)}, bf16[256,128]{1,0:T(8,128)(2,1)S(1)}, bf16[27,256,256]{2,1,0:T(8,128)(2,1)S(1)}, bf16[256,256]{1,0:T(8,128)(2,1)S(1)}) custom-call(bf16[2,1,64,256]{3,2,1,0:T(8,128)(2,1)} %bitcast.16, bf16[2,1,64,256]{3,2,1,0:T(8,128)(2,1)} %bitcast.18, ...), custom_call_target="tpu_custom_call" | custom-call | tf_op jit(solution)/shard_map/prepare/pallas_call | solution.py:369
  6.7 0.6 %collective-permute-done.refs_2_ = bf16[3,1,64,256]{3,2,1,0:T(8,128)(2,1)S(1)} collective-permute-done((bf16[3,1,64,256]{3,2,1,0:T(8,128)(2,1)S(1)}, bf16[3,1,64,256]{3,2,1,0:T(8,128)(2,1)S(1)}, u32[]{:S(2)}, u32[]{:S(2)}) %collective-permute-start) | collective-permute-done | bytes 98336 | tf_op jit(solution)/shard_map/ppermute | solution.py:29
  7.3 0.2 first_block.1
  7.5 1.9 %collective-permute-start.1 = (bf16[256,128]{1,0:T(8,128)(2,1)S(1)}, bf16[256,128]{1,0:T(8,128)(2,1)S(1)}, u32[]{:S(2)}, u32[]{:S(2)}) collective-permute-start(bf16[256,128]{1,0:T(8,128)(2,1)S(1)} %get-tuple-element.24), channel_id=1, source_target_pairs={{8,0},{0,8},{24,16},{16,24},{9,1},{1,9},{25,17},{17,25},{10,2},{2,... | collective-permute-start | bytes 196616 | tf_op jit(solution)/shard_map/ppermute | solution.py:447
  9.5 0.1 pack.1
  9.5 0.1 collective-permute-start.3
  9.6 1.6 %collective-permute-start.4 = (bf16[576,128]{1,0:T(8,128)(2,1)S(1)}, bf16[576,128]{1,0:T(8,128)(2,1)S(1)}, u32[]{:S(2)}, u32[]{:S(2)}) collective-permute-start(bf16[576,128]{1,0:T(8,128)(2,1)S(1)} %get-tuple-element.29), channel_id=1, source_target_pairs={{4,0},{5,1},{6,2},{7,3},{0,4},{1,5},{2,6},{3,7},{12,8},{13,9},{14,... | collective-permute-start | bytes 442376 | tf_op jit(solution)/shard_map/ppermute | solution.py:29
  11.2 0.3 collective-permute-start.5
  11.5 0.4 %collective-permute-done.1.grad_ref.refs_1_ = bf16[256,128]{1,0:T(8,128)(2,1)S(1)} collective-permute-done((bf16[256,128]{1,0:T(8,128)(2,1)S(1)}, bf16[256,128]{1,0:T(8,128)(2,1)S(1)}, u32[]{:S(2)}, u32[]{:S(2)}) %collective-permute-start.1) | collective-permute-done | bytes 65568 | tf_op jit(solution)/shard_map/ppermute | solution.py:447
  11.8 5.3 %collective-permute-start.2 = (bf16[256,128]{1,0:T(8,128)(2,1)S(1)}, bf16[256,128]{1,0:T(8,128)(2,1)S(1)}, u32[]{:S(2)}, u32[]{:S(2)}) collective-permute-start(bf16[256,128]{1,0:T(8,128)(2,1)S(1)} %block.2), channel_id=1, source_target_pairs={{8,0},{16,8},{24,16},{0,24},{9,1},{17,9},{25,17},{1,25},{10,2},{18... | collective-permute-start | bytes 196616 | tf_op jit(solution)/shard_map/ppermute | solution.py:447
  17.1 0.0 collective-permute-done.3.refs_1_.refs_4_.refs_5_
  17.1 0.0 collective-permute-done.4.refs_2_.refs_3_
  17.1 1.5 %collective-permute-done.5.refs_3_.refs_4_.refs_5_ = bf16[576,128]{1,0:T(8,128)(2,1)S(1)} collective-permute-done((bf16[576,128]{1,0:T(8,128)(2,1)S(1)}, bf16[576,128]{1,0:T(8,128)(2,1)S(1)}, u32[]{:S(2)}, u32[]{:S(2)}) %collective-permute-start.5) | collective-permute-done | bytes 147488 | tf_op jit(solution)/shard_map/ppermute | solution.py:29
  18.6 1.5 %collective-permute-start.9 = (bf16[256,128]{1,0:T(8,128)(2,1)S(1)}, bf16[256,128]{1,0:T(8,128)(2,1)S(1)}, u32[]{:S(2)}, u32[]{:S(2)}) collective-permute-start(bf16[256,128]{1,0:T(8,128)(2,1)S(1)} %collect.1.refs_0_), channel_id=1, source_target_pairs={{1,0},{0,1},{3,2},{2,3},{5,4},{4,5},{7,6},{6,7},{9,8},{8,9},{11,10... | collective-permute-start | bytes 196616 | tf_op jit(solution)/shard_map/ppermute | solution.py:29
  20.1 0.0 collective-permute-done.2.grad_ref.refs_2_
  20.1 2.3 %collective-permute-start.8 = (bf16[256,128]{1,0:T(8,128)(2,1)S(1)}, bf16[256,128]{1,0:T(8,128)(2,1)S(1)}, u32[]{:S(2)}, u32[]{:S(2)}) collective-permute-start(bf16[256,128]{1,0:T(8,128)(2,1)S(1)} %block.3.refs_3_), channel_id=1, source_target_pairs={{9,0},{8,1},{1,8},{0,9},{25,16},{24,17},{17,24},{16,25},{11,2},{10... | collective-permute-start | bytes 196616 | tf_op jit(solution)/shard_map/ppermute | solution.py:486
  22.4 0.0 collective-permute-start.7
  22.4 1.2 %collective-permute-start.6 = (bf16[256,128]{1,0:T(8,128)(2,1)S(1)}, bf16[256,128]{1,0:T(8,128)(2,1)S(1)}, u32[]{:S(2)}, u32[]{:S(2)}) collective-permute-start(bf16[256,128]{1,0:T(8,128)(2,1)S(1)} %early.1.refs_0_), channel_id=1, source_target_pairs={{1,0},{0,1},{3,2},{2,3},{5,4},{4,5},{7,6},{6,7},{9,8},{8,9},{11,10... | collective-permute-start | bytes 196616 | tf_op jit(solution)/shard_map/ppermute | solution.py:29
  23.6 0.0 collective-permute-done.9.refs_1_
  23.6 1.5 %unfold.1.refs_2_.refs_6_ = bf16[2,1728,512]{2,1,0:T(8,128)(2,1)S(1)} custom-call(bf16[256,128]{1,0:T(8,128)(2,1)S(1)} %collect.1.refs_0_, bf16[256,128]{1,0:T(8,128)(2,1)S(1)} %collective-permute-done.9.refs_1_), custom_call_target="tpu_custom_call" | custom-call | tf_op jit(solution)/shard_map/unfold/pallas_call | solution.py:369
  25.1 0.2 collective-permute-done.8.refs_1_
  25.4 1.3 %collective-permute-done.7.refs_0_ = bf16[256,128]{1,0:T(8,128)(2,1)S(1)} collective-permute-done((bf16[256,128]{1,0:T(8,128)(2,1)S(1)}, bf16[256,128]{1,0:T(8,128)(2,1)S(1)}, u32[]{:S(2)}, u32[]{:S(2)}) %collective-permute-start.7) | collective-permute-done | bytes 65568 | tf_op jit(solution)/shard_map/ppermute | solution.py:447
  26.7 0.0 collective-permute-done.6.refs_1_
  26.7 1.6 %collective-permute-start.10 = (bf16[512,128]{1,0:T(8,128)(2,1)S(1)}, bf16[512,128]{1,0:T(8,128)(2,1)S(1)}, u32[]{:S(2)}, u32[]{:S(2)}) collective-permute-start(bf16[512,128]{1,0:T(8,128)(2,1)S(1)} %choose.1.refs_0_.refs_1_), channel_id=1, source_target_pairs={{4,0},{5,1},{6,2},{7,3},{0,4},{1,5},{2,6},{3,7},{12,8},{13,9},{14,... | collective-permute-start | bytes 393224 | tf_op jit(solution)/shard_map/ppermute | solution.py:29
  28.3 2.2 %own_slab.1.refs_0_ = bf16[2,1,64,256]{3,2,1,0:T(8,128)(2,1)} custom-call(bf16[512,128]{1,0:T(8,128)(2,1)S(1)} %choose.1.refs_0_.refs_1_, bf16[512,128]{1,0:T(8,128)(2,1)S(1)} %choose.1.refs_0_.refs_1_, bf16[512,128]{1,0:T(8,128)(2,1)S(1)} %get-tuple-element.25.pre_ref.refs_2_, bf16[27,256,256]{2,1,0:T(8,128)(2,1)S(1)} %get-tuple-element.21.refs_3_.conv_ref, ...), custom_call_target="tpu_custom_call" | custom-call | tf_op jit(solution)/shard_map/own_slab/pallas_call | solution.py:369
  30.4 0.0 collective-permute-start.12
  30.5 1.3 %collective-permute-done.10.block_ref = bf16[512,128]{1,0:T(8,128)(2,1)S(1)} collective-permute-done((bf16[512,128]{1,0:T(8,128)(2,1)S(1)}, bf16[512,128]{1,0:T(8,128)(2,1)S(1)}, u32[]{:S(2)}, u32[]{:S(2)}) %collective-permute-start.10) | collective-permute-done | bytes 131104 | tf_op jit(solution)/shard_map/ppermute | solution.py:29
  31.8 0.1 collective-permute-start.11
  31.8 0.0 collective-permute-done.12.refs_1_
  31.8 1.0 %part_weight_grads.1 = (f32[1728,256]{1,0:T(8,128)S(1)}, f32[64,256]{1,0:T(8,128)S(1)}) custom-call(bf16[512,128]{1,0:T(8,128)(2,1)S(1)} %choose.1.refs_0_.refs_1_, bf16[512,128]{1,0:T(8,128)(2,1)S(1)} %collective-permute-done.12.refs_1_, bf16[576,128]{1,0:T(8,128)(2,1)S(1)} %get-tuple-element.27.refs_0_.refs_2_.refs_3_, ...), custom_call_target="tpu_custom_call" | custom-call | tf_op jit(solution)/shard_map/part_weight_grads/pallas_call | solution.py:369
  32.8 0.3 collective-permute-done.11.refs_1_
  33.2 2.6 %weight_grads.1 = (f32[1728,256]{1,0:T(8,128)}, f32[64,256]{1,0:T(8,128)}) custom-call(bf16[512,128]{1,0:T(8,128)(2,1)S(1)} %hand_on.1.refs_0_, bf16[512,128]{1,0:T(8,128)(2,1)S(1)} %collective-permute-done.11.refs_1_, bf16[576,128]{1,0:T(8,128)(2,1)S(1)} %collective-permute-done.4.refs_2_.refs_3_, ...), custom_call_target="tpu_custom_call" | custom-call | tf_op jit(solution)/shard_map/weight_grads/pallas_call | solution.py:369
  (7 shorter events, 0.0 us)
Async XLA Ops:
  1.5 5.8 %collective-permute-start = (bf16[3,1,64,256]{3,2,1,0:T(8,128)(2,1)S(1)}, bf16[3,1,64,256]{3,2,1,0:T(8,128)(2,1)S(1)}, u32[]{:S(2)}, u32[]{:S(2)}) collective-permute-start(bf16[3,1,64,256]{3,2,1,0:T(8,128)(2,1)S(1)} %outgoing.1), channel_id=1, source_target_pairs={{1,0},{0,1},{3,2},{2,3},{5,4},{4,5},{7,6},{6,7},{9,8},{8,9},{11,10... | collective-permute-start | bytes 294920 | tf_op jit(solution)/shard_map/ppermute | solution.py:29
  7.5 4.3 %collective-permute-start.1 = (bf16[256,128]{1,0:T(8,128)(2,1)S(1)}, bf16[256,128]{1,0:T(8,128)(2,1)S(1)}, u32[]{:S(2)}, u32[]{:S(2)}) collective-permute-start(bf16[256,128]{1,0:T(8,128)(2,1)S(1)} %get-tuple-element.24), channel_id=1, source_target_pairs={{8,0},{0,8},{24,16},{16,24},{9,1},{1,9},{25,17},{17,25},{10,2},{2,... | collective-permute-start | bytes 196616 | tf_op jit(solution)/shard_map/ppermute | solution.py:447
  9.5 7.6 %collective-permute-start.3 = (bf16[576,128]{1,0:T(8,128)(2,1)S(1)}, bf16[576,128]{1,0:T(8,128)(2,1)S(1)}, u32[]{:S(2)}, u32[]{:S(2)}) collective-permute-start(bf16[576,128]{1,0:T(8,128)(2,1)S(1)} %get-tuple-element.28), channel_id=1, source_target_pairs={{2,0},{3,1},{0,2},{1,3},{6,4},{7,5},{4,6},{5,7},{10,8},{11,9},{8,1... | collective-permute-start | bytes 442376 | tf_op jit(solution)/shard_map/ppermute | solution.py:29
  9.6 7.5 %collective-permute-start.4 = (bf16[576,128]{1,0:T(8,128)(2,1)S(1)}, bf16[576,128]{1,0:T(8,128)(2,1)S(1)}, u32[]{:S(2)}, u32[]{:S(2)}) collective-permute-start(bf16[576,128]{1,0:T(8,128)(2,1)S(1)} %get-tuple-element.29), channel_id=1, source_target_pairs={{4,0},{5,1},{6,2},{7,3},{0,4},{1,5},{2,6},{3,7},{12,8},{13,9},{14,... | collective-permute-start | bytes 442376 | tf_op jit(solution)/shard_map/ppermute | solution.py:29
  11.2 7.4 %collective-permute-start.5 = (bf16[576,128]{1,0:T(8,128)(2,1)S(1)}, bf16[576,128]{1,0:T(8,128)(2,1)S(1)}, u32[]{:S(2)}, u32[]{:S(2)}) collective-permute-start(bf16[576,128]{1,0:T(8,128)(2,1)S(1)} %get-tuple-element.30), channel_id=1, source_target_pairs={{6,0},{7,1},{4,2},{5,3},{2,4},{3,5},{0,6},{1,7},{14,8},{15,9},{12,... | collective-permute-start | bytes 442376 | tf_op jit(solution)/shard_map/ppermute | solution.py:29
  11.8 8.3 %collective-permute-start.2 = (bf16[256,128]{1,0:T(8,128)(2,1)S(1)}, bf16[256,128]{1,0:T(8,128)(2,1)S(1)}, u32[]{:S(2)}, u32[]{:S(2)}) collective-permute-start(bf16[256,128]{1,0:T(8,128)(2,1)S(1)} %block.2), channel_id=1, source_target_pairs={{8,0},{16,8},{24,16},{0,24},{9,1},{17,9},{25,17},{1,25},{10,2},{18... | collective-permute-start | bytes 196616 | tf_op jit(solution)/shard_map/ppermute | solution.py:447
  18.6 5.0 %collective-permute-start.9 = (bf16[256,128]{1,0:T(8,128)(2,1)S(1)}, bf16[256,128]{1,0:T(8,128)(2,1)S(1)}, u32[]{:S(2)}, u32[]{:S(2)}) collective-permute-start(bf16[256,128]{1,0:T(8,128)(2,1)S(1)} %collect.1.refs_0_), channel_id=1, source_target_pairs={{1,0},{0,1},{3,2},{2,3},{5,4},{4,5},{7,6},{6,7},{9,8},{8,9},{11,10... | collective-permute-start | bytes 196616 | tf_op jit(solution)/shard_map/ppermute | solution.py:29
  20.1 5.2 %collective-permute-start.8 = (bf16[256,128]{1,0:T(8,128)(2,1)S(1)}, bf16[256,128]{1,0:T(8,128)(2,1)S(1)}, u32[]{:S(2)}, u32[]{:S(2)}) collective-permute-start(bf16[256,128]{1,0:T(8,128)(2,1)S(1)} %block.3.refs_3_), channel_id=1, source_target_pairs={{9,0},{8,1},{1,8},{0,9},{25,16},{24,17},{17,24},{16,25},{11,2},{10... | collective-permute-start | bytes 196616 | tf_op jit(solution)/shard_map/ppermute | solution.py:486
  22.4 4.3 %collective-permute-start.7 = (bf16[256,128]{1,0:T(8,128)(2,1)S(1)}, bf16[256,128]{1,0:T(8,128)(2,1)S(1)}, u32[]{:S(2)}, u32[]{:S(2)}) collective-permute-start(bf16[256,128]{1,0:T(8,128)(2,1)S(1)} %block.3.refs_3_), channel_id=1, source_target_pairs={{8,0},{0,8},{24,16},{16,24},{9,1},{1,9},{25,17},{17,25},{10,2},{2,... | collective-permute-start | bytes 196616 | tf_op jit(solution)/shard_map/ppermute | solution.py:447
  22.4 4.3 %collective-permute-start.6 = (bf16[256,128]{1,0:T(8,128)(2,1)S(1)}, bf16[256,128]{1,0:T(8,128)(2,1)S(1)}, u32[]{:S(2)}, u32[]{:S(2)}) collective-permute-start(bf16[256,128]{1,0:T(8,128)(2,1)S(1)} %early.1.refs_0_), channel_id=1, source_target_pairs={{1,0},{0,1},{3,2},{2,3},{5,4},{4,5},{7,6},{6,7},{9,8},{8,9},{11,10... | collective-permute-start | bytes 196616 | tf_op jit(solution)/shard_map/ppermute | solution.py:29
  26.7 5.0 %collective-permute-start.10 = (bf16[512,128]{1,0:T(8,128)(2,1)S(1)}, bf16[512,128]{1,0:T(8,128)(2,1)S(1)}, u32[]{:S(2)}, u32[]{:S(2)}) collective-permute-start(bf16[512,128]{1,0:T(8,128)(2,1)S(1)} %choose.1.refs_0_.refs_1_), channel_id=1, source_target_pairs={{4,0},{5,1},{6,2},{7,3},{0,4},{1,5},{2,6},{3,7},{12,8},{13,9},{14,... | collective-permute-start | bytes 393224 | tf_op jit(solution)/shard_map/ppermute | solution.py:29
  30.4 1.4 %collective-permute-start.12 = (bf16[512,128]{1,0:T(8,128)(2,1)S(1)}, bf16[512,128]{1,0:T(8,128)(2,1)S(1)}, u32[]{:S(2)}, u32[]{:S(2)}) collective-permute-start(bf16[512,128]{1,0:T(8,128)(2,1)S(1)} %choose.1.refs_0_.refs_1_), channel_id=1, source_target_pairs={{2,0},{3,1},{0,2},{1,3},{6,4},{7,5},{4,6},{5,7},{10,8},{11,9},{8,1... | collective-permute-start | bytes 393224 | tf_op jit(solution)/shard_map/ppermute | solution.py:29
  31.8 1.4 %collective-permute-start.11 = (bf16[512,128]{1,0:T(8,128)(2,1)S(1)}, bf16[512,128]{1,0:T(8,128)(2,1)S(1)}, u32[]{:S(2)}, u32[]{:S(2)}) collective-permute-start(bf16[512,128]{1,0:T(8,128)(2,1)S(1)} %hand_on.1.refs_0_), channel_id=1, source_target_pairs={{2,0},{3,1},{0,2},{1,3},{6,4},{7,5},{4,6},{5,7},{10,8},{11,9},{8,1... | collective-permute-start | bytes 393224 | tf_op jit(solution)/shard_map/ppermute | solution.py:29

commit v4 on v3

--- a/solution.py
+++ b/solution.py
@@ -289,10 +289,15 @@
             continue
         rows_ref, sems = refs[3:]
         rows_ref[span] = total * scale
-        copies.append(
-            pltpu.make_async_copy(rows_ref.at[span], conv_out_ref.at[span], sems.at[cut])
-        )
-        copies[-1].start()
+        parts = 1 if size % 32 else 2
+        for half in range(parts):
+            piece = pl.ds(cut * size + half * (size // parts), size // parts)
+            copies.append(
+                pltpu.make_async_copy(
+                    rows_ref.at[piece], conv_out_ref.at[piece], sems.at[2 * cut + half]
+                )
+            )
+            copies[-1].start(priority=half)
     for copy in copies:
         copy.wait()
 
@@ -530,7 +535,7 @@
         scratch = [pltpu.VMEM((channels, len(columns) * lanes), bfloat)]
         out_specs = whole(2)
         if final:
-            scratch += [pltpu.VMEM(conv_shape.shape, jnp.float32), pltpu.SemaphoreType.DMA((cuts,))]
+            scratch += [pltpu.VMEM(conv_shape.shape, jnp.float32), pltpu.SemaphoreType.DMA((2 * cuts,))]
             out_specs = [hbm] + whole()
         return kernel_call(
             functools.partial(

time: 35.9 us -> 35.9 us (level)
  no operation moved by 1% of the time
where the time goes in v4:
time: 35.9 us; the launch traced here: 35.8 us
  starting transfers between devices  18.8 us (52%)
  Pallas kernels  10.6 us (30%)
  waiting for transfers between devices  5.67 us (16%)
  between operations  0.72 us (2%)
    pallas_call x15, Pallas kernels, kernel_call(): pl.pallas_call(body, out_shape=outs if single else tuple(outs), in_specs=...  10.6 us
    ppermute x9, starting transfers between devices, moved(): return lax.ppermute(block, ('dp', 'space'), pairs)  9.32 us
    ppermute x3, starting transfers between devices, shards(): lax.ppermute(results[-1], 'section', hop_pairs(section_count, step))  7.21 us
    ppermute x9, waiting for transfers between devices, moved(): return lax.ppermute(block, ('dp', 'space'), pairs)  3.79 us
    ppermute x1, starting transfers between devices, shards(): lax.ppermute(results[-1], ('section', 'space'), [(source * slabs + peer(i...  2.28 us
    ppermute x3, waiting for transfers between devices, shards(): lax.ppermute(results[-1], 'section', hop_pairs(section_count, step))  1.67 us
  transfers between devices with their start and end apart: 13, of which 7 were waited for; matrix products, arithmetic and copies ran while one was open for 0% of the time, Pallas kernels for 19%

profile of v4, /device:TPU:0, one launch (start us, length us, event | category | flops | bytes accessed | tf_op | source)
XLA Modules:
  0.0 35.8 jit_solution(5122267117460524314)
XLA Ops:
  0.6 0.9 %outgoing.1 = bf16[3,1,64,256]{3,2,1,0:T(8,128)(2,1)S(1)} custom-call(bf16[2,1,64,256]{3,2,1,0:T(8,128)(2,1)} %bitcast.15, bf16[2,1,64,256]{3,2,1,0:T(8,128)(2,1)} %bitcast.17), custom_call_target="tpu_custom_call" | custom-call | tf_op jit(solution)/shard_map/outgoing/pallas_call | solution.py:374
  1.5 3.0 %collective-permute-start = (bf16[3,1,64,256]{3,2,1,0:T(8,128)(2,1)S(1)}, bf16[3,1,64,256]{3,2,1,0:T(8,128)(2,1)S(1)}, u32[]{:S(2)}, u32[]{:S(2)}) collective-permute-start(bf16[3,1,64,256]{3,2,1,0:T(8,128)(2,1)S(1)} %outgoing.1), channel_id=1, source_target_pairs={{1,0},{0,1},{3,2},{2,3},{5,4},{4,5},{7,6},{6,7},{9,8},{8,9},{11,10... | collective-permute-start | bytes 294920 | tf_op jit(solution)/shard_map/ppermute | solution.py:29
  4.6 2.1 %prepare.1 = (bf16[1,1,64,256]{3,2,1,0:T(8,128)(2,1)S(1)}, bf16[2,1,64,256]{3,2,1,0:T(8,128)(2,1)S(1)}, bf16[256,128]{1,0:T(8,128)(2,1)S(1)}, bf16[27,256,256]{2,1,0:T(8,128)(2,1)S(1)}, bf16[256,256]{1,0:T(8,128)(2,1)S(1)}) custom-call(bf16[2,1,64,256]{3,2,1,0:T(8,128)(2,1)} %bitcast.16, bf16[2,1,64,256]{3,2,1,0:T(8,128)(2,1)} %bitcast.18, ...), custom_call_target="tpu_custom_call" | custom-call | tf_op jit(solution)/shard_map/prepare/pallas_call | solution.py:374
  6.7 0.6 %collective-permute-done.refs_2_ = bf16[3,1,64,256]{3,2,1,0:T(8,128)(2,1)S(1)} collective-permute-done((bf16[3,1,64,256]{3,2,1,0:T(8,128)(2,1)S(1)}, bf16[3,1,64,256]{3,2,1,0:T(8,128)(2,1)S(1)}, u32[]{:S(2)}, u32[]{:S(2)}) %collective-permute-start) | collective-permute-done | bytes 98336 | tf_op jit(solution)/shard_map/ppermute | solution.py:29
  7.3 0.2 first_block.1
  7.5 1.9 %collective-permute-start.1 = (bf16[256,128]{1,0:T(8,128)(2,1)S(1)}, bf16[256,128]{1,0:T(8,128)(2,1)S(1)}, u32[]{:S(2)}, u32[]{:S(2)}) collective-permute-start(bf16[256,128]{1,0:T(8,128)(2,1)S(1)} %get-tuple-element.24), channel_id=1, source_target_pairs={{8,0},{0,8},{24,16},{16,24},{9,1},{1,9},{25,17},{17,25},{10,2},{2,... | collective-permute-start | bytes 196616 | tf_op jit(solution)/shard_map/ppermute | solution.py:452
  9.5 0.1 pack.1
  9.5 0.1 collective-permute-start.3
  9.6 1.6 %collective-permute-start.4 = (bf16[576,128]{1,0:T(8,128)(2,1)S(1)}, bf16[576,128]{1,0:T(8,128)(2,1)S(1)}, u32[]{:S(2)}, u32[]{:S(2)}) collective-permute-start(bf16[576,128]{1,0:T(8,128)(2,1)S(1)} %get-tuple-element.29), channel_id=1, source_target_pairs={{4,0},{5,1},{6,2},{7,3},{0,4},{1,5},{2,6},{3,7},{12,8},{13,9},{14,... | collective-permute-start | bytes 442376 | tf_op jit(solution)/shard_map/ppermute | solution.py:29
  11.2 0.3 collective-permute-start.5
  11.5 0.4 %collective-permute-done.1.grad_ref.refs_1_ = bf16[256,128]{1,0:T(8,128)(2,1)S(1)} collective-permute-done((bf16[256,128]{1,0:T(8,128)(2,1)S(1)}, bf16[256,128]{1,0:T(8,128)(2,1)S(1)}, u32[]{:S(2)}, u32[]{:S(2)}) %collective-permute-start.1) | collective-permute-done | bytes 65568 | tf_op jit(solution)/shard_map/ppermute | solution.py:452
  11.8 5.3 %collective-permute-start.2 = (bf16[256,128]{1,0:T(8,128)(2,1)S(1)}, bf16[256,128]{1,0:T(8,128)(2,1)S(1)}, u32[]{:S(2)}, u32[]{:S(2)}) collective-permute-start(bf16[256,128]{1,0:T(8,128)(2,1)S(1)} %block.2), channel_id=1, source_target_pairs={{8,0},{16,8},{24,16},{0,24},{9,1},{17,9},{25,17},{1,25},{10,2},{18... | collective-permute-start | bytes 196616 | tf_op jit(solution)/shard_map/ppermute | solution.py:452
  17.1 0.0 collective-permute-done.3.refs_1_.refs_4_.refs_5_
  17.1 0.0 collective-permute-done.4.refs_2_.refs_3_
  17.1 1.5 %collective-permute-done.5.refs_3_.refs_4_.refs_5_ = bf16[576,128]{1,0:T(8,128)(2,1)S(1)} collective-permute-done((bf16[576,128]{1,0:T(8,128)(2,1)S(1)}, bf16[576,128]{1,0:T(8,128)(2,1)S(1)}, u32[]{:S(2)}, u32[]{:S(2)}) %collective-permute-start.5) | collective-permute-done | bytes 147488 | tf_op jit(solution)/shard_map/ppermute | solution.py:29
  18.6 1.5 %collective-permute-start.9 = (bf16[256,128]{1,0:T(8,128)(2,1)S(1)}, bf16[256,128]{1,0:T(8,128)(2,1)S(1)}, u32[]{:S(2)}, u32[]{:S(2)}) collective-permute-start(bf16[256,128]{1,0:T(8,128)(2,1)S(1)} %collect.1.refs_0_), channel_id=1, source_target_pairs={{1,0},{0,1},{3,2},{2,3},{5,4},{4,5},{7,6},{6,7},{9,8},{8,9},{11,10... | collective-permute-start | bytes 196616 | tf_op jit(solution)/shard_map/ppermute | solution.py:29
  20.1 0.0 collective-permute-done.2.grad_ref.refs_2_
  20.1 2.3 %collective-permute-start.8 = (bf16[256,128]{1,0:T(8,128)(2,1)S(1)}, bf16[256,128]{1,0:T(8,128)(2,1)S(1)}, u32[]{:S(2)}, u32[]{:S(2)}) collective-permute-start(bf16[256,128]{1,0:T(8,128)(2,1)S(1)} %block.3.refs_3_), channel_id=1, source_target_pairs={{9,0},{8,1},{1,8},{0,9},{25,16},{24,17},{17,24},{16,25},{11,2},{10... | collective-permute-start | bytes 196616 | tf_op jit(solution)/shard_map/ppermute | solution.py:491
  22.4 0.0 collective-permute-start.7
  22.4 1.2 %collective-permute-start.6 = (bf16[256,128]{1,0:T(8,128)(2,1)S(1)}, bf16[256,128]{1,0:T(8,128)(2,1)S(1)}, u32[]{:S(2)}, u32[]{:S(2)}) collective-permute-start(bf16[256,128]{1,0:T(8,128)(2,1)S(1)} %early.1.refs_0_), channel_id=1, source_target_pairs={{1,0},{0,1},{3,2},{2,3},{5,4},{4,5},{7,6},{6,7},{9,8},{8,9},{11,10... | collective-permute-start | bytes 196616 | tf_op jit(solution)/shard_map/ppermute | solution.py:29
  23.6 0.0 collective-permute-done.9.refs_1_
  23.6 1.5 %unfold.1.refs_2_.refs_6_ = bf16[2,1728,512]{2,1,0:T(8,128)(2,1)S(1)} custom-call(bf16[256,128]{1,0:T(8,128)(2,1)S(1)} %collect.1.refs_0_, bf16[256,128]{1,0:T(8,128)(2,1)S(1)} %collective-permute-done.9.refs_1_), custom_call_target="tpu_custom_call" | custom-call | tf_op jit(solution)/shard_map/unfold/pallas_call | solution.py:374
  25.1 0.2 collective-permute-done.8.refs_1_
  25.4 1.3 %collective-permute-done.7.refs_0_ = bf16[256,128]{1,0:T(8,128)(2,1)S(1)} collective-permute-done((bf16[256,128]{1,0:T(8,128)(2,1)S(1)}, bf16[256,128]{1,0:T(8,128)(2,1)S(1)}, u32[]{:S(2)}, u32[]{:S(2)}) %collective-permute-start.7) | collective-permute-done | bytes 65568 | tf_op jit(solution)/shard_map/ppermute | solution.py:452
  26.7 0.0 collective-permute-done.6.refs_1_
  26.7 1.6 %collective-permute-start.10 = (bf16[512,128]{1,0:T(8,128)(2,1)S(1)}, bf16[512,128]{1,0:T(8,128)(2,1)S(1)}, u32[]{:S(2)}, u32[]{:S(2)}) collective-permute-start(bf16[512,128]{1,0:T(8,128)(2,1)S(1)} %choose.1.refs_0_.refs_1_), channel_id=1, source_target_pairs={{4,0},{5,1},{6,2},{7,3},{0,4},{1,5},{2,6},{3,7},{12,8},{13,9},{14,... | collective-permute-start | bytes 393224 | tf_op jit(solution)/shard_map/ppermute | solution.py:29
  28.3 2.2 %own_slab.1.refs_0_ = bf16[2,1,64,256]{3,2,1,0:T(8,128)(2,1)} custom-call(bf16[512,128]{1,0:T(8,128)(2,1)S(1)} %choose.1.refs_0_.refs_1_, bf16[512,128]{1,0:T(8,128)(2,1)S(1)} %choose.1.refs_0_.refs_1_, bf16[512,128]{1,0:T(8,128)(2,1)S(1)} %get-tuple-element.25.pre_ref.refs_2_, bf16[27,256,256]{2,1,0:T(8,128)(2,1)S(1)} %get-tuple-element.21.refs_3_.conv_ref, ...), custom_call_target="tpu_custom_call" | custom-call | tf_op jit(solution)/shard_map/own_slab/pallas_call | solution.py:374
  30.4 0.0 collective-permute-start.12
  30.5 1.3 %collective-permute-done.10.block_ref = bf16[512,128]{1,0:T(8,128)(2,1)S(1)} collective-permute-done((bf16[512,128]{1,0:T(8,128)(2,1)S(1)}, bf16[512,128]{1,0:T(8,128)(2,1)S(1)}, u32[]{:S(2)}, u32[]{:S(2)}) %collective-permute-start.10) | collective-permute-done | bytes 131104 | tf_op jit(solution)/shard_map/ppermute | solution.py:29
  31.8 0.1 collective-permute-start.11
  31.8 0.0 collective-permute-done.12.refs_1_
  31.8 1.0 %part_weight_grads.1 = (f32[1728,256]{1,0:T(8,128)S(1)}, f32[64,256]{1,0:T(8,128)S(1)}) custom-call(bf16[512,128]{1,0:T(8,128)(2,1)S(1)} %choose.1.refs_0_.refs_1_, bf16[512,128]{1,0:T(8,128)(2,1)S(1)} %collective-permute-done.12.refs_1_, bf16[576,128]{1,0:T(8,128)(2,1)S(1)} %get-tuple-element.27.refs_0_.refs_2_.refs_3_, ...), custom_call_target="tpu_custom_call" | custom-call | tf_op jit(solution)/shard_map/part_weight_grads/pallas_call | solution.py:374
  32.8 0.3 collective-permute-done.11.refs_1_
  33.2 2.6 %weight_grads.1 = (f32[1728,256]{1,0:T(8,128)}, f32[64,256]{1,0:T(8,128)}) custom-call(bf16[512,128]{1,0:T(8,128)(2,1)S(1)} %hand_on.1.refs_0_, bf16[512,128]{1,0:T(8,128)(2,1)S(1)} %collective-permute-done.11.refs_1_, bf16[576,128]{1,0:T(8,128)(2,1)S(1)} %collective-permute-done.4.refs_2_.refs_3_, ...), custom_call_target="tpu_custom_call" | custom-call | tf_op jit(solution)/shard_map/weight_grads/pallas_call | solution.py:374
  (7 shorter events, 0.0 us)
Async XLA Ops:
  1.5 5.8 %collective-permute-start = (bf16[3,1,64,256]{3,2,1,0:T(8,128)(2,1)S(1)}, bf16[3,1,64,256]{3,2,1,0:T(8,128)(2,1)S(1)}, u32[]{:S(2)}, u32[]{:S(2)}) collective-permute-start(bf16[3,1,64,256]{3,2,1,0:T(8,128)(2,1)S(1)} %outgoing.1), channel_id=1, source_target_pairs={{1,0},{0,1},{3,2},{2,3},{5,4},{4,5},{7,6},{6,7},{9,8},{8,9},{11,10... | collective-permute-start | bytes 294920 | tf_op jit(solution)/shard_map/ppermute | solution.py:29
  7.5 4.3 %collective-permute-start.1 = (bf16[256,128]{1,0:T(8,128)(2,1)S(1)}, bf16[256,128]{1,0:T(8,128)(2,1)S(1)}, u32[]{:S(2)}, u32[]{:S(2)}) collective-permute-start(bf16[256,128]{1,0:T(8,128)(2,1)S(1)} %get-tuple-element.24), channel_id=1, source_target_pairs={{8,0},{0,8},{24,16},{16,24},{9,1},{1,9},{25,17},{17,25},{10,2},{2,... | collective-permute-start | bytes 196616 | tf_op jit(solution)/shard_map/ppermute | solution.py:452
  9.5 7.6 %collective-permute-start.3 = (bf16[576,128]{1,0:T(8,128)(2,1)S(1)}, bf16[576,128]{1,0:T(8,128)(2,1)S(1)}, u32[]{:S(2)}, u32[]{:S(2)}) collective-permute-start(bf16[576,128]{1,0:T(8,128)(2,1)S(1)} %get-tuple-element.28), channel_id=1, source_target_pairs={{2,0},{3,1},{0,2},{1,3},{6,4},{7,5},{4,6},{5,7},{10,8},{11,9},{8,1... | collective-permute-start | bytes 442376 | tf_op jit(solution)/shard_map/ppermute | solution.py:29
  9.6 7.5 %collective-permute-start.4 = (bf16[576,128]{1,0:T(8,128)(2,1)S(1)}, bf16[576,128]{1,0:T(8,128)(2,1)S(1)}, u32[]{:S(2)}, u32[]{:S(2)}) collective-permute-start(bf16[576,128]{1,0:T(8,128)(2,1)S(1)} %get-tuple-element.29), channel_id=1, source_target_pairs={{4,0},{5,1},{6,2},{7,3},{0,4},{1,5},{2,6},{3,7},{12,8},{13,9},{14,... | collective-permute-start | bytes 442376 | tf_op jit(solution)/shard_map/ppermute | solution.py:29
  11.2 7.4 %collective-permute-start.5 = (bf16[576,128]{1,0:T(8,128)(2,1)S(1)}, bf16[576,128]{1,0:T(8,128)(2,1)S(1)}, u32[]{:S(2)}, u32[]{:S(2)}) collective-permute-start(bf16[576,128]{1,0:T(8,128)(2,1)S(1)} %get-tuple-element.30), channel_id=1, source_target_pairs={{6,0},{7,1},{4,2},{5,3},{2,4},{3,5},{0,6},{1,7},{14,8},{15,9},{12,... | collective-permute-start | bytes 442376 | tf_op jit(solution)/shard_map/ppermute | solution.py:29
  11.8 8.3 %collective-permute-start.2 = (bf16[256,128]{1,0:T(8,128)(2,1)S(1)}, bf16[256,128]{1,0:T(8,128)(2,1)S(1)}, u32[]{:S(2)}, u32[]{:S(2)}) collective-permute-start(bf16[256,128]{1,0:T(8,128)(2,1)S(1)} %block.2), channel_id=1, source_target_pairs={{8,0},{16,8},{24,16},{0,24},{9,1},{17,9},{25,17},{1,25},{10,2},{18... | collective-permute-start | bytes 196616 | tf_op jit(solution)/shard_map/ppermute | solution.py:452
  18.6 5.0 %collective-permute-start.9 = (bf16[256,128]{1,0:T(8,128)(2,1)S(1)}, bf16[256,128]{1,0:T(8,128)(2,1)S(1)}, u32[]{:S(2)}, u32[]{:S(2)}) collective-permute-start(bf16[256,128]{1,0:T(8,128)(2,1)S(1)} %collect.1.refs_0_), channel_id=1, source_target_pairs={{1,0},{0,1},{3,2},{2,3},{5,4},{4,5},{7,6},{6,7},{9,8},{8,9},{11,10... | collective-permute-start | bytes 196616 | tf_op jit(solution)/shard_map/ppermute | solution.py:29
  20.1 5.2 %collective-permute-start.8 = (bf16[256,128]{1,0:T(8,128)(2,1)S(1)}, bf16[256,128]{1,0:T(8,128)(2,1)S(1)}, u32[]{:S(2)}, u32[]{:S(2)}) collective-permute-start(bf16[256,128]{1,0:T(8,128)(2,1)S(1)} %block.3.refs_3_), channel_id=1, source_target_pairs={{9,0},{8,1},{1,8},{0,9},{25,16},{24,17},{17,24},{16,25},{11,2},{10... | collective-permute-start | bytes 196616 | tf_op jit(solution)/shard_map/ppermute | solution.py:491
  22.4 4.3 %collective-permute-start.7 = (bf16[256,128]{1,0:T(8,128)(2,1)S(1)}, bf16[256,128]{1,0:T(8,128)(2,1)S(1)}, u32[]{:S(2)}, u32[]{:S(2)}) collective-permute-start(bf16[256,128]{1,0:T(8,128)(2,1)S(1)} %block.3.refs_3_), channel_id=1, source_target_pairs={{8,0},{0,8},{24,16},{16,24},{9,1},{1,9},{25,17},{17,25},{10,2},{2,... | collective-permute-start | bytes 196616 | tf_op jit(solution)/shard_map/ppermute | solution.py:452
  22.4 4.3 %collective-permute-start.6 = (bf16[256,128]{1,0:T(8,128)(2,1)S(1)}, bf16[256,128]{1,0:T(8,128)(2,1)S(1)}, u32[]{:S(2)}, u32[]{:S(2)}) collective-permute-start(bf16[256,128]{1,0:T(8,128)(2,1)S(1)} %early.1.refs_0_), channel_id=1, source_target_pairs={{1,0},{0,1},{3,2},{2,3},{5,4},{4,5},{7,6},{6,7},{9,8},{8,9},{11,10... | collective-permute-start | bytes 196616 | tf_op jit(solution)/shard_map/ppermute | solution.py:29
  26.7 5.0 %collective-permute-start.10 = (bf16[512,128]{1,0:T(8,128)(2,1)S(1)}, bf16[512,128]{1,0:T(8,128)(2,1)S(1)}, u32[]{:S(2)}, u32[]{:S(2)}) collective-permute-start(bf16[512,128]{1,0:T(8,128)(2,1)S(1)} %choose.1.refs_0_.refs_1_), channel_id=1, source_target_pairs={{4,0},{5,1},{6,2},{7,3},{0,4},{1,5},{2,6},{3,7},{12,8},{13,9},{14,... | collective-permute-start | bytes 393224 | tf_op jit(solution)/shard_map/ppermute | solution.py:29
  30.4 1.4 %collective-permute-start.12 = (bf16[512,128]{1,0:T(8,128)(2,1)S(1)}, bf16[512,128]{1,0:T(8,128)(2,1)S(1)}, u32[]{:S(2)}, u32[]{:S(2)}) collective-permute-start(bf16[512,128]{1,0:T(8,128)(2,1)S(1)} %choose.1.refs_0_.refs_1_), channel_id=1, source_target_pairs={{2,0},{3,1},{0,2},{1,3},{6,4},{7,5},{4,6},{5,7},{10,8},{11,9},{8,1... | collective-permute-start | bytes 393224 | tf_op jit(solution)/shard_map/ppermute | solution.py:29
  31.8 1.4 %collective-permute-start.11 = (bf16[512,128]{1,0:T(8,128)(2,1)S(1)}, bf16[512,128]{1,0:T(8,128)(2,1)S(1)}, u32[]{:S(2)}, u32[]{:S(2)}) collective-permute-start(bf16[512,128]{1,0:T(8,128)(2,1)S(1)} %hand_on.1.refs_0_), channel_id=1, source_target_pairs={{2,0},{3,1},{0,2},{1,3},{6,4},{7,5},{4,6},{5,7},{10,8},{11,9},{8,1... | collective-permute-start | bytes 393224 | tf_op jit(solution)/shard_map/ppermute | solution.py:29

commit v5 on v3

--- a/solution.py
+++ b/solution.py
@@ -267,7 +267,13 @@
     proj_total = block_terms(blocks, columns, grad_refs, parcel_refs, proj_ref, masked_ref, shard)
     if has_before:
         proj_total = before_refs[1][...] + proj_total
-    proj_out_ref[...] = proj_total * scale
+    if final:
+        rows_ref, proj_rows_ref, sems = refs[3:]
+        proj_rows_ref[...] = proj_total * scale
+        copies.append(pltpu.make_async_copy(proj_rows_ref, proj_out_ref, sems.at[cuts]))
+        copies[-1].start()
+    else:
+        proj_out_ref[...] = proj_total
     lanes = grad_refs[0].shape[1]
     size = conv_out_ref.shape[0] // cuts
     for cut in range(cuts):
@@ -287,7 +293,6 @@
         if not final:
             conv_out_ref[span] = total
             continue
-        rows_ref, sems = refs[3:]
         rows_ref[span] = total * scale
         copies.append(
             pltpu.make_async_copy(rows_ref.at[span], conv_out_ref.at[span], sems.at[cut])
@@ -530,8 +535,12 @@
         scratch = [pltpu.VMEM((channels, len(columns) * lanes), bfloat)]
         out_specs = whole(2)
         if final:
-            scratch += [pltpu.VMEM(conv_shape.shape, jnp.float32), pltpu.SemaphoreType.DMA((cuts,))]
-            out_specs = [hbm] + whole()
+            scratch += [
+                pltpu.VMEM(conv_shape.shape, jnp.float32),
+                pltpu.VMEM(proj_shape.shape, jnp.float32),
+                pltpu.SemaphoreType.DMA((cuts + 1,)),
+            ]
+            out_specs = [hbm] * 2
         return kernel_call(
             functools.partial(
                 weights_kernel, plan, shard, bool(before), final, scale_term, cuts if final else 1

time: 35.9 us -> 35.3 us (0.983)
  Pallas kernels: 10.6 us -> 9.93 us
    pallas_call x15, Pallas kernels: 10.6 us -> 9.93 us  [kernel_call(): pl.pallas_call(body, out_shape=outs if single else tuple(outs), in_specs=...]
  transfers between devices with their start and end apart: 13 -> 13, of which waited for: 7 -> 7; matrix products, arithmetic and copies ran while one was open for 0% -> 0% of each run, Pallas kernels for 19% -> 20%
where the time goes in v5:
time: 35.3 us; the launch traced here: 35.1 us
  starting transfers between devices  18.8 us (53%)
  Pallas kernels  9.93 us (28%)
  waiting for transfers between devices  5.67 us (16%)
  between operations  0.72 us (2%)
    pallas_call x15, Pallas kernels, kernel_call(): pl.pallas_call(body, out_shape=outs if single else tuple(outs), in_specs=...  9.93 us
    ppermute x9, starting transfers between devices, moved(): return lax.ppermute(block, ('dp', 'space'), pairs)  9.32 us
    ppermute x3, starting transfers between devices, shards(): lax.ppermute(results[-1], 'section', hop_pairs(section_count, step))  7.21 us
    ppermute x9, waiting for transfers between devices, moved(): return lax.ppermute(block, ('dp', 'space'), pairs)  3.79 us
    ppermute x1, starting transfers between devices, shards(): lax.ppermute(results[-1], ('section', 'space'), [(source * slabs + peer(i...  2.28 us
    ppermute x3, waiting for transfers between devices, shards(): lax.ppermute(results[-1], 'section', hop_pairs(section_count, step))  1.67 us
  transfers between devices with their start and end apart: 13, of which 7 were waited for; matrix products, arithmetic and copies ran while one was open for 0% of the time, Pallas kernels for 20%

profile of v5, /device:TPU:0, one launch (start us, length us, event | category | flops | bytes accessed | tf_op | source)
XLA Modules:
  0.0 35.1 jit_solution(1657466851112753155)
XLA Ops:
  0.6 0.9 %outgoing.1 = bf16[3,1,64,256]{3,2,1,0:T(8,128)(2,1)S(1)} custom-call(bf16[2,1,64,256]{3,2,1,0:T(8,128)(2,1)} %bitcast.15, bf16[2,1,64,256]{3,2,1,0:T(8,128)(2,1)} %bitcast.17), custom_call_target="tpu_custom_call" | custom-call | tf_op jit(solution)/shard_map/outgoing/pallas_call | solution.py:374
  1.5 3.0 %collective-permute-start = (bf16[3,1,64,256]{3,2,1,0:T(8,128)(2,1)S(1)}, bf16[3,1,64,256]{3,2,1,0:T(8,128)(2,1)S(1)}, u32[]{:S(2)}, u32[]{:S(2)}) collective-permute-start(bf16[3,1,64,256]{3,2,1,0:T(8,128)(2,1)S(1)} %outgoing.1), channel_id=1, source_target_pairs={{1,0},{0,1},{3,2},{2,3},{5,4},{4,5},{7,6},{6,7},{9,8},{8,9},{11,10... | collective-permute-start | bytes 294920 | tf_op jit(solution)/shard_map/ppermute | solution.py:29
  4.6 2.1 %prepare.1 = (bf16[1,1,64,256]{3,2,1,0:T(8,128)(2,1)S(1)}, bf16[2,1,64,256]{3,2,1,0:T(8,128)(2,1)S(1)}, bf16[256,128]{1,0:T(8,128)(2,1)S(1)}, bf16[27,256,256]{2,1,0:T(8,128)(2,1)S(1)}, bf16[256,256]{1,0:T(8,128)(2,1)S(1)}) custom-call(bf16[2,1,64,256]{3,2,1,0:T(8,128)(2,1)} %bitcast.16, bf16[2,1,64,256]{3,2,1,0:T(8,128)(2,1)} %bitcast.18, ...), custom_call_target="tpu_custom_call" | custom-call | tf_op jit(solution)/shard_map/prepare/pallas_call | solution.py:374
  6.7 0.6 %collective-permute-done.refs_2_ = bf16[3,1,64,256]{3,2,1,0:T(8,128)(2,1)S(1)} collective-permute-done((bf16[3,1,64,256]{3,2,1,0:T(8,128)(2,1)S(1)}, bf16[3,1,64,256]{3,2,1,0:T(8,128)(2,1)S(1)}, u32[]{:S(2)}, u32[]{:S(2)}) %collective-permute-start) | collective-permute-done | bytes 98336 | tf_op jit(solution)/shard_map/ppermute | solution.py:29
  7.3 0.2 first_block.1
  7.5 1.9 %collective-permute-start.1 = (bf16[256,128]{1,0:T(8,128)(2,1)S(1)}, bf16[256,128]{1,0:T(8,128)(2,1)S(1)}, u32[]{:S(2)}, u32[]{:S(2)}) collective-permute-start(bf16[256,128]{1,0:T(8,128)(2,1)S(1)} %get-tuple-element.24), channel_id=1, source_target_pairs={{8,0},{0,8},{24,16},{16,24},{9,1},{1,9},{25,17},{17,25},{10,2},{2,... | collective-permute-start | bytes 196616 | tf_op jit(solution)/shard_map/ppermute | solution.py:452
  9.5 0.1 pack.1
  9.5 0.1 collective-permute-start.3
  9.6 1.6 %collective-permute-start.4 = (bf16[576,128]{1,0:T(8,128)(2,1)S(1)}, bf16[576,128]{1,0:T(8,128)(2,1)S(1)}, u32[]{:S(2)}, u32[]{:S(2)}) collective-permute-start(bf16[576,128]{1,0:T(8,128)(2,1)S(1)} %get-tuple-element.29), channel_id=1, source_target_pairs={{4,0},{5,1},{6,2},{7,3},{0,4},{1,5},{2,6},{3,7},{12,8},{13,9},{14,... | collective-permute-start | bytes 442376 | tf_op jit(solution)/shard_map/ppermute | solution.py:29
  11.2 0.3 collective-permute-start.5
  11.5 0.4 %collective-permute-done.1.grad_ref.refs_1_ = bf16[256,128]{1,0:T(8,128)(2,1)S(1)} collective-permute-done((bf16[256,128]{1,0:T(8,128)(2,1)S(1)}, bf16[256,128]{1,0:T(8,128)(2,1)S(1)}, u32[]{:S(2)}, u32[]{:S(2)}) %collective-permute-start.1) | collective-permute-done | bytes 65568 | tf_op jit(solution)/shard_map/ppermute | solution.py:452
  11.8 5.3 %collective-permute-start.2 = (bf16[256,128]{1,0:T(8,128)(2,1)S(1)}, bf16[256,128]{1,0:T(8,128)(2,1)S(1)}, u32[]{:S(2)}, u32[]{:S(2)}) collective-permute-start(bf16[256,128]{1,0:T(8,128)(2,1)S(1)} %block.2), channel_id=1, source_target_pairs={{8,0},{16,8},{24,16},{0,24},{9,1},{17,9},{25,17},{1,25},{10,2},{18... | collective-permute-start | bytes 196616 | tf_op jit(solution)/shard_map/ppermute | solution.py:452
  17.1 0.0 collective-permute-done.3.refs_1_.refs_4_.refs_5_
  17.1 0.0 collective-permute-done.4.refs_2_.refs_3_
  17.1 1.5 %collective-permute-done.5.refs_3_.refs_4_.refs_5_ = bf16[576,128]{1,0:T(8,128)(2,1)S(1)} collective-permute-done((bf16[576,128]{1,0:T(8,128)(2,1)S(1)}, bf16[576,128]{1,0:T(8,128)(2,1)S(1)}, u32[]{:S(2)}, u32[]{:S(2)}) %collective-permute-start.5) | collective-permute-done | bytes 147488 | tf_op jit(solution)/shard_map/ppermute | solution.py:29
  18.6 1.5 %collective-permute-start.9 = (bf16[256,128]{1,0:T(8,128)(2,1)S(1)}, bf16[256,128]{1,0:T(8,128)(2,1)S(1)}, u32[]{:S(2)}, u32[]{:S(2)}) collective-permute-start(bf16[256,128]{1,0:T(8,128)(2,1)S(1)} %collect.1.refs_0_), channel_id=1, source_target_pairs={{1,0},{0,1},{3,2},{2,3},{5,4},{4,5},{7,6},{6,7},{9,8},{8,9},{11,10... | collective-permute-start | bytes 196616 | tf_op jit(solution)/shard_map/ppermute | solution.py:29
  20.1 0.0 collective-permute-done.2.grad_ref.refs_2_
  20.1 2.3 %collective-permute-start.8 = (bf16[256,128]{1,0:T(8,128)(2,1)S(1)}, bf16[256,128]{1,0:T(8,128)(2,1)S(1)}, u32[]{:S(2)}, u32[]{:S(2)}) collective-permute-start(bf16[256,128]{1,0:T(8,128)(2,1)S(1)} %block.3.refs_3_), channel_id=1, source_target_pairs={{9,0},{8,1},{1,8},{0,9},{25,16},{24,17},{17,24},{16,25},{11,2},{10... | collective-permute-start | bytes 196616 | tf_op jit(solution)/shard_map/ppermute | solution.py:491
  22.4 0.0 collective-permute-start.7
  22.4 1.2 %collective-permute-start.6 = (bf16[256,128]{1,0:T(8,128)(2,1)S(1)}, bf16[256,128]{1,0:T(8,128)(2,1)S(1)}, u32[]{:S(2)}, u32[]{:S(2)}) collective-permute-start(bf16[256,128]{1,0:T(8,128)(2,1)S(1)} %early.1.refs_0_), channel_id=1, source_target_pairs={{1,0},{0,1},{3,2},{2,3},{5,4},{4,5},{7,6},{6,7},{9,8},{8,9},{11,10... | collective-permute-start | bytes 196616 | tf_op jit(solution)/shard_map/ppermute | solution.py:29
  23.6 0.0 collective-permute-done.9.refs_1_
  23.6 1.5 %unfold.1.refs_2_.refs_6_ = bf16[2,1728,512]{2,1,0:T(8,128)(2,1)S(1)} custom-call(bf16[256,128]{1,0:T(8,128)(2,1)S(1)} %collect.1.refs_0_, bf16[256,128]{1,0:T(8,128)(2,1)S(1)} %collective-permute-done.9.refs_1_), custom_call_target="tpu_custom_call" | custom-call | tf_op jit(solution)/shard_map/unfold/pallas_call | solution.py:374
  25.1 0.2 collective-permute-done.8.refs_1_
  25.4 1.3 %collective-permute-done.7.refs_0_ = bf16[256,128]{1,0:T(8,128)(2,1)S(1)} collective-permute-done((bf16[256,128]{1,0:T(8,128)(2,1)S(1)}, bf16[256,128]{1,0:T(8,128)(2,1)S(1)}, u32[]{:S(2)}, u32[]{:S(2)}) %collective-permute-start.7) | collective-permute-done | bytes 65568 | tf_op jit(solution)/shard_map/ppermute | solution.py:452
  26.7 0.0 collective-permute-done.6.refs_1_
  26.7 1.6 %collective-permute-start.10 = (bf16[512,128]{1,0:T(8,128)(2,1)S(1)}, bf16[512,128]{1,0:T(8,128)(2,1)S(1)}, u32[]{:S(2)}, u32[]{:S(2)}) collective-permute-start(bf16[512,128]{1,0:T(8,128)(2,1)S(1)} %choose.1.refs_0_.refs_1_), channel_id=1, source_target_pairs={{4,0},{5,1},{6,2},{7,3},{0,4},{1,5},{2,6},{3,7},{12,8},{13,9},{14,... | collective-permute-start | bytes 393224 | tf_op jit(solution)/shard_map/ppermute | solution.py:29
  28.3 2.2 %own_slab.1.refs_0_ = bf16[2,1,64,256]{3,2,1,0:T(8,128)(2,1)} custom-call(bf16[512,128]{1,0:T(8,128)(2,1)S(1)} %choose.1.refs_0_.refs_1_, bf16[512,128]{1,0:T(8,128)(2,1)S(1)} %choose.1.refs_0_.refs_1_, bf16[512,128]{1,0:T(8,128)(2,1)S(1)} %get-tuple-element.25.pre_ref.refs_2_, bf16[27,256,256]{2,1,0:T(8,128)(2,1)S(1)} %get-tuple-element.21.refs_3_.conv_ref, ...), custom_call_target="tpu_custom_call" | custom-call | tf_op jit(solution)/shard_map/own_slab/pallas_call | solution.py:374
  30.4 0.0 collective-permute-start.12
  30.5 1.3 %collective-permute-done.10.block_ref = bf16[512,128]{1,0:T(8,128)(2,1)S(1)} collective-permute-done((bf16[512,128]{1,0:T(8,128)(2,1)S(1)}, bf16[512,128]{1,0:T(8,128)(2,1)S(1)}, u32[]{:S(2)}, u32[]{:S(2)}) %collective-permute-start.10) | collective-permute-done | bytes 131104 | tf_op jit(solution)/shard_map/ppermute | solution.py:29
  31.8 0.1 collective-permute-start.11
  31.8 0.0 collective-permute-done.12.refs_1_
  31.8 1.0 %part_weight_grads.1 = (f32[1728,256]{1,0:T(8,128)S(1)}, f32[64,256]{1,0:T(8,128)S(1)}) custom-call(bf16[512,128]{1,0:T(8,128)(2,1)S(1)} %choose.1.refs_0_.refs_1_, bf16[512,128]{1,0:T(8,128)(2,1)S(1)} %collective-permute-done.12.refs_1_, bf16[576,128]{1,0:T(8,128)(2,1)S(1)} %get-tuple-element.27.refs_0_.refs_2_.refs_3_, ...), custom_call_target="tpu_custom_call" | custom-call | tf_op jit(solution)/shard_map/part_weight_grads/pallas_call | solution.py:374
  32.8 0.3 collective-permute-done.11.refs_1_
  33.2 2.0 %weight_grads.1 = (f32[1728,256]{1,0:T(8,128)}, f32[64,256]{1,0:T(8,128)}) custom-call(bf16[512,128]{1,0:T(8,128)(2,1)S(1)} %hand_on.1.refs_0_, bf16[512,128]{1,0:T(8,128)(2,1)S(1)} %collective-permute-done.11.refs_1_, bf16[576,128]{1,0:T(8,128)(2,1)S(1)} %collective-permute-done.4.refs_2_.refs_3_, ...), custom_call_target="tpu_custom_call" | custom-call | tf_op jit(solution)/shard_map/weight_grads/pallas_call | solution.py:374
  (7 shorter events, 0.0 us)
Async XLA Ops:
  1.5 5.8 %collective-permute-start = (bf16[3,1,64,256]{3,2,1,0:T(8,128)(2,1)S(1)}, bf16[3,1,64,256]{3,2,1,0:T(8,128)(2,1)S(1)}, u32[]{:S(2)}, u32[]{:S(2)}) collective-permute-start(bf16[3,1,64,256]{3,2,1,0:T(8,128)(2,1)S(1)} %outgoing.1), channel_id=1, source_target_pairs={{1,0},{0,1},{3,2},{2,3},{5,4},{4,5},{7,6},{6,7},{9,8},{8,9},{11,10... | collective-permute-start | bytes 294920 | tf_op jit(solution)/shard_map/ppermute | solution.py:29
  7.5 4.3 %collective-permute-start.1 = (bf16[256,128]{1,0:T(8,128)(2,1)S(1)}, bf16[256,128]{1,0:T(8,128)(2,1)S(1)}, u32[]{:S(2)}, u32[]{:S(2)}) collective-permute-start(bf16[256,128]{1,0:T(8,128)(2,1)S(1)} %get-tuple-element.24), channel_id=1, source_target_pairs={{8,0},{0,8},{24,16},{16,24},{9,1},{1,9},{25,17},{17,25},{10,2},{2,... | collective-permute-start | bytes 196616 | tf_op jit(solution)/shard_map/ppermute | solution.py:452
  9.5 7.6 %collective-permute-start.3 = (bf16[576,128]{1,0:T(8,128)(2,1)S(1)}, bf16[576,128]{1,0:T(8,128)(2,1)S(1)}, u32[]{:S(2)}, u32[]{:S(2)}) collective-permute-start(bf16[576,128]{1,0:T(8,128)(2,1)S(1)} %get-tuple-element.28), channel_id=1, source_target_pairs={{2,0},{3,1},{0,2},{1,3},{6,4},{7,5},{4,6},{5,7},{10,8},{11,9},{8,1... | collective-permute-start | bytes 442376 | tf_op jit(solution)/shard_map/ppermute | solution.py:29
  9.6 7.5 %collective-permute-start.4 = (bf16[576,128]{1,0:T(8,128)(2,1)S(1)}, bf16[576,128]{1,0:T(8,128)(2,1)S(1)}, u32[]{:S(2)}, u32[]{:S(2)}) collective-permute-start(bf16[576,128]{1,0:T(8,128)(2,1)S(1)} %get-tuple-element.29), channel_id=1, source_target_pairs={{4,0},{5,1},{6,2},{7,3},{0,4},{1,5},{2,6},{3,7},{12,8},{13,9},{14,... | collective-permute-start | bytes 442376 | tf_op jit(solution)/shard_map/ppermute | solution.py:29
  11.2 7.4 %collective-permute-start.5 = (bf16[576,128]{1,0:T(8,128)(2,1)S(1)}, bf16[576,128]{1,0:T(8,128)(2,1)S(1)}, u32[]{:S(2)}, u32[]{:S(2)}) collective-permute-start(bf16[576,128]{1,0:T(8,128)(2,1)S(1)} %get-tuple-element.30), channel_id=1, source_target_pairs={{6,0},{7,1},{4,2},{5,3},{2,4},{3,5},{0,6},{1,7},{14,8},{15,9},{12,... | collective-permute-start | bytes 442376 | tf_op jit(solution)/shard_map/ppermute | solution.py:29
  11.8 8.3 %collective-permute-start.2 = (bf16[256,128]{1,0:T(8,128)(2,1)S(1)}, bf16[256,128]{1,0:T(8,128)(2,1)S(1)}, u32[]{:S(2)}, u32[]{:S(2)}) collective-permute-start(bf16[256,128]{1,0:T(8,128)(2,1)S(1)} %block.2), channel_id=1, source_target_pairs={{8,0},{16,8},{24,16},{0,24},{9,1},{17,9},{25,17},{1,25},{10,2},{18... | collective-permute-start | bytes 196616 | tf_op jit(solution)/shard_map/ppermute | solution.py:452
  18.6 5.0 %collective-permute-start.9 = (bf16[256,128]{1,0:T(8,128)(2,1)S(1)}, bf16[256,128]{1,0:T(8,128)(2,1)S(1)}, u32[]{:S(2)}, u32[]{:S(2)}) collective-permute-start(bf16[256,128]{1,0:T(8,128)(2,1)S(1)} %collect.1.refs_0_), channel_id=1, source_target_pairs={{1,0},{0,1},{3,2},{2,3},{5,4},{4,5},{7,6},{6,7},{9,8},{8,9},{11,10... | collective-permute-start | bytes 196616 | tf_op jit(solution)/shard_map/ppermute | solution.py:29
  20.1 5.2 %collective-permute-start.8 = (bf16[256,128]{1,0:T(8,128)(2,1)S(1)}, bf16[256,128]{1,0:T(8,128)(2,1)S(1)}, u32[]{:S(2)}, u32[]{:S(2)}) collective-permute-start(bf16[256,128]{1,0:T(8,128)(2,1)S(1)} %block.3.refs_3_), channel_id=1, source_target_pairs={{9,0},{8,1},{1,8},{0,9},{25,16},{24,17},{17,24},{16,25},{11,2},{10... | collective-permute-start | bytes 196616 | tf_op jit(solution)/shard_map/ppermute | solution.py:491
  22.4 4.3 %collective-permute-start.7 = (bf16[256,128]{1,0:T(8,128)(2,1)S(1)}, bf16[256,128]{1,0:T(8,128)(2,1)S(1)}, u32[]{:S(2)}, u32[]{:S(2)}) collective-permute-start(bf16[256,128]{1,0:T(8,128)(2,1)S(1)} %block.3.refs_3_), channel_id=1, source_target_pairs={{8,0},{0,8},{24,16},{16,24},{9,1},{1,9},{25,17},{17,25},{10,2},{2,... | collective-permute-start | bytes 196616 | tf_op jit(solution)/shard_map/ppermute | solution.py:452
  22.4 4.3 %collective-permute-start.6 = (bf16[256,128]{1,0:T(8,128)(2,1)S(1)}, bf16[256,128]{1,0:T(8,128)(2,1)S(1)}, u32[]{:S(2)}, u32[]{:S(2)}) collective-permute-start(bf16[256,128]{1,0:T(8,128)(2,1)S(1)} %early.1.refs_0_), channel_id=1, source_target_pairs={{1,0},{0,1},{3,2},{2,3},{5,4},{4,5},{7,6},{6,7},{9,8},{8,9},{11,10... | collective-permute-start | bytes 196616 | tf_op jit(solution)/shard_map/ppermute | solution.py:29
  26.7 5.0 %collective-permute-start.10 = (bf16[512,128]{1,0:T(8,128)(2,1)S(1)}, bf16[512,128]{1,0:T(8,128)(2,1)S(1)}, u32[]{:S(2)}, u32[]{:S(2)}) collective-permute-start(bf16[512,128]{1,0:T(8,128)(2,1)S(1)} %choose.1.refs_0_.refs_1_), channel_id=1, source_target_pairs={{4,0},{5,1},{6,2},{7,3},{0,4},{1,5},{2,6},{3,7},{12,8},{13,9},{14,... | collective-permute-start | bytes 393224 | tf_op jit(solution)/shard_map/ppermute | solution.py:29
  30.4 1.4 %collective-permute-start.12 = (bf16[512,128]{1,0:T(8,128)(2,1)S(1)}, bf16[512,128]{1,0:T(8,128)(2,1)S(1)}, u32[]{:S(2)}, u32[]{:S(2)}) collective-permute-start(bf16[512,128]{1,0:T(8,128)(2,1)S(1)} %choose.1.refs_0_.refs_1_), channel_id=1, source_target_pairs={{2,0},{3,1},{0,2},{1,3},{6,4},{7,5},{4,6},{5,7},{10,8},{11,9},{8,1... | collective-permute-start | bytes 393224 | tf_op jit(solution)/shard_map/ppermute | solution.py:29
  31.8 1.4 %collective-permute-start.11 = (bf16[512,128]{1,0:T(8,128)(2,1)S(1)}, bf16[512,128]{1,0:T(8,128)(2,1)S(1)}, u32[]{:S(2)}, u32[]{:S(2)}) collective-permute-start(bf16[512,128]{1,0:T(8,128)(2,1)S(1)} %hand_on.1.refs_0_), channel_id=1, source_target_pairs={{2,0},{3,1},{0,2},{1,3},{6,4},{7,5},{4,6},{5,7},{10,8},{11,9},{8,1... | collective-permute-start | bytes 393224 | tf_op jit(solution)/shard_map/ppermute | solution.py:29

commit v6 on v5

--- a/solution.py
+++ b/solution.py
@@ -570,12 +570,13 @@
         across = kernel_call(
             pass_kernel,
             "hand_on",
-            [across, *kept_in_hbm(section_out)],
+            [across, *kept_in_hbm(section_out), sums[1]],
             crop_volume,
-            in_specs=whole() + unread(),
-        )
-        arrays = [across] + [moved(across, crop, 0) for crop in range(1, near)]
-        conv_rows, proj_rows = weight_sums(arrays, *plan_of(range(near, crops)), sums, True)
+            in_specs=whole() + unread(2),
+        )
+        arrays = [moved(across, crop, 0) for crop in range(1, near)]
+        sums = weight_sums([across], *plan_of([near]), sums, False)
+        conv_rows, proj_rows = weight_sums(arrays, *plan_of(range(near + 1, crops)), sums, True)
 
     section_grads = section_out.reshape(inputs.shape)
     grad_conv = conv_rows.reshape(taps, shard, channels).swapaxes(0, 1)[None]

time: 35.3 us -> 36.1 us (1.023)
  Pallas kernels: 9.93 us -> 10.4 us
    pallas_call x15 -> x16, Pallas kernels: 9.93 us -> 10.4 us  [kernel_call(): pl.pallas_call(body, out_shape=outs if single else tuple(outs), in_specs=...]
  transfers between devices with their start and end apart: 13 -> 13, of which waited for: 7 -> 7; matrix products, arithmetic and copies ran while one was open for 0% -> 0% of each run, Pallas kernels for 20% -> 21%
where the time goes in v6:
time: 36.1 us; the launch traced here: 35.9 us
  starting transfers between devices  18.9 us (52%)
  Pallas kernels  10.4 us (29%)
  waiting for transfers between devices  5.91 us (16%)
  between operations  0.73 us (2%)
    pallas_call x16, Pallas kernels, kernel_call(): pl.pallas_call(body, out_shape=outs if single else tuple(outs), in_specs=...  10.4 us
    ppermute x9, starting transfers between devices, moved(): return lax.ppermute(block, ('dp', 'space'), pairs)  9.39 us
    ppermute x3, starting transfers between devices, shards(): lax.ppermute(results[-1], 'section', hop_pairs(section_count, step))  7.21 us
    ppermute x9, waiting for transfers between devices, moved(): return lax.ppermute(block, ('dp', 'space'), pairs)  4.03 us
    ppermute x1, starting transfers between devices, shards(): lax.ppermute(results[-1], ('section', 'space'), [(source * slabs + peer(i...  2.28 us
    ppermute x3, waiting for transfers between devices, shards(): lax.ppermute(results[-1], 'section', hop_pairs(section_count, step))  1.67 us
  transfers between devices with their start and end apart: 13, of which 7 were waited for; matrix products, arithmetic and copies ran while one was open for 0% of the time, Pallas kernels for 21%

profile of v6, /device:TPU:0, one launch (start us, length us, event | category | flops | bytes accessed | tf_op | source)
XLA Modules:
  0.0 35.9 jit_solution(8750594536260917443)
XLA Ops:
  0.6 0.9 %outgoing.1 = bf16[3,1,64,256]{3,2,1,0:T(8,128)(2,1)S(1)} custom-call(bf16[2,1,64,256]{3,2,1,0:T(8,128)(2,1)} %bitcast.15, bf16[2,1,64,256]{3,2,1,0:T(8,128)(2,1)} %bitcast.17), custom_call_target="tpu_custom_call" | custom-call | tf_op jit(solution)/shard_map/outgoing/pallas_call | solution.py:374
  1.5 3.0 %collective-permute-start = (bf16[3,1,64,256]{3,2,1,0:T(8,128)(2,1)S(1)}, bf16[3,1,64,256]{3,2,1,0:T(8,128)(2,1)S(1)}, u32[]{:S(2)}, u32[]{:S(2)}) collective-permute-start(bf16[3,1,64,256]{3,2,1,0:T(8,128)(2,1)S(1)} %outgoing.1), channel_id=1, source_target_pairs={{1,0},{0,1},{3,2},{2,3},{5,4},{4,5},{7,6},{6,7},{9,8},{8,9},{11,10... | collective-permute-start | bytes 294920 | tf_op jit(solution)/shard_map/ppermute | solution.py:29
  4.6 2.1 %prepare.1 = (bf16[1,1,64,256]{3,2,1,0:T(8,128)(2,1)S(1)}, bf16[2,1,64,256]{3,2,1,0:T(8,128)(2,1)S(1)}, bf16[256,128]{1,0:T(8,128)(2,1)S(1)}, bf16[27,256,256]{2,1,0:T(8,128)(2,1)S(1)}, bf16[256,256]{1,0:T(8,128)(2,1)S(1)}) custom-call(bf16[2,1,64,256]{3,2,1,0:T(8,128)(2,1)} %bitcast.16, bf16[2,1,64,256]{3,2,1,0:T(8,128)(2,1)} %bitcast.18, ...), custom_call_target="tpu_custom_call" | custom-call | tf_op jit(solution)/shard_map/prepare/pallas_call | solution.py:374
  6.7 0.6 %collective-permute-done.refs_2_ = bf16[3,1,64,256]{3,2,1,0:T(8,128)(2,1)S(1)} collective-permute-done((bf16[3,1,64,256]{3,2,1,0:T(8,128)(2,1)S(1)}, bf16[3,1,64,256]{3,2,1,0:T(8,128)(2,1)S(1)}, u32[]{:S(2)}, u32[]{:S(2)}) %collective-permute-start) | collective-permute-done | bytes 98336 | tf_op jit(solution)/shard_map/ppermute | solution.py:29
  7.3 0.2 first_block.1
  7.5 1.9 %collective-permute-start.1 = (bf16[256,128]{1,0:T(8,128)(2,1)S(1)}, bf16[256,128]{1,0:T(8,128)(2,1)S(1)}, u32[]{:S(2)}, u32[]{:S(2)}) collective-permute-start(bf16[256,128]{1,0:T(8,128)(2,1)S(1)} %get-tuple-element.26), channel_id=1, source_target_pairs={{8,0},{0,8},{24,16},{16,24},{9,1},{1,9},{25,17},{17,25},{10,2},{2,... | collective-permute-start | bytes 196616 | tf_op jit(solution)/shard_map/ppermute | solution.py:452
  9.5 0.1 pack.1
  9.5 0.1 collective-permute-start.3
  9.6 1.6 %collective-permute-start.4 = (bf16[576,128]{1,0:T(8,128)(2,1)S(1)}, bf16[576,128]{1,0:T(8,128)(2,1)S(1)}, u32[]{:S(2)}, u32[]{:S(2)}) collective-permute-start(bf16[576,128]{1,0:T(8,128)(2,1)S(1)} %get-tuple-element.31), channel_id=1, source_target_pairs={{4,0},{5,1},{6,2},{7,3},{0,4},{1,5},{2,6},{3,7},{12,8},{13,9},{14,... | collective-permute-start | bytes 442376 | tf_op jit(solution)/shard_map/ppermute | solution.py:29
  11.2 0.3 collective-permute-start.5
  11.5 0.4 collective-permute-done.1.grad_ref.refs_1_
  11.8 5.3 %collective-permute-start.2 = (bf16[256,128]{1,0:T(8,128)(2,1)S(1)}, bf16[256,128]{1,0:T(8,128)(2,1)S(1)}, u32[]{:S(2)}, u32[]{:S(2)}) collective-permute-start(bf16[256,128]{1,0:T(8,128)(2,1)S(1)} %block.2), channel_id=1, source_target_pairs={{8,0},{16,8},{24,16},{0,24},{9,1},{17,9},{25,17},{1,25},{10,2},{18... | collective-permute-start | bytes 196616 | tf_op jit(solution)/shard_map/ppermute | solution.py:452
  17.1 0.0 collective-permute-done.3.refs_1_.refs_4_.refs_5_
  17.1 0.0 collective-permute-done.4.refs_2_.refs_1_
  17.1 1.5 %collective-permute-done.5.refs_3_.refs_1_.refs_2_ = bf16[576,128]{1,0:T(8,128)(2,1)S(1)} collective-permute-done((bf16[576,128]{1,0:T(8,128)(2,1)S(1)}, bf16[576,128]{1,0:T(8,128)(2,1)S(1)}, u32[]{:S(2)}, u32[]{:S(2)}) %collective-permute-start.5) | collective-permute-done | bytes 147488 | tf_op jit(solution)/shard_map/ppermute | solution.py:29
  18.6 1.5 %collective-permute-start.9 = (bf16[256,128]{1,0:T(8,128)(2,1)S(1)}, bf16[256,128]{1,0:T(8,128)(2,1)S(1)}, u32[]{:S(2)}, u32[]{:S(2)}) collective-permute-start(bf16[256,128]{1,0:T(8,128)(2,1)S(1)} %collect.1.refs_0_), channel_id=1, source_target_pairs={{1,0},{0,1},{3,2},{2,3},{5,4},{4,5},{7,6},{6,7},{9,8},{8,9},{11,10... | collective-permute-start | bytes 196616 | tf_op jit(solution)/shard_map/ppermute | solution.py:29
  20.1 0.0 collective-permute-done.2.grad_ref.refs_2_
  20.1 2.3 %collective-permute-start.8 = (bf16[256,128]{1,0:T(8,128)(2,1)S(1)}, bf16[256,128]{1,0:T(8,128)(2,1)S(1)}, u32[]{:S(2)}, u32[]{:S(2)}) collective-permute-start(bf16[256,128]{1,0:T(8,128)(2,1)S(1)} %block.3.refs_3_), channel_id=1, source_target_pairs={{9,0},{8,1},{1,8},{0,9},{25,16},{24,17},{17,24},{16,25},{11,2},{10... | collective-permute-start | bytes 196616 | tf_op jit(solution)/shard_map/ppermute | solution.py:491
  22.4 0.0 collective-permute-start.7
  22.4 1.2 %collective-permute-start.6 = (bf16[256,128]{1,0:T(8,128)(2,1)S(1)}, bf16[256,128]{1,0:T(8,128)(2,1)S(1)}, u32[]{:S(2)}, u32[]{:S(2)}) collective-permute-start(bf16[256,128]{1,0:T(8,128)(2,1)S(1)} %early.1.refs_0_), channel_id=1, source_target_pairs={{1,0},{0,1},{3,2},{2,3},{5,4},{4,5},{7,6},{6,7},{9,8},{8,9},{11,10... | collective-permute-start | bytes 196616 | tf_op jit(solution)/shard_map/ppermute | solution.py:29
  23.6 0.0 collective-permute-done.9.refs_1_
  23.6 1.5 %unfold.1.refs_2_.refs_6_.refs_3_ = bf16[2,1728,512]{2,1,0:T(8,128)(2,1)S(1)} custom-call(bf16[256,128]{1,0:T(8,128)(2,1)S(1)} %collect.1.refs_0_, bf16[256,128]{1,0:T(8,128)(2,1)S(1)} %collective-permute-done.9.refs_1_), custom_call_target="tpu_custom_call" | custom-call | tf_op jit(solution)/shard_map/unfold/pallas_call | solution.py:374
  25.1 0.2 collective-permute-done.8.refs_1_
  25.4 1.3 %collective-permute-done.7.refs_0_ = bf16[256,128]{1,0:T(8,128)(2,1)S(1)} collective-permute-done((bf16[256,128]{1,0:T(8,128)(2,1)S(1)}, bf16[256,128]{1,0:T(8,128)(2,1)S(1)}, u32[]{:S(2)}, u32[]{:S(2)}) %collective-permute-start.7) | collective-permute-done | bytes 65568 | tf_op jit(solution)/shard_map/ppermute | solution.py:452
  26.7 0.0 collective-permute-done.6.refs_1_
  26.7 0.1 collective-permute-start.11
  26.8 1.6 %collective-permute-start.10 = (bf16[512,128]{1,0:T(8,128)(2,1)S(1)}, bf16[512,128]{1,0:T(8,128)(2,1)S(1)}, u32[]{:S(2)}, u32[]{:S(2)}) collective-permute-start(bf16[512,128]{1,0:T(8,128)(2,1)S(1)} %choose.1.refs_0_.refs_1_), channel_id=1, source_target_pairs={{4,0},{5,1},{6,2},{7,3},{0,4},{1,5},{2,6},{3,7},{12,8},{13,9},{14,... | collective-permute-start | bytes 393224 | tf_op jit(solution)/shard_map/ppermute | solution.py:29
  28.3 2.2 %own_slab.1.refs_0_ = bf16[2,1,64,256]{3,2,1,0:T(8,128)(2,1)} custom-call(bf16[512,128]{1,0:T(8,128)(2,1)S(1)} %choose.1.refs_0_.refs_1_, bf16[512,128]{1,0:T(8,128)(2,1)S(1)} %choose.1.refs_0_.refs_1_, bf16[512,128]{1,0:T(8,128)(2,1)S(1)} %get-tuple-element.27.pre_ref.refs_2_, bf16[27,256,256]{2,1,0:T(8,128)(2,1)S(1)} %get-tuple-element.23.refs_3_.conv_ref, ...), custom_call_target="tpu_custom_call" | custom-call | tf_op jit(solution)/shard_map/own_slab/pallas_call | solution.py:374
  30.5 0.0 collective-permute-done.11.refs_1_
  30.5 1.0 %part_weight_grads.2 = (f32[1728,256]{1,0:T(8,128)S(1)}, f32[64,256]{1,0:T(8,128)S(1)}) custom-call(bf16[512,128]{1,0:T(8,128)(2,1)S(1)} %choose.1.refs_0_.refs_1_, bf16[512,128]{1,0:T(8,128)(2,1)S(1)} %collective-permute-done.11.refs_1_, bf16[576,128]{1,0:T(8,128)(2,1)S(1)} %get-tuple-element.29.refs_0_.refs_2_.refs_3_, ...), custom_call_target="tpu_custom_call" | custom-call | tf_op jit(solution)/shard_map/part_weight_grads/pallas_call | solution.py:374
  31.5 1.2 %collective-permute-done.10.block_ref = bf16[512,128]{1,0:T(8,128)(2,1)S(1)} collective-permute-done((bf16[512,128]{1,0:T(8,128)(2,1)S(1)}, bf16[512,128]{1,0:T(8,128)(2,1)S(1)}, u32[]{:S(2)}, u32[]{:S(2)}) %collective-permute-start.10) | collective-permute-done | bytes 131104 | tf_op jit(solution)/shard_map/ppermute | solution.py:29
  32.7 0.1 collective-permute-start.12
  32.8 0.7 %part_weight_grads.3 = (f32[1728,256]{1,0:T(8,128)S(1)}, f32[64,256]{1,0:T(8,128)S(1)}) custom-call(bf16[512,128]{1,0:T(8,128)(2,1)S(1)} %hand_on.1.refs_0_, bf16[576,128]{1,0:T(8,128)(2,1)S(1)} %collective-permute-done.4.refs_2_.refs_1_, bf16[576,128]{1,0:T(8,128)(2,1)S(1)} %collective-permute-done.4.refs_2_.refs_1_, ...), custom_call_target="tpu_custom_call" | custom-call | tf_op jit(solution)/shard_map/part_weight_grads/pallas_call | solution.py:374
  33.5 0.7 %collective-permute-done.12.refs_0_ = bf16[512,128]{1,0:T(8,128)(2,1)S(1)} collective-permute-done((bf16[512,128]{1,0:T(8,128)(2,1)S(1)}, bf16[512,128]{1,0:T(8,128)(2,1)S(1)}, u32[]{:S(2)}, u32[]{:S(2)}) %collective-permute-start.12) | collective-permute-done | bytes 131104 | tf_op jit(solution)/shard_map/ppermute | solution.py:29
  34.1 1.8 %weight_grads.1 = (f32[1728,256]{1,0:T(8,128)}, f32[64,256]{1,0:T(8,128)}) custom-call(bf16[512,128]{1,0:T(8,128)(2,1)S(1)} %collective-permute-done.12.refs_0_, bf16[576,128]{1,0:T(8,128)(2,1)S(1)} %collective-permute-done.5.refs_3_.refs_1_.refs_2_, bf16[576,128]{1,0:T(8,128)(2,1)S(1)} %collective-permute-done.5.refs_3_.refs_1_.refs_2_, ...), custom_call_target="tpu_custom_call" | custom-call | tf_op jit(solution)/shard_map/weight_grads/pallas_call | solution.py:374
  (7 shorter events, 0.0 us)
Async XLA Ops:
  1.5 5.8 %collective-permute-start = (bf16[3,1,64,256]{3,2,1,0:T(8,128)(2,1)S(1)}, bf16[3,1,64,256]{3,2,1,0:T(8,128)(2,1)S(1)}, u32[]{:S(2)}, u32[]{:S(2)}) collective-permute-start(bf16[3,1,64,256]{3,2,1,0:T(8,128)(2,1)S(1)} %outgoing.1), channel_id=1, source_target_pairs={{1,0},{0,1},{3,2},{2,3},{5,4},{4,5},{7,6},{6,7},{9,8},{8,9},{11,10... | collective-permute-start | bytes 294920 | tf_op jit(solution)/shard_map/ppermute | solution.py:29
  7.5 4.3 %collective-permute-start.1 = (bf16[256,128]{1,0:T(8,128)(2,1)S(1)}, bf16[256,128]{1,0:T(8,128)(2,1)S(1)}, u32[]{:S(2)}, u32[]{:S(2)}) collective-permute-start(bf16[256,128]{1,0:T(8,128)(2,1)S(1)} %get-tuple-element.26), channel_id=1, source_target_pairs={{8,0},{0,8},{24,16},{16,24},{9,1},{1,9},{25,17},{17,25},{10,2},{2,... | collective-permute-start | bytes 196616 | tf_op jit(solution)/shard_map/ppermute | solution.py:452
  9.5 7.6 %collective-permute-start.3 = (bf16[576,128]{1,0:T(8,128)(2,1)S(1)}, bf16[576,128]{1,0:T(8,128)(2,1)S(1)}, u32[]{:S(2)}, u32[]{:S(2)}) collective-permute-start(bf16[576,128]{1,0:T(8,128)(2,1)S(1)} %get-tuple-element.30), channel_id=1, source_target_pairs={{2,0},{3,1},{0,2},{1,3},{6,4},{7,5},{4,6},{5,7},{10,8},{11,9},{8,1... | collective-permute-start | bytes 442376 | tf_op jit(solution)/shard_map/ppermute | solution.py:29
  9.6 7.5 %collective-permute-start.4 = (bf16[576,128]{1,0:T(8,128)(2,1)S(1)}, bf16[576,128]{1,0:T(8,128)(2,1)S(1)}, u32[]{:S(2)}, u32[]{:S(2)}) collective-permute-start(bf16[576,128]{1,0:T(8,128)(2,1)S(1)} %get-tuple-element.31), channel_id=1, source_target_pairs={{4,0},{5,1},{6,2},{7,3},{0,4},{1,5},{2,6},{3,7},{12,8},{13,9},{14,... | collective-permute-start | bytes 442376 | tf_op jit(solution)/shard_map/ppermute | solution.py:29
  11.2 7.4 %collective-permute-start.5 = (bf16[576,128]{1,0:T(8,128)(2,1)S(1)}, bf16[576,128]{1,0:T(8,128)(2,1)S(1)}, u32[]{:S(2)}, u32[]{:S(2)}) collective-permute-start(bf16[576,128]{1,0:T(8,128)(2,1)S(1)} %get-tuple-element.32), channel_id=1, source_target_pairs={{6,0},{7,1},{4,2},{5,3},{2,4},{3,5},{0,6},{1,7},{14,8},{15,9},{12,... | collective-permute-start | bytes 442376 | tf_op jit(solution)/shard_map/ppermute | solution.py:29
  11.8 8.3 %collective-permute-start.2 = (bf16[256,128]{1,0:T(8,128)(2,1)S(1)}, bf16[256,128]{1,0:T(8,128)(2,1)S(1)}, u32[]{:S(2)}, u32[]{:S(2)}) collective-permute-start(bf16[256,128]{1,0:T(8,128)(2,1)S(1)} %block.2), channel_id=1, source_target_pairs={{8,0},{16,8},{24,16},{0,24},{9,1},{17,9},{25,17},{1,25},{10,2},{18... | collective-permute-start | bytes 196616 | tf_op jit(solution)/shard_map/ppermute | solution.py:452
  18.6 5.0 %collective-permute-start.9 = (bf16[256,128]{1,0:T(8,128)(2,1)S(1)}, bf16[256,128]{1,0:T(8,128)(2,1)S(1)}, u32[]{:S(2)}, u32[]{:S(2)}) collective-permute-start(bf16[256,128]{1,0:T(8,128)(2,1)S(1)} %collect.1.refs_0_), channel_id=1, source_target_pairs={{1,0},{0,1},{3,2},{2,3},{5,4},{4,5},{7,6},{6,7},{9,8},{8,9},{11,10... | collective-permute-start | bytes 196616 | tf_op jit(solution)/shard_map/ppermute | solution.py:29
  20.1 5.2 %collective-permute-start.8 = (bf16[256,128]{1,0:T(8,128)(2,1)S(1)}, bf16[256,128]{1,0:T(8,128)(2,1)S(1)}, u32[]{:S(2)}, u32[]{:S(2)}) collective-permute-start(bf16[256,128]{1,0:T(8,128)(2,1)S(1)} %block.3.refs_3_), channel_id=1, source_target_pairs={{9,0},{8,1},{1,8},{0,9},{25,16},{24,17},{17,24},{16,25},{11,2},{10... | collective-permute-start | bytes 196616 | tf_op jit(solution)/shard_map/ppermute | solution.py:491
  22.4 4.3 %collective-permute-start.7 = (bf16[256,128]{1,0:T(8,128)(2,1)S(1)}, bf16[256,128]{1,0:T(8,128)(2,1)S(1)}, u32[]{:S(2)}, u32[]{:S(2)}) collective-permute-start(bf16[256,128]{1,0:T(8,128)(2,1)S(1)} %block.3.refs_3_), channel_id=1, source_target_pairs={{8,0},{0,8},{24,16},{16,24},{9,1},{1,9},{25,17},{17,25},{10,2},{2,... | collective-permute-start | bytes 196616 | tf_op jit(solution)/shard_map/ppermute | solution.py:452
  22.4 4.3 %collective-permute-start.6 = (bf16[256,128]{1,0:T(8,128)(2,1)S(1)}, bf16[256,128]{1,0:T(8,128)(2,1)S(1)}, u32[]{:S(2)}, u32[]{:S(2)}) collective-permute-start(bf16[256,128]{1,0:T(8,128)(2,1)S(1)} %early.1.refs_0_), channel_id=1, source_target_pairs={{1,0},{0,1},{3,2},{2,3},{5,4},{4,5},{7,6},{6,7},{9,8},{8,9},{11,10... | collective-permute-start | bytes 196616 | tf_op jit(solution)/shard_map/ppermute | solution.py:29
  26.7 3.8 %collective-permute-start.11 = (bf16[512,128]{1,0:T(8,128)(2,1)S(1)}, bf16[512,128]{1,0:T(8,128)(2,1)S(1)}, u32[]{:S(2)}, u32[]{:S(2)}) collective-permute-start(bf16[512,128]{1,0:T(8,128)(2,1)S(1)} %choose.1.refs_0_.refs_1_), channel_id=1, source_target_pairs={{2,0},{3,1},{0,2},{1,3},{6,4},{7,5},{4,6},{5,7},{10,8},{11,9},{8,1... | collective-permute-start | bytes 393224 | tf_op jit(solution)/shard_map/ppermute | solution.py:29
  26.8 5.9 %collective-permute-start.10 = (bf16[512,128]{1,0:T(8,128)(2,1)S(1)}, bf16[512,128]{1,0:T(8,128)(2,1)S(1)}, u32[]{:S(2)}, u32[]{:S(2)}) collective-permute-start(bf16[512,128]{1,0:T(8,128)(2,1)S(1)} %choose.1.refs_0_.refs_1_), channel_id=1, source_target_pairs={{4,0},{5,1},{6,2},{7,3},{0,4},{1,5},{2,6},{3,7},{12,8},{13,9},{14,... | collective-permute-start | bytes 393224 | tf_op jit(solution)/shard_map/ppermute | solution.py:29
  32.7 1.4 %collective-permute-start.12 = (bf16[512,128]{1,0:T(8,128)(2,1)S(1)}, bf16[512,128]{1,0:T(8,128)(2,1)S(1)}, u32[]{:S(2)}, u32[]{:S(2)}) collective-permute-start(bf16[512,128]{1,0:T(8,128)(2,1)S(1)} %hand_on.1.refs_0_), channel_id=1, source_target_pairs={{2,0},{3,1},{0,2},{1,3},{6,4},{7,5},{4,6},{5,7},{10,8},{11,9},{8,1... | collective-permute-start | bytes 393224 | tf_op jit(solution)/shard_map/ppermute | solution.py:29

commit v7 on v5

--- a/solution.py
+++ b/solution.py
@@ -59,23 +59,15 @@
     return jnp.where(pre.astype(jnp.float32) > 0, hidden_grad, 0.0).astype(jnp.bfloat16)
 
 
-def outgoing_kernel(seed_ref, pre_ref, *refs):
+def outgoing_kernel(seed_ref, *refs):
     out_refs, sems = refs[:-1], refs[-1]
     here, count = lax.axis_index("space"), lax.axis_size("space")
-    micro = pre_ref.shape[0]
-    group = micro // count
     copies = []
     for distance, out_ref in enumerate(out_refs, 1):
+        group = out_ref.shape[0]
         span = pl.ds(peer(here, distance, count, back=True) * group, group)
-        pairs = (
-            (seed_ref.at[span], out_ref.at[pl.ds(0, group)]),
-            (pre_ref, out_ref.at[pl.ds(group, micro)]),
-        )
-        for place, (source, target) in enumerate(pairs):
-            copies.append(
-                pltpu.make_async_copy(source, target, sems.at[distance - 1, place])
-            )
-            copies[-1].start()
+        copies.append(pltpu.make_async_copy(seed_ref.at[span], out_ref, sems.at[distance - 1]))
+        copies[-1].start()
     for copy in copies:
         copy.wait()
 
@@ -105,21 +97,17 @@
 
 
 def first_kernel(others, extent, *refs):
-    seed_ref, pre_ref, arrived_refs = refs[0], refs[1], refs[2 : 2 + others]
-    conv_ref, proj_ref, grad_ref, pre_out_ref, out_ref, seed_scratch, pre_scratch = refs[
-        2 + others :
-    ]
+    seed_refs, refs = refs[: 1 + others], refs[1 + others :]
+    pre_refs, refs = refs[: 1 + others], refs[1 + others :]
+    conv_ref, proj_ref, grad_ref, pre_out_ref, out_ref, seed_scratch, pre_scratch = refs
     here, count = lax.axis_index("space"), lax.axis_size("space")
-    group, depth_dev = seed_ref.shape[:2]
-    channels = seed_ref.shape[-1]
+    group, depth_dev = seed_refs[0].shape[:2]
+    channels = seed_refs[0].shape[-1]
     for distance in range(count):
         start = peer(here, distance, count) * depth_dev
-        arrived = arrived_refs[distance - 1]
-        seeds = seed_ref if distance == 0 else arrived.at[pl.ds(0, group)]
-        pres = pre_ref if distance == 0 else arrived.at[pl.ds(group, group * count)]
         for depth in range(depth_dev):
-            seed_scratch[:, start + depth] = seeds[:, depth].astype(jnp.float32)
-            pre_scratch[:, start + depth] = pres[:, depth].astype(jnp.float32)
+            seed_scratch[:, start + depth] = seed_refs[distance][:, depth].astype(jnp.float32)
+            pre_scratch[:, start + depth] = pre_refs[distance][:, depth].astype(jnp.float32)
     grad_ref[...] = seed_scratch[...].reshape(-1, channels).T.astype(jnp.bfloat16)
     for distance in range(count):
         span = pl.ds(peer(here, distance, count) * group, group)
@@ -408,15 +396,16 @@
     parcel = jax.ShapeDtypeStruct((slabs * channels + padded, lanes), bfloat)
     hbm = pl.BlockSpec(memory_space=pltpu.HBM)
 
-    arrived = kernel_call(
+    pre_rows = [moved(pre_acts, 0, distance) for distance in range(1, slabs)]
+    seed_rows = kernel_call(
         outgoing_kernel,
         "outgoing",
-        kept_in_hbm(seeds, pre_acts),
-        [jax.ShapeDtypeStruct((group + micro,) + part.shape[1:], bfloat)] * others,
-        scratch=[pltpu.SemaphoreType.DMA((others, 2))],
-        in_specs=[hbm] * 2,
-    )
-    arrived = [moved(block, 0, distance) for distance, block in enumerate(arrived, 1)]
+        kept_in_hbm(seeds),
+        [part] * others,
+        scratch=[pltpu.SemaphoreType.DMA((others,))],
+        in_specs=[hbm],
+    )
+    seed_rows = [moved(block, 0, distance) for distance, block in enumerate(seed_rows, 1)]
     seed_own, pre_own, acts_own, conv_weight, proj_weight = kernel_call(
         prepare_kernel,
         "prepare",
@@ -434,7 +423,7 @@
     grad_first, pre_all, result = kernel_call(
         functools.partial(first_kernel, others, extent),
         "first_block",
-        [seed_own, pre_own, *arrived, conv_weight, proj_weight],
+        [seed_own, *seed_rows, pre_own, *pre_rows, conv_weight, proj_weight],
         [volume, crop_volume, volume],
         scratch=[
             pltpu.VMEM((size, depth_all, area, channels), jnp.float32) for size in (group, micro)

time: 35.3 us -> 36 us (1.020)
  waiting for transfers between devices: 5.67 us -> 7.44 us
  starting transfers between devices: 18.8 us -> 17.5 us
    ppermute x9 -> x10, starting transfers between devices: 9.32 us -> 7.94 us  [moved(): return lax.ppermute(block, ('dp', 'space'), pairs)]
    ppermute x9 -> x10, waiting for transfers between devices: 3.79 us -> 5.01 us  [moved(): return lax.ppermute(block, ('dp', 'space'), pairs)]
    ppermute x1, starting transfers between devices: 2.28 us -> 2.83 us  [shards(): lax.ppermute(results[-1], ('section', 'space'), [(source * slabs + peer(i...]
    ppermute x3, waiting for transfers between devices: 1.67 us -> 2.13 us  [shards(): lax.ppermute(results[-1], 'section', hop_pairs(section_count, step))]
    ppermute x3, starting transfers between devices: 7.21 us -> 6.76 us  [shards(): lax.ppermute(results[-1], 'section', hop_pairs(section_count, step))]
  transfers between devices with their start and end apart: 13 -> 14, of which waited for: 7 -> 8; matrix products, arithmetic and copies ran while one was open for 0% -> 0% of each run, Pallas kernels for 20% -> 22%
where the time goes in v7:
time: 36 us; the launch traced here: 35.5 us
  starting transfers between devices  17.5 us (49%)
  Pallas kernels  9.79 us (27%)
  waiting for transfers between devices  7.44 us (21%)
  between operations  0.72 us (2%)
    pallas_call x15, Pallas kernels, kernel_call(): pl.pallas_call(body, out_shape=outs if single else tuple(outs), in_specs=...  9.79 us
    ppermute x10, starting transfers between devices, moved(): return lax.ppermute(block, ('dp', 'space'), pairs)  7.94 us
    ppermute x3, starting transfers between devices, shards(): lax.ppermute(results[-1], 'section', hop_pairs(section_count, step))  6.76 us
    ppermute x10, waiting for transfers between devices, moved(): return lax.ppermute(block, ('dp', 'space'), pairs)  5.01 us
    ppermute x1, starting transfers between devices, shards(): lax.ppermute(results[-1], ('section', 'space'), [(source * slabs + peer(i...  2.83 us
    ppermute x3, waiting for transfers between devices, shards(): lax.ppermute(results[-1], 'section', hop_pairs(section_count, step))  2.13 us
  transfers between devices with their start and end apart: 14, of which 8 were waited for; matrix products, arithmetic and copies ran while one was open for 0% of the time, Pallas kernels for 22%

profile of v7, /device:TPU:0, one launch (start us, length us, event | category | flops | bytes accessed | tf_op | source)
XLA Modules:
  0.0 35.5 jit_solution(7663399979899577330)
XLA Ops:
  0.6 3.0 %collective-permute-start.1 = (bf16[2,1,64,256]{3,2,1,0:T(8,128)(2,1)}, bf16[2,1,64,256]{3,2,1,0:T(8,128)(2,1)S(1)}, u32[]{:S(2)}, u32[]{:S(2)}) collective-permute-start(bf16[2,1,64,256]{3,2,1,0:T(8,128)(2,1)} %bitcast.20), channel_id=1, source_target_pairs={{1,0},{0,1},{3,2},{2,3},{5,4},{4,5},{7,6},{6,7},{9,8},{8,9},{11,10... | collective-permute-start | bytes 196616 | tf_op jit(solution)/shard_map/ppermute | solution.py:29
  3.7 0.8 %outgoing.1 = bf16[1,1,64,256]{3,2,1,0:T(8,128)(2,1)S(1)} custom-call(bf16[2,1,64,256]{3,2,1,0:T(8,128)(2,1)} %bitcast.16), custom_call_target="tpu_custom_call" | custom-call | tf_op jit(solution)/shard_map/outgoing/pallas_call | solution.py:362
  4.4 0.1 collective-permute-start
  4.5 2.1 %prepare.1 = (bf16[1,1,64,256]{3,2,1,0:T(8,128)(2,1)S(1)}, bf16[2,1,64,256]{3,2,1,0:T(8,128)(2,1)S(1)}, bf16[256,128]{1,0:T(8,128)(2,1)S(1)}, bf16[27,256,256]{2,1,0:T(8,128)(2,1)S(1)}, bf16[256,256]{1,0:T(8,128)(2,1)S(1)}) custom-call(bf16[2,1,64,256]{3,2,1,0:T(8,128)(2,1)} %bitcast.17, bf16[2,1,64,256]{3,2,1,0:T(8,128)(2,1)} %bitcast.21, ...), custom_call_target="tpu_custom_call" | custom-call | tf_op jit(solution)/shard_map/prepare/pallas_call | solution.py:362
  6.7 1.7 %collective-permute-done.refs_1_ = bf16[1,1,64,256]{3,2,1,0:T(8,128)(2,1)S(1)} collective-permute-done((bf16[1,1,64,256]{3,2,1,0:T(8,128)(2,1)S(1)}, bf16[1,1,64,256]{3,2,1,0:T(8,128)(2,1)S(1)}, u32[]{:S(2)}, u32[]{:S(2)}) %collective-permute-start) | collective-permute-done | bytes 32800 | tf_op jit(solution)/shard_map/ppermute | solution.py:29
  8.4 0.0 collective-permute-done.1.refs_3_
  8.4 0.2 first_block.1
  8.6 1.6 %collective-permute-start.2 = (bf16[256,128]{1,0:T(8,128)(2,1)S(1)}, bf16[256,128]{1,0:T(8,128)(2,1)S(1)}, u32[]{:S(2)}, u32[]{:S(2)}) collective-permute-start(bf16[256,128]{1,0:T(8,128)(2,1)S(1)} %get-tuple-element.24), channel_id=1, source_target_pairs={{8,0},{0,8},{24,16},{16,24},{9,1},{1,9},{25,17},{17,25},{10,2},{2,... | collective-permute-start | bytes 196616 | tf_op jit(solution)/shard_map/ppermute | solution.py:441
  10.2 0.1 pack.1
  10.3 0.1 collective-permute-start.4
  10.4 1.6 %collective-permute-start.5 = (bf16[576,128]{1,0:T(8,128)(2,1)S(1)}, bf16[576,128]{1,0:T(8,128)(2,1)S(1)}, u32[]{:S(2)}, u32[]{:S(2)}) collective-permute-start(bf16[576,128]{1,0:T(8,128)(2,1)S(1)} %get-tuple-element.29), channel_id=1, source_target_pairs={{4,0},{5,1},{6,2},{7,3},{0,4},{1,5},{2,6},{3,7},{12,8},{13,9},{14,... | collective-permute-start | bytes 442376 | tf_op jit(solution)/shard_map/ppermute | solution.py:29
  11.9 0.3 collective-permute-start.6
  12.3 0.7 %collective-permute-done.2.grad_ref.refs_1_ = bf16[256,128]{1,0:T(8,128)(2,1)S(1)} collective-permute-done((bf16[256,128]{1,0:T(8,128)(2,1)S(1)}, bf16[256,128]{1,0:T(8,128)(2,1)S(1)}, u32[]{:S(2)}, u32[]{:S(2)}) %collective-permute-start.2) | collective-permute-done | bytes 65568 | tf_op jit(solution)/shard_map/ppermute | solution.py:441
  12.9 5.0 %collective-permute-start.3 = (bf16[256,128]{1,0:T(8,128)(2,1)S(1)}, bf16[256,128]{1,0:T(8,128)(2,1)S(1)}, u32[]{:S(2)}, u32[]{:S(2)}) collective-permute-start(bf16[256,128]{1,0:T(8,128)(2,1)S(1)} %block.2), channel_id=1, source_target_pairs={{8,0},{16,8},{24,16},{0,24},{9,1},{17,9},{25,17},{1,25},{10,2},{18... | collective-permute-start | bytes 196616 | tf_op jit(solution)/shard_map/ppermute | solution.py:441
  17.9 0.0 collective-permute-done.4.refs_1_.refs_4_.refs_5_
  17.9 0.0 collective-permute-done.5.refs_2_.refs_3_
  17.9 1.5 %collective-permute-done.6.refs_3_.refs_4_.refs_5_ = bf16[576,128]{1,0:T(8,128)(2,1)S(1)} collective-permute-done((bf16[576,128]{1,0:T(8,128)(2,1)S(1)}, bf16[576,128]{1,0:T(8,128)(2,1)S(1)}, u32[]{:S(2)}, u32[]{:S(2)}) %collective-permute-start.6) | collective-permute-done | bytes 147488 | tf_op jit(solution)/shard_map/ppermute | solution.py:29
  19.4 0.5 %collective-permute-start.10 = (bf16[256,128]{1,0:T(8,128)(2,1)S(1)}, bf16[256,128]{1,0:T(8,128)(2,1)S(1)}, u32[]{:S(2)}, u32[]{:S(2)}) collective-permute-start(bf16[256,128]{1,0:T(8,128)(2,1)S(1)} %collect.1.refs_0_), channel_id=1, source_target_pairs={{1,0},{0,1},{3,2},{2,3},{5,4},{4,5},{7,6},{6,7},{9,8},{8,9},{11,10... | collective-permute-start | bytes 196616 | tf_op jit(solution)/shard_map/ppermute | solution.py:29
  19.9 0.0 collective-permute-done.3.grad_ref.refs_2_
  19.9 2.8 %collective-permute-start.9 = (bf16[256,128]{1,0:T(8,128)(2,1)S(1)}, bf16[256,128]{1,0:T(8,128)(2,1)S(1)}, u32[]{:S(2)}, u32[]{:S(2)}) collective-permute-start(bf16[256,128]{1,0:T(8,128)(2,1)S(1)} %block.3.refs_3_), channel_id=1, source_target_pairs={{9,0},{8,1},{1,8},{0,9},{25,16},{24,17},{17,24},{16,25},{11,2},{10... | collective-permute-start | bytes 196616 | tf_op jit(solution)/shard_map/ppermute | solution.py:480
  22.7 0.2 collective-permute-start.8
  22.9 0.8 %collective-permute-start.7 = (bf16[256,128]{1,0:T(8,128)(2,1)S(1)}, bf16[256,128]{1,0:T(8,128)(2,1)S(1)}, u32[]{:S(2)}, u32[]{:S(2)}) collective-permute-start(bf16[256,128]{1,0:T(8,128)(2,1)S(1)} %early.1.refs_0_), channel_id=1, source_target_pairs={{1,0},{0,1},{3,2},{2,3},{5,4},{4,5},{7,6},{6,7},{9,8},{8,9},{11,10... | collective-permute-start | bytes 196616 | tf_op jit(solution)/shard_map/ppermute | solution.py:29
  23.7 0.0 collective-permute-done.10.refs_1_
  23.7 1.5 %unfold.1.refs_2_.refs_6_ = bf16[2,1728,512]{2,1,0:T(8,128)(2,1)S(1)} custom-call(bf16[256,128]{1,0:T(8,128)(2,1)S(1)} %collect.1.refs_0_, bf16[256,128]{1,0:T(8,128)(2,1)S(1)} %collective-permute-done.10.refs_1_), custom_call_target="tpu_custom_call" | custom-call | tf_op jit(solution)/shard_map/unfold/pallas_call | solution.py:362
  25.2 0.3 collective-permute-done.9.refs_1_
  25.5 1.5 %collective-permute-done.8.refs_0_ = bf16[256,128]{1,0:T(8,128)(2,1)S(1)} collective-permute-done((bf16[256,128]{1,0:T(8,128)(2,1)S(1)}, bf16[256,128]{1,0:T(8,128)(2,1)S(1)}, u32[]{:S(2)}, u32[]{:S(2)}) %collective-permute-start.8) | collective-permute-done | bytes 65568 | tf_op jit(solution)/shard_map/ppermute | solution.py:441
  27.0 0.1 collective-permute-done.7.refs_1_
  27.1 1.5 %collective-permute-start.11 = (bf16[512,128]{1,0:T(8,128)(2,1)S(1)}, bf16[512,128]{1,0:T(8,128)(2,1)S(1)}, u32[]{:S(2)}, u32[]{:S(2)}) collective-permute-start(bf16[512,128]{1,0:T(8,128)(2,1)S(1)} %choose.1.refs_0_.refs_1_), channel_id=1, source_target_pairs={{4,0},{5,1},{6,2},{7,3},{0,4},{1,5},{2,6},{3,7},{12,8},{13,9},{14,... | collective-permute-start | bytes 393224 | tf_op jit(solution)/shard_map/ppermute | solution.py:29
  28.6 2.2 %own_slab.1.refs_0_ = bf16[2,1,64,256]{3,2,1,0:T(8,128)(2,1)} custom-call(bf16[512,128]{1,0:T(8,128)(2,1)S(1)} %choose.1.refs_0_.refs_1_, bf16[512,128]{1,0:T(8,128)(2,1)S(1)} %choose.1.refs_0_.refs_1_, bf16[512,128]{1,0:T(8,128)(2,1)S(1)} %get-tuple-element.25.pre_ref.refs_2_, bf16[27,256,256]{2,1,0:T(8,128)(2,1)S(1)} %get-tuple-element.21.refs_4_.conv_ref.refs_3_, ...), custom_call_target="tpu_custom_call" | custom-call | tf_op jit(solution)/shard_map/own_slab/pallas_call | solution.py:362
  30.8 0.0 collective-permute-start.13
  30.8 1.3 %collective-permute-done.11.block_ref = bf16[512,128]{1,0:T(8,128)(2,1)S(1)} collective-permute-done((bf16[512,128]{1,0:T(8,128)(2,1)S(1)}, bf16[512,128]{1,0:T(8,128)(2,1)S(1)}, u32[]{:S(2)}, u32[]{:S(2)}) %collective-permute-start.11) | collective-permute-done | bytes 131104 | tf_op jit(solution)/shard_map/ppermute | solution.py:29
  32.1 0.1 collective-permute-start.12
  32.2 0.0 collective-permute-done.13.refs_1_
  32.2 1.0 %part_weight_grads.1 = (f32[1728,256]{1,0:T(8,128)S(1)}, f32[64,256]{1,0:T(8,128)S(1)}) custom-call(bf16[512,128]{1,0:T(8,128)(2,1)S(1)} %choose.1.refs_0_.refs_1_, bf16[512,128]{1,0:T(8,128)(2,1)S(1)} %collective-permute-done.13.refs_1_, bf16[576,128]{1,0:T(8,128)(2,1)S(1)} %get-tuple-element.27.refs_0_.refs_2_.refs_3_, ...), custom_call_target="tpu_custom_call" | custom-call | tf_op jit(solution)/shard_map/part_weight_grads/pallas_call | solution.py:362
  33.2 0.3 collective-permute-done.12.refs_1_
  33.5 2.0 %weight_grads.1 = (f32[1728,256]{1,0:T(8,128)}, f32[64,256]{1,0:T(8,128)}) custom-call(bf16[512,128]{1,0:T(8,128)(2,1)S(1)} %hand_on.1.refs_0_, bf16[512,128]{1,0:T(8,128)(2,1)S(1)} %collective-permute-done.12.refs_1_, bf16[576,128]{1,0:T(8,128)(2,1)S(1)} %collective-permute-done.5.refs_2_.refs_3_, ...), custom_call_target="tpu_custom_call" | custom-call | tf_op jit(solution)/shard_map/weight_grads/pallas_call | solution.py:362
  (7 shorter events, 0.0 us)
Async XLA Ops:
  0.6 7.8 %collective-permute-start.1 = (bf16[2,1,64,256]{3,2,1,0:T(8,128)(2,1)}, bf16[2,1,64,256]{3,2,1,0:T(8,128)(2,1)S(1)}, u32[]{:S(2)}, u32[]{:S(2)}) collective-permute-start(bf16[2,1,64,256]{3,2,1,0:T(8,128)(2,1)} %bitcast.20), channel_id=1, source_target_pairs={{1,0},{0,1},{3,2},{2,3},{5,4},{4,5},{7,6},{6,7},{9,8},{8,9},{11,10... | collective-permute-start | bytes 196616 | tf_op jit(solution)/shard_map/ppermute | solution.py:29
  4.4 4.0 %collective-permute-start = (bf16[1,1,64,256]{3,2,1,0:T(8,128)(2,1)S(1)}, bf16[1,1,64,256]{3,2,1,0:T(8,128)(2,1)S(1)}, u32[]{:S(2)}, u32[]{:S(2)}) collective-permute-start(bf16[1,1,64,256]{3,2,1,0:T(8,128)(2,1)S(1)} %outgoing.1), channel_id=1, source_target_pairs={{1,0},{0,1},{3,2},{2,3},{5,4},{4,5},{7,6},{6,7},{9,8},{8,9},{11,10... | collective-permute-start | bytes 98312 | tf_op jit(solution)/shard_map/ppermute | solution.py:29
  8.6 4.3 %collective-permute-start.2 = (bf16[256,128]{1,0:T(8,128)(2,1)S(1)}, bf16[256,128]{1,0:T(8,128)(2,1)S(1)}, u32[]{:S(2)}, u32[]{:S(2)}) collective-permute-start(bf16[256,128]{1,0:T(8,128)(2,1)S(1)} %get-tuple-element.24), channel_id=1, source_target_pairs={{8,0},{0,8},{24,16},{16,24},{9,1},{1,9},{25,17},{17,25},{10,2},{2,... | collective-permute-start | bytes 196616 | tf_op jit(solution)/shard_map/ppermute | solution.py:441
  10.3 7.6 %collective-permute-start.4 = (bf16[576,128]{1,0:T(8,128)(2,1)S(1)}, bf16[576,128]{1,0:T(8,128)(2,1)S(1)}, u32[]{:S(2)}, u32[]{:S(2)}) collective-permute-start(bf16[576,128]{1,0:T(8,128)(2,1)S(1)} %get-tuple-element.28), channel_id=1, source_target_pairs={{2,0},{3,1},{0,2},{1,3},{6,4},{7,5},{4,6},{5,7},{10,8},{11,9},{8,1... | collective-permute-start | bytes 442376 | tf_op jit(solution)/shard_map/ppermute | solution.py:29
  10.4 7.5 %collective-permute-start.5 = (bf16[576,128]{1,0:T(8,128)(2,1)S(1)}, bf16[576,128]{1,0:T(8,128)(2,1)S(1)}, u32[]{:S(2)}, u32[]{:S(2)}) collective-permute-start(bf16[576,128]{1,0:T(8,128)(2,1)S(1)} %get-tuple-element.29), channel_id=1, source_target_pairs={{4,0},{5,1},{6,2},{7,3},{0,4},{1,5},{2,6},{3,7},{12,8},{13,9},{14,... | collective-permute-start | bytes 442376 | tf_op jit(solution)/shard_map/ppermute | solution.py:29
  11.9 7.4 %collective-permute-start.6 = (bf16[576,128]{1,0:T(8,128)(2,1)S(1)}, bf16[576,128]{1,0:T(8,128)(2,1)S(1)}, u32[]{:S(2)}, u32[]{:S(2)}) collective-permute-start(bf16[576,128]{1,0:T(8,128)(2,1)S(1)} %get-tuple-element.30), channel_id=1, source_target_pairs={{6,0},{7,1},{4,2},{5,3},{2,4},{3,5},{0,6},{1,7},{14,8},{15,9},{12,... | collective-permute-start | bytes 442376 | tf_op jit(solution)/shard_map/ppermute | solution.py:29
  12.9 7.0 %collective-permute-start.3 = (bf16[256,128]{1,0:T(8,128)(2,1)S(1)}, bf16[256,128]{1,0:T(8,128)(2,1)S(1)}, u32[]{:S(2)}, u32[]{:S(2)}) collective-permute-start(bf16[256,128]{1,0:T(8,128)(2,1)S(1)} %block.2), channel_id=1, source_target_pairs={{8,0},{16,8},{24,16},{0,24},{9,1},{17,9},{25,17},{1,25},{10,2},{18... | collective-permute-start | bytes 196616 | tf_op jit(solution)/shard_map/ppermute | solution.py:441
  19.4 4.3 %collective-permute-start.10 = (bf16[256,128]{1,0:T(8,128)(2,1)S(1)}, bf16[256,128]{1,0:T(8,128)(2,1)S(1)}, u32[]{:S(2)}, u32[]{:S(2)}) collective-permute-start(bf16[256,128]{1,0:T(8,128)(2,1)S(1)} %collect.1.refs_0_), channel_id=1, source_target_pairs={{1,0},{0,1},{3,2},{2,3},{5,4},{4,5},{7,6},{6,7},{9,8},{8,9},{11,10... | collective-permute-start | bytes 196616 | tf_op jit(solution)/shard_map/ppermute | solution.py:29
  19.9 5.6 %collective-permute-start.9 = (bf16[256,128]{1,0:T(8,128)(2,1)S(1)}, bf16[256,128]{1,0:T(8,128)(2,1)S(1)}, u32[]{:S(2)}, u32[]{:S(2)}) collective-permute-start(bf16[256,128]{1,0:T(8,128)(2,1)S(1)} %block.3.refs_3_), channel_id=1, source_target_pairs={{9,0},{8,1},{1,8},{0,9},{25,16},{24,17},{17,24},{16,25},{11,2},{10... | collective-permute-start | bytes 196616 | tf_op jit(solution)/shard_map/ppermute | solution.py:480
  22.7 4.3 %collective-permute-start.8 = (bf16[256,128]{1,0:T(8,128)(2,1)S(1)}, bf16[256,128]{1,0:T(8,128)(2,1)S(1)}, u32[]{:S(2)}, u32[]{:S(2)}) collective-permute-start(bf16[256,128]{1,0:T(8,128)(2,1)S(1)} %block.3.refs_3_), channel_id=1, source_target_pairs={{8,0},{0,8},{24,16},{16,24},{9,1},{1,9},{25,17},{17,25},{10,2},{2,... | collective-permute-start | bytes 196616 | tf_op jit(solution)/shard_map/ppermute | solution.py:441
  22.9 4.3 %collective-permute-start.7 = (bf16[256,128]{1,0:T(8,128)(2,1)S(1)}, bf16[256,128]{1,0:T(8,128)(2,1)S(1)}, u32[]{:S(2)}, u32[]{:S(2)}) collective-permute-start(bf16[256,128]{1,0:T(8,128)(2,1)S(1)} %early.1.refs_0_), channel_id=1, source_target_pairs={{1,0},{0,1},{3,2},{2,3},{5,4},{4,5},{7,6},{6,7},{9,8},{8,9},{11,10... | collective-permute-start | bytes 196616 | tf_op jit(solution)/shard_map/ppermute | solution.py:29
  27.1 5.0 %collective-permute-start.11 = (bf16[512,128]{1,0:T(8,128)(2,1)S(1)}, bf16[512,128]{1,0:T(8,128)(2,1)S(1)}, u32[]{:S(2)}, u32[]{:S(2)}) collective-permute-start(bf16[512,128]{1,0:T(8,128)(2,1)S(1)} %choose.1.refs_0_.refs_1_), channel_id=1, source_target_pairs={{4,0},{5,1},{6,2},{7,3},{0,4},{1,5},{2,6},{3,7},{12,8},{13,9},{14,... | collective-permute-start | bytes 393224 | tf_op jit(solution)/shard_map/ppermute | solution.py:29
  30.8 1.4 %collective-permute-start.13 = (bf16[512,128]{1,0:T(8,128)(2,1)S(1)}, bf16[512,128]{1,0:T(8,128)(2,1)S(1)}, u32[]{:S(2)}, u32[]{:S(2)}) collective-permute-start(bf16[512,128]{1,0:T(8,128)(2,1)S(1)} %choose.1.refs_0_.refs_1_), channel_id=1, source_target_pairs={{2,0},{3,1},{0,2},{1,3},{6,4},{7,5},{4,6},{5,7},{10,8},{11,9},{8,1... | collective-permute-start | bytes 393224 | tf_op jit(solution)/shard_map/ppermute | solution.py:29
  32.1 1.4 %collective-permute-start.12 = (bf16[512,128]{1,0:T(8,128)(2,1)S(1)}, bf16[512,128]{1,0:T(8,128)(2,1)S(1)}, u32[]{:S(2)}, u32[]{:S(2)}) collective-permute-start(bf16[512,128]{1,0:T(8,128)(2,1)S(1)} %hand_on.1.refs_0_), channel_id=1, source_target_pairs={{2,0},{3,1},{0,2},{1,3},{6,4},{7,5},{4,6},{5,7},{10,8},{11,9},{8,1... | collective-permute-start | bytes 393224 | tf_op jit(solution)/shard_map/ppermute | solution.py:29

commit v8 on v6

--- a/solution.py
+++ b/solution.py
@@ -566,7 +566,7 @@
     else:
         across = moved(crop_grad, near, 0)
         arrays = [crop_grad] + [moved(crop_grad, crop, 0) for crop in range(1, near)]
-        sums = weight_sums(arrays, *plan_of(range(near)), (), False)
+        sums = weight_sums(arrays[:1], *plan_of([0]), (), False)
         across = kernel_call(
             pass_kernel,
             "hand_on",
@@ -574,8 +574,9 @@
             crop_volume,
             in_specs=whole() + unread(2),
         )
+        arrays = arrays[1:] + [across]
+        sums = weight_sums(arrays, *plan_of(range(1, near + 1)), sums, False)
         arrays = [moved(across, crop, 0) for crop in range(1, near)]
-        sums = weight_sums([across], *plan_of([near]), sums, False)
         conv_rows, proj_rows = weight_sums(arrays, *plan_of(range(near + 1, crops)), sums, True)
 
     section_grads = section_out.reshape(inputs.shape)

time: 36.1 us -> 35.1 us (0.972)
  waiting for transfers between devices: 5.91 us -> 5.01 us
    ppermute x9, waiting for transfers between devices: 4.03 us -> 3.14 us  [moved(): return lax.ppermute(block, ('dp', 'space'), pairs)]
  transfers between devices with their start and end apart: 13 -> 13, of which waited for: 7 -> 7; matrix products, arithmetic and copies ran while one was open for 0% -> 0% of each run, Pallas kernels for 21% -> 22%
where the time goes in v8:
time: 35.1 us; the launch traced here: 35 us
  starting transfers between devices  18.8 us (54%)
  Pallas kernels  10.4 us (30%)
  waiting for transfers between devices  5.01 us (14%)
  between operations  0.72 us (2%)
    pallas_call x16, Pallas kernels, kernel_call(): pl.pallas_call(body, out_shape=outs if single else tuple(outs), in_specs=...  10.4 us
    ppermute x9, starting transfers between devices, moved(): return lax.ppermute(block, ('dp', 'space'), pairs)  9.32 us
    ppermute x3, starting transfers between devices, shards(): lax.ppermute(results[-1], 'section', hop_pairs(section_count, step))  7.21 us
    ppermute x9, waiting for transfers between devices, moved(): return lax.ppermute(block, ('dp', 'space'), pairs)  3.14 us
    ppermute x1, starting transfers between devices, shards(): lax.ppermute(results[-1], ('section', 'space'), [(source * slabs + peer(i...  2.28 us
    ppermute x3, waiting for transfers between devices, shards(): lax.ppermute(results[-1], 'section', hop_pairs(section_count, step))  1.67 us
  transfers between devices with their start and end apart: 13, of which 7 were waited for; matrix products, arithmetic and copies ran while one was open for 0% of the time, Pallas kernels for 22%

profile of v8, /device:TPU:0, one launch (start us, length us, event | category | flops | bytes accessed | tf_op | source)
XLA Modules:
  0.0 35.0 jit_solution(12814694489141004019)
XLA Ops:
  0.6 0.9 %outgoing.1 = bf16[3,1,64,256]{3,2,1,0:T(8,128)(2,1)S(1)} custom-call(bf16[2,1,64,256]{3,2,1,0:T(8,128)(2,1)} %bitcast.15, bf16[2,1,64,256]{3,2,1,0:T(8,128)(2,1)} %bitcast.17), custom_call_target="tpu_custom_call" | custom-call | tf_op jit(solution)/shard_map/outgoing/pallas_call | solution.py:374
  1.5 3.0 %collective-permute-start = (bf16[3,1,64,256]{3,2,1,0:T(8,128)(2,1)S(1)}, bf16[3,1,64,256]{3,2,1,0:T(8,128)(2,1)S(1)}, u32[]{:S(2)}, u32[]{:S(2)}) collective-permute-start(bf16[3,1,64,256]{3,2,1,0:T(8,128)(2,1)S(1)} %outgoing.1), channel_id=1, source_target_pairs={{1,0},{0,1},{3,2},{2,3},{5,4},{4,5},{7,6},{6,7},{9,8},{8,9},{11,10... | collective-permute-start | bytes 294920 | tf_op jit(solution)/shard_map/ppermute | solution.py:29
  4.6 2.1 %prepare.1 = (bf16[1,1,64,256]{3,2,1,0:T(8,128)(2,1)S(1)}, bf16[2,1,64,256]{3,2,1,0:T(8,128)(2,1)S(1)}, bf16[256,128]{1,0:T(8,128)(2,1)S(1)}, bf16[27,256,256]{2,1,0:T(8,128)(2,1)S(1)}, bf16[256,256]{1,0:T(8,128)(2,1)S(1)}) custom-call(bf16[2,1,64,256]{3,2,1,0:T(8,128)(2,1)} %bitcast.16, bf16[2,1,64,256]{3,2,1,0:T(8,128)(2,1)} %bitcast.18, ...), custom_call_target="tpu_custom_call" | custom-call | tf_op jit(solution)/shard_map/prepare/pallas_call | solution.py:374
  6.7 0.6 %collective-permute-done.refs_2_ = bf16[3,1,64,256]{3,2,1,0:T(8,128)(2,1)S(1)} collective-permute-done((bf16[3,1,64,256]{3,2,1,0:T(8,128)(2,1)S(1)}, bf16[3,1,64,256]{3,2,1,0:T(8,128)(2,1)S(1)}, u32[]{:S(2)}, u32[]{:S(2)}) %collective-permute-start) | collective-permute-done | bytes 98336 | tf_op jit(solution)/shard_map/ppermute | solution.py:29
  7.3 0.2 first_block.1
  7.5 1.9 %collective-permute-start.1 = (bf16[256,128]{1,0:T(8,128)(2,1)S(1)}, bf16[256,128]{1,0:T(8,128)(2,1)S(1)}, u32[]{:S(2)}, u32[]{:S(2)}) collective-permute-start(bf16[256,128]{1,0:T(8,128)(2,1)S(1)} %get-tuple-element.26), channel_id=1, source_target_pairs={{8,0},{0,8},{24,16},{16,24},{9,1},{1,9},{25,17},{17,25},{10,2},{2,... | collective-permute-start | bytes 196616 | tf_op jit(solution)/shard_map/ppermute | solution.py:452
  9.5 0.1 pack.1
  9.5 0.1 collective-permute-start.3
  9.6 1.6 %collective-permute-start.4 = (bf16[576,128]{1,0:T(8,128)(2,1)S(1)}, bf16[576,128]{1,0:T(8,128)(2,1)S(1)}, u32[]{:S(2)}, u32[]{:S(2)}) collective-permute-start(bf16[576,128]{1,0:T(8,128)(2,1)S(1)} %get-tuple-element.31), channel_id=1, source_target_pairs={{4,0},{5,1},{6,2},{7,3},{0,4},{1,5},{2,6},{3,7},{12,8},{13,9},{14,... | collective-permute-start | bytes 442376 | tf_op jit(solution)/shard_map/ppermute | solution.py:29
  11.2 0.3 collective-permute-start.5
  11.5 0.4 %collective-permute-done.1.grad_ref.refs_1_ = bf16[256,128]{1,0:T(8,128)(2,1)S(1)} collective-permute-done((bf16[256,128]{1,0:T(8,128)(2,1)S(1)}, bf16[256,128]{1,0:T(8,128)(2,1)S(1)}, u32[]{:S(2)}, u32[]{:S(2)}) %collective-permute-start.1) | collective-permute-done | bytes 65568 | tf_op jit(solution)/shard_map/ppermute | solution.py:452
  11.8 5.3 %collective-permute-start.2 = (bf16[256,128]{1,0:T(8,128)(2,1)S(1)}, bf16[256,128]{1,0:T(8,128)(2,1)S(1)}, u32[]{:S(2)}, u32[]{:S(2)}) collective-permute-start(bf16[256,128]{1,0:T(8,128)(2,1)S(1)} %block.2), channel_id=1, source_target_pairs={{8,0},{16,8},{24,16},{0,24},{9,1},{17,9},{25,17},{1,25},{10,2},{18... | collective-permute-start | bytes 196616 | tf_op jit(solution)/shard_map/ppermute | solution.py:452
  17.1 0.0 collective-permute-done.3.refs_1_.refs_2_.refs_3_
  17.1 0.0 collective-permute-done.4.refs_2_.refs_4_.refs_5_
  17.1 1.5 %collective-permute-done.5.refs_3_.refs_1_.refs_2_ = bf16[576,128]{1,0:T(8,128)(2,1)S(1)} collective-permute-done((bf16[576,128]{1,0:T(8,128)(2,1)S(1)}, bf16[576,128]{1,0:T(8,128)(2,1)S(1)}, u32[]{:S(2)}, u32[]{:S(2)}) %collective-permute-start.5) | collective-permute-done | bytes 147488 | tf_op jit(solution)/shard_map/ppermute | solution.py:29
  18.6 1.5 %collective-permute-start.9 = (bf16[256,128]{1,0:T(8,128)(2,1)S(1)}, bf16[256,128]{1,0:T(8,128)(2,1)S(1)}, u32[]{:S(2)}, u32[]{:S(2)}) collective-permute-start(bf16[256,128]{1,0:T(8,128)(2,1)S(1)} %collect.1.refs_0_), channel_id=1, source_target_pairs={{1,0},{0,1},{3,2},{2,3},{5,4},{4,5},{7,6},{6,7},{9,8},{8,9},{11,10... | collective-permute-start | bytes 196616 | tf_op jit(solution)/shard_map/ppermute | solution.py:29
  20.1 0.0 collective-permute-done.2.grad_ref.refs_2_
  20.1 2.3 %collective-permute-start.8 = (bf16[256,128]{1,0:T(8,128)(2,1)S(1)}, bf16[256,128]{1,0:T(8,128)(2,1)S(1)}, u32[]{:S(2)}, u32[]{:S(2)}) collective-permute-start(bf16[256,128]{1,0:T(8,128)(2,1)S(1)} %block.3.refs_3_), channel_id=1, source_target_pairs={{9,0},{8,1},{1,8},{0,9},{25,16},{24,17},{17,24},{16,25},{11,2},{10... | collective-permute-start | bytes 196616 | tf_op jit(solution)/shard_map/ppermute | solution.py:491
  22.4 0.0 collective-permute-start.7
  22.4 1.2 %collective-permute-start.6 = (bf16[256,128]{1,0:T(8,128)(2,1)S(1)}, bf16[256,128]{1,0:T(8,128)(2,1)S(1)}, u32[]{:S(2)}, u32[]{:S(2)}) collective-permute-start(bf16[256,128]{1,0:T(8,128)(2,1)S(1)} %early.1.refs_0_), channel_id=1, source_target_pairs={{1,0},{0,1},{3,2},{2,3},{5,4},{4,5},{7,6},{6,7},{9,8},{8,9},{11,10... | collective-permute-start | bytes 196616 | tf_op jit(solution)/shard_map/ppermute | solution.py:29
  23.6 0.0 collective-permute-done.9.refs_1_
  23.6 1.5 %unfold.1.refs_2_.refs_3_.refs_6_ = bf16[2,1728,512]{2,1,0:T(8,128)(2,1)S(1)} custom-call(bf16[256,128]{1,0:T(8,128)(2,1)S(1)} %collect.1.refs_0_, bf16[256,128]{1,0:T(8,128)(2,1)S(1)} %collective-permute-done.9.refs_1_), custom_call_target="tpu_custom_call" | custom-call | tf_op jit(solution)/shard_map/unfold/pallas_call | solution.py:374
  25.1 0.2 collective-permute-done.8.refs_1_
  25.4 1.3 %collective-permute-done.7.refs_0_ = bf16[256,128]{1,0:T(8,128)(2,1)S(1)} collective-permute-done((bf16[256,128]{1,0:T(8,128)(2,1)S(1)}, bf16[256,128]{1,0:T(8,128)(2,1)S(1)}, u32[]{:S(2)}, u32[]{:S(2)}) %collective-permute-start.7) | collective-permute-done | bytes 65568 | tf_op jit(solution)/shard_map/ppermute | solution.py:452
  26.7 0.0 collective-permute-done.6.refs_1_
  26.7 1.6 %collective-permute-start.10 = (bf16[512,128]{1,0:T(8,128)(2,1)S(1)}, bf16[512,128]{1,0:T(8,128)(2,1)S(1)}, u32[]{:S(2)}, u32[]{:S(2)}) collective-permute-start(bf16[512,128]{1,0:T(8,128)(2,1)S(1)} %choose.1.refs_0_.refs_1_), channel_id=1, source_target_pairs={{4,0},{5,1},{6,2},{7,3},{0,4},{1,5},{2,6},{3,7},{12,8},{13,9},{14,... | collective-permute-start | bytes 393224 | tf_op jit(solution)/shard_map/ppermute | solution.py:29
  28.3 2.2 %own_slab.1.refs_0_ = bf16[2,1,64,256]{3,2,1,0:T(8,128)(2,1)} custom-call(bf16[512,128]{1,0:T(8,128)(2,1)S(1)} %choose.1.refs_0_.refs_1_, bf16[512,128]{1,0:T(8,128)(2,1)S(1)} %choose.1.refs_0_.refs_1_, bf16[512,128]{1,0:T(8,128)(2,1)S(1)} %get-tuple-element.27.pre_ref.refs_2_, bf16[27,256,256]{2,1,0:T(8,128)(2,1)S(1)} %get-tuple-element.23.refs_3_.conv_ref, ...), custom_call_target="tpu_custom_call" | custom-call | tf_op jit(solution)/shard_map/own_slab/pallas_call | solution.py:374
  30.4 0.0 collective-permute-start.12
  30.5 0.7 %part_weight_grads.2 = (f32[1728,256]{1,0:T(8,128)S(1)}, f32[64,256]{1,0:T(8,128)S(1)}) custom-call(bf16[512,128]{1,0:T(8,128)(2,1)S(1)} %choose.1.refs_0_.refs_1_, bf16[576,128]{1,0:T(8,128)(2,1)S(1)} %get-tuple-element.29.refs_0_.refs_1_.refs_2_, bf16[576,128]{1,0:T(8,128)(2,1)S(1)} %get-tuple-element.29.refs_0_.refs_1_.refs_2_, ...), custom_call_target="tpu_custom_call" | custom-call | tf_op jit(solution)/shard_map/part_weight_grads/pallas_call | solution.py:374
  31.1 0.6 %collective-permute-done.10.block_ref = bf16[512,128]{1,0:T(8,128)(2,1)S(1)} collective-permute-done((bf16[512,128]{1,0:T(8,128)(2,1)S(1)}, bf16[512,128]{1,0:T(8,128)(2,1)S(1)}, u32[]{:S(2)}, u32[]{:S(2)}) %collective-permute-start.10) | collective-permute-done | bytes 131104 | tf_op jit(solution)/shard_map/ppermute | solution.py:29
  31.8 0.1 collective-permute-start.11
  31.8 0.0 collective-permute-done.12.refs_0_
  31.8 1.0 %part_weight_grads.3 = (f32[1728,256]{1,0:T(8,128)S(1)}, f32[64,256]{1,0:T(8,128)S(1)}) custom-call(bf16[512,128]{1,0:T(8,128)(2,1)S(1)} %collective-permute-done.12.refs_0_, bf16[512,128]{1,0:T(8,128)(2,1)S(1)} %hand_on.1.refs_1_, bf16[576,128]{1,0:T(8,128)(2,1)S(1)} %collective-permute-done.3.refs_1_.refs_2_.refs_3_, ...), custom_call_target="tpu_custom_call" | custom-call | tf_op jit(solution)/shard_map/part_weight_grads/pallas_call | solution.py:374
  32.8 0.3 collective-permute-done.11.refs_0_
  33.2 1.8 %weight_grads.1 = (f32[1728,256]{1,0:T(8,128)}, f32[64,256]{1,0:T(8,128)}) custom-call(bf16[512,128]{1,0:T(8,128)(2,1)S(1)} %collective-permute-done.11.refs_0_, bf16[576,128]{1,0:T(8,128)(2,1)S(1)} %collective-permute-done.5.refs_3_.refs_1_.refs_2_, bf16[576,128]{1,0:T(8,128)(2,1)S(1)} %collective-permute-done.5.refs_3_.refs_1_.refs_2_, ...), custom_call_target="tpu_custom_call" | custom-call | tf_op jit(solution)/shard_map/weight_grads/pallas_call | solution.py:374
  (7 shorter events, 0.0 us)
Async XLA Ops:
  1.5 5.8 %collective-permute-start = (bf16[3,1,64,256]{3,2,1,0:T(8,128)(2,1)S(1)}, bf16[3,1,64,256]{3,2,1,0:T(8,128)(2,1)S(1)}, u32[]{:S(2)}, u32[]{:S(2)}) collective-permute-start(bf16[3,1,64,256]{3,2,1,0:T(8,128)(2,1)S(1)} %outgoing.1), channel_id=1, source_target_pairs={{1,0},{0,1},{3,2},{2,3},{5,4},{4,5},{7,6},{6,7},{9,8},{8,9},{11,10... | collective-permute-start | bytes 294920 | tf_op jit(solution)/shard_map/ppermute | solution.py:29
  7.5 4.3 %collective-permute-start.1 = (bf16[256,128]{1,0:T(8,128)(2,1)S(1)}, bf16[256,128]{1,0:T(8,128)(2,1)S(1)}, u32[]{:S(2)}, u32[]{:S(2)}) collective-permute-start(bf16[256,128]{1,0:T(8,128)(2,1)S(1)} %get-tuple-element.26), channel_id=1, source_target_pairs={{8,0},{0,8},{24,16},{16,24},{9,1},{1,9},{25,17},{17,25},{10,2},{2,... | collective-permute-start | bytes 196616 | tf_op jit(solution)/shard_map/ppermute | solution.py:452
  9.5 7.6 %collective-permute-start.3 = (bf16[576,128]{1,0:T(8,128)(2,1)S(1)}, bf16[576,128]{1,0:T(8,128)(2,1)S(1)}, u32[]{:S(2)}, u32[]{:S(2)}) collective-permute-start(bf16[576,128]{1,0:T(8,128)(2,1)S(1)} %get-tuple-element.30), channel_id=1, source_target_pairs={{2,0},{3,1},{0,2},{1,3},{6,4},{7,5},{4,6},{5,7},{10,8},{11,9},{8,1... | collective-permute-start | bytes 442376 | tf_op jit(solution)/shard_map/ppermute | solution.py:29
  9.6 7.5 %collective-permute-start.4 = (bf16[576,128]{1,0:T(8,128)(2,1)S(1)}, bf16[576,128]{1,0:T(8,128)(2,1)S(1)}, u32[]{:S(2)}, u32[]{:S(2)}) collective-permute-start(bf16[576,128]{1,0:T(8,128)(2,1)S(1)} %get-tuple-element.31), channel_id=1, source_target_pairs={{4,0},{5,1},{6,2},{7,3},{0,4},{1,5},{2,6},{3,7},{12,8},{13,9},{14,... | collective-permute-start | bytes 442376 | tf_op jit(solution)/shard_map/ppermute | solution.py:29
  11.2 7.4 %collective-permute-start.5 = (bf16[576,128]{1,0:T(8,128)(2,1)S(1)}, bf16[576,128]{1,0:T(8,128)(2,1)S(1)}, u32[]{:S(2)}, u32[]{:S(2)}) collective-permute-start(bf16[576,128]{1,0:T(8,128)(2,1)S(1)} %get-tuple-element.32), channel_id=1, source_target_pairs={{6,0},{7,1},{4,2},{5,3},{2,4},{3,5},{0,6},{1,7},{14,8},{15,9},{12,... | collective-permute-start | bytes 442376 | tf_op jit(solution)/shard_map/ppermute | solution.py:29
  11.8 8.3 %collective-permute-start.2 = (bf16[256,128]{1,0:T(8,128)(2,1)S(1)}, bf16[256,128]{1,0:T(8,128)(2,1)S(1)}, u32[]{:S(2)}, u32[]{:S(2)}) collective-permute-start(bf16[256,128]{1,0:T(8,128)(2,1)S(1)} %block.2), channel_id=1, source_target_pairs={{8,0},{16,8},{24,16},{0,24},{9,1},{17,9},{25,17},{1,25},{10,2},{18... | collective-permute-start | bytes 196616 | tf_op jit(solution)/shard_map/ppermute | solution.py:452
  18.6 5.0 %collective-permute-start.9 = (bf16[256,128]{1,0:T(8,128)(2,1)S(1)}, bf16[256,128]{1,0:T(8,128)(2,1)S(1)}, u32[]{:S(2)}, u32[]{:S(2)}) collective-permute-start(bf16[256,128]{1,0:T(8,128)(2,1)S(1)} %collect.1.refs_0_), channel_id=1, source_target_pairs={{1,0},{0,1},{3,2},{2,3},{5,4},{4,5},{7,6},{6,7},{9,8},{8,9},{11,10... | collective-permute-start | bytes 196616 | tf_op jit(solution)/shard_map/ppermute | solution.py:29
  20.1 5.2 %collective-permute-start.8 = (bf16[256,128]{1,0:T(8,128)(2,1)S(1)}, bf16[256,128]{1,0:T(8,128)(2,1)S(1)}, u32[]{:S(2)}, u32[]{:S(2)}) collective-permute-start(bf16[256,128]{1,0:T(8,128)(2,1)S(1)} %block.3.refs_3_), channel_id=1, source_target_pairs={{9,0},{8,1},{1,8},{0,9},{25,16},{24,17},{17,24},{16,25},{11,2},{10... | collective-permute-start | bytes 196616 | tf_op jit(solution)/shard_map/ppermute | solution.py:491
  22.4 4.3 %collective-permute-start.7 = (bf16[256,128]{1,0:T(8,128)(2,1)S(1)}, bf16[256,128]{1,0:T(8,128)(2,1)S(1)}, u32[]{:S(2)}, u32[]{:S(2)}) collective-permute-start(bf16[256,128]{1,0:T(8,128)(2,1)S(1)} %block.3.refs_3_), channel_id=1, source_target_pairs={{8,0},{0,8},{24,16},{16,24},{9,1},{1,9},{25,17},{17,25},{10,2},{2,... | collective-permute-start | bytes 196616 | tf_op jit(solution)/shard_map/ppermute | solution.py:452
  22.4 4.3 %collective-permute-start.6 = (bf16[256,128]{1,0:T(8,128)(2,1)S(1)}, bf16[256,128]{1,0:T(8,128)(2,1)S(1)}, u32[]{:S(2)}, u32[]{:S(2)}) collective-permute-start(bf16[256,128]{1,0:T(8,128)(2,1)S(1)} %early.1.refs_0_), channel_id=1, source_target_pairs={{1,0},{0,1},{3,2},{2,3},{5,4},{4,5},{7,6},{6,7},{9,8},{8,9},{11,10... | collective-permute-start | bytes 196616 | tf_op jit(solution)/shard_map/ppermute | solution.py:29
  26.7 5.0 %collective-permute-start.10 = (bf16[512,128]{1,0:T(8,128)(2,1)S(1)}, bf16[512,128]{1,0:T(8,128)(2,1)S(1)}, u32[]{:S(2)}, u32[]{:S(2)}) collective-permute-start(bf16[512,128]{1,0:T(8,128)(2,1)S(1)} %choose.1.refs_0_.refs_1_), channel_id=1, source_target_pairs={{4,0},{5,1},{6,2},{7,3},{0,4},{1,5},{2,6},{3,7},{12,8},{13,9},{14,... | collective-permute-start | bytes 393224 | tf_op jit(solution)/shard_map/ppermute | solution.py:29
  30.4 1.4 %collective-permute-start.12 = (bf16[512,128]{1,0:T(8,128)(2,1)S(1)}, bf16[512,128]{1,0:T(8,128)(2,1)S(1)}, u32[]{:S(2)}, u32[]{:S(2)}) collective-permute-start(bf16[512,128]{1,0:T(8,128)(2,1)S(1)} %choose.1.refs_0_.refs_1_), channel_id=1, source_target_pairs={{2,0},{3,1},{0,2},{1,3},{6,4},{7,5},{4,6},{5,7},{10,8},{11,9},{8,1... | collective-permute-start | bytes 393224 | tf_op jit(solution)/shard_map/ppermute | solution.py:29
  31.8 1.4 %collective-permute-start.11 = (bf16[512,128]{1,0:T(8,128)(2,1)S(1)}, bf16[512,128]{1,0:T(8,128)(2,1)S(1)}, u32[]{:S(2)}, u32[]{:S(2)}) collective-permute-start(bf16[512,128]{1,0:T(8,128)(2,1)S(1)} %hand_on.1.refs_1_), channel_id=1, source_target_pairs={{2,0},{3,1},{0,2},{1,3},{6,4},{7,5},{4,6},{5,7},{10,8},{11,9},{8,1... | collective-permute-start | bytes 393224 | tf_op jit(solution)/shard_map/ppermute | solution.py:29

commit v9 on v8

--- a/solution.py
+++ b/solution.py
@@ -526,7 +526,7 @@
 
     conv_shape = jax.ShapeDtypeStruct((taps * shard, channels), jnp.float32)
     proj_shape = jax.ShapeDtypeStruct((shard, channels), jnp.float32)
-    cuts = len(SIDE) if (taps // len(SIDE) * shard) % 16 == 0 else 1
+    cuts = len(SIDE) ** 2 if (taps // len(SIDE) ** 2 * shard) % 16 == 0 else 1
 
     def weight_sums(arrays, blocks, columns, before, final):
         plan = (len(arrays), blocks, columns)

time: 35.1 us -> 35.1 us (level)
  no operation moved by 1% of the time
where the time goes in v9:
time: 35.1 us; the launch traced here: 34.9 us
  starting transfers between devices  18.8 us (54%)
  Pallas kernels  10.4 us (30%)
  waiting for transfers between devices  5.01 us (14%)
  between operations  0.72 us (2%)
    pallas_call x16, Pallas kernels, kernel_call(): pl.pallas_call(body, out_shape=outs if single else tuple(outs), in_specs=...  10.4 us
    ppermute x9, starting transfers between devices, moved(): return lax.ppermute(block, ('dp', 'space'), pairs)  9.32 us
    ppermute x3, starting transfers between devices, shards(): lax.ppermute(results[-1], 'section', hop_pairs(section_count, step))  7.21 us
    ppermute x9, waiting for transfers between devices, moved(): return lax.ppermute(block, ('dp', 'space'), pairs)  3.14 us
    ppermute x1, starting transfers between devices, shards(): lax.ppermute(results[-1], ('section', 'space'), [(source * slabs + peer(i...  2.28 us
    ppermute x3, waiting for transfers between devices, shards(): lax.ppermute(results[-1], 'section', hop_pairs(section_count, step))  1.67 us
  transfers between devices with their start and end apart: 13, of which 7 were waited for; matrix products, arithmetic and copies ran while one was open for 0% of the time, Pallas kernels for 22%

profile of v9, /device:TPU:0, one launch (start us, length us, event | category | flops | bytes accessed | tf_op | source)
XLA Modules:
  0.0 34.9 jit_solution(40000684990124503)
XLA Ops:
  0.6 0.9 %outgoing.1 = bf16[3,1,64,256]{3,2,1,0:T(8,128)(2,1)S(1)} custom-call(bf16[2,1,64,256]{3,2,1,0:T(8,128)(2,1)} %bitcast.15, bf16[2,1,64,256]{3,2,1,0:T(8,128)(2,1)} %bitcast.17), custom_call_target="tpu_custom_call" | custom-call | tf_op jit(solution)/shard_map/outgoing/pallas_call | solution.py:374
  1.5 3.0 %collective-permute-start = (bf16[3,1,64,256]{3,2,1,0:T(8,128)(2,1)S(1)}, bf16[3,1,64,256]{3,2,1,0:T(8,128)(2,1)S(1)}, u32[]{:S(2)}, u32[]{:S(2)}) collective-permute-start(bf16[3,1,64,256]{3,2,1,0:T(8,128)(2,1)S(1)} %outgoing.1), channel_id=1, source_target_pairs={{1,0},{0,1},{3,2},{2,3},{5,4},{4,5},{7,6},{6,7},{9,8},{8,9},{11,10... | collective-permute-start | bytes 294920 | tf_op jit(solution)/shard_map/ppermute | solution.py:29
  4.6 2.1 %prepare.1 = (bf16[1,1,64,256]{3,2,1,0:T(8,128)(2,1)S(1)}, bf16[2,1,64,256]{3,2,1,0:T(8,128)(2,1)S(1)}, bf16[256,128]{1,0:T(8,128)(2,1)S(1)}, bf16[27,256,256]{2,1,0:T(8,128)(2,1)S(1)}, bf16[256,256]{1,0:T(8,128)(2,1)S(1)}) custom-call(bf16[2,1,64,256]{3,2,1,0:T(8,128)(2,1)} %bitcast.16, bf16[2,1,64,256]{3,2,1,0:T(8,128)(2,1)} %bitcast.18, ...), custom_call_target="tpu_custom_call" | custom-call | tf_op jit(solution)/shard_map/prepare/pallas_call | solution.py:374
  6.7 0.6 %collective-permute-done.refs_2_ = bf16[3,1,64,256]{3,2,1,0:T(8,128)(2,1)S(1)} collective-permute-done((bf16[3,1,64,256]{3,2,1,0:T(8,128)(2,1)S(1)}, bf16[3,1,64,256]{3,2,1,0:T(8,128)(2,1)S(1)}, u32[]{:S(2)}, u32[]{:S(2)}) %collective-permute-start) | collective-permute-done | bytes 98336 | tf_op jit(solution)/shard_map/ppermute | solution.py:29
  7.3 0.2 first_block.1
  7.5 1.9 %collective-permute-start.1 = (bf16[256,128]{1,0:T(8,128)(2,1)S(1)}, bf16[256,128]{1,0:T(8,128)(2,1)S(1)}, u32[]{:S(2)}, u32[]{:S(2)}) collective-permute-start(bf16[256,128]{1,0:T(8,128)(2,1)S(1)} %get-tuple-element.26), channel_id=1, source_target_pairs={{8,0},{0,8},{24,16},{16,24},{9,1},{1,9},{25,17},{17,25},{10,2},{2,... | collective-permute-start | bytes 196616 | tf_op jit(solution)/shard_map/ppermute | solution.py:452
  9.5 0.1 pack.1
  9.5 0.1 collective-permute-start.3
  9.6 1.6 %collective-permute-start.4 = (bf16[576,128]{1,0:T(8,128)(2,1)S(1)}, bf16[576,128]{1,0:T(8,128)(2,1)S(1)}, u32[]{:S(2)}, u32[]{:S(2)}) collective-permute-start(bf16[576,128]{1,0:T(8,128)(2,1)S(1)} %get-tuple-element.31), channel_id=1, source_target_pairs={{4,0},{5,1},{6,2},{7,3},{0,4},{1,5},{2,6},{3,7},{12,8},{13,9},{14,... | collective-permute-start | bytes 442376 | tf_op jit(solution)/shard_map/ppermute | solution.py:29
  11.2 0.3 collective-permute-start.5
  11.5 0.4 %collective-permute-done.1.grad_ref.refs_1_ = bf16[256,128]{1,0:T(8,128)(2,1)S(1)} collective-permute-done((bf16[256,128]{1,0:T(8,128)(2,1)S(1)}, bf16[256,128]{1,0:T(8,128)(2,1)S(1)}, u32[]{:S(2)}, u32[]{:S(2)}) %collective-permute-start.1) | collective-permute-done | bytes 65568 | tf_op jit(solution)/shard_map/ppermute | solution.py:452
  11.8 5.3 %collective-permute-start.2 = (bf16[256,128]{1,0:T(8,128)(2,1)S(1)}, bf16[256,128]{1,0:T(8,128)(2,1)S(1)}, u32[]{:S(2)}, u32[]{:S(2)}) collective-permute-start(bf16[256,128]{1,0:T(8,128)(2,1)S(1)} %block.2), channel_id=1, source_target_pairs={{8,0},{16,8},{24,16},{0,24},{9,1},{17,9},{25,17},{1,25},{10,2},{18... | collective-permute-start | bytes 196616 | tf_op jit(solution)/shard_map/ppermute | solution.py:452
  17.1 0.0 collective-permute-done.3.refs_1_.refs_2_.refs_3_
  17.1 0.0 collective-permute-done.4.refs_2_.refs_4_.refs_5_
  17.1 1.5 %collective-permute-done.5.refs_3_.refs_1_.refs_2_ = bf16[576,128]{1,0:T(8,128)(2,1)S(1)} collective-permute-done((bf16[576,128]{1,0:T(8,128)(2,1)S(1)}, bf16[576,128]{1,0:T(8,128)(2,1)S(1)}, u32[]{:S(2)}, u32[]{:S(2)}) %collective-permute-start.5) | collective-permute-done | bytes 147488 | tf_op jit(solution)/shard_map/ppermute | solution.py:29
  18.6 1.5 %collective-permute-start.9 = (bf16[256,128]{1,0:T(8,128)(2,1)S(1)}, bf16[256,128]{1,0:T(8,128)(2,1)S(1)}, u32[]{:S(2)}, u32[]{:S(2)}) collective-permute-start(bf16[256,128]{1,0:T(8,128)(2,1)S(1)} %collect.1.refs_0_), channel_id=1, source_target_pairs={{1,0},{0,1},{3,2},{2,3},{5,4},{4,5},{7,6},{6,7},{9,8},{8,9},{11,10... | collective-permute-start | bytes 196616 | tf_op jit(solution)/shard_map/ppermute | solution.py:29
  20.1 0.0 collective-permute-done.2.grad_ref.refs_2_
  20.1 2.3 %collective-permute-start.8 = (bf16[256,128]{1,0:T(8,128)(2,1)S(1)}, bf16[256,128]{1,0:T(8,128)(2,1)S(1)}, u32[]{:S(2)}, u32[]{:S(2)}) collective-permute-start(bf16[256,128]{1,0:T(8,128)(2,1)S(1)} %block.3.refs_3_), channel_id=1, source_target_pairs={{9,0},{8,1},{1,8},{0,9},{25,16},{24,17},{17,24},{16,25},{11,2},{10... | collective-permute-start | bytes 196616 | tf_op jit(solution)/shard_map/ppermute | solution.py:491
  22.4 0.0 collective-permute-start.7
  22.4 1.2 %collective-permute-start.6 = (bf16[256,128]{1,0:T(8,128)(2,1)S(1)}, bf16[256,128]{1,0:T(8,128)(2,1)S(1)}, u32[]{:S(2)}, u32[]{:S(2)}) collective-permute-start(bf16[256,128]{1,0:T(8,128)(2,1)S(1)} %early.1.refs_0_), channel_id=1, source_target_pairs={{1,0},{0,1},{3,2},{2,3},{5,4},{4,5},{7,6},{6,7},{9,8},{8,9},{11,10... | collective-permute-start | bytes 196616 | tf_op jit(solution)/shard_map/ppermute | solution.py:29
  23.6 0.0 collective-permute-done.9.refs_1_
  23.6 1.5 %unfold.1.refs_2_.refs_3_.refs_6_ = bf16[2,1728,512]{2,1,0:T(8,128)(2,1)S(1)} custom-call(bf16[256,128]{1,0:T(8,128)(2,1)S(1)} %collect.1.refs_0_, bf16[256,128]{1,0:T(8,128)(2,1)S(1)} %collective-permute-done.9.refs_1_), custom_call_target="tpu_custom_call" | custom-call | tf_op jit(solution)/shard_map/unfold/pallas_call | solution.py:374
  25.1 0.2 collective-permute-done.8.refs_1_
  25.4 1.3 %collective-permute-done.7.refs_0_ = bf16[256,128]{1,0:T(8,128)(2,1)S(1)} collective-permute-done((bf16[256,128]{1,0:T(8,128)(2,1)S(1)}, bf16[256,128]{1,0:T(8,128)(2,1)S(1)}, u32[]{:S(2)}, u32[]{:S(2)}) %collective-permute-start.7) | collective-permute-done | bytes 65568 | tf_op jit(solution)/shard_map/ppermute | solution.py:452
  26.7 0.0 collective-permute-done.6.refs_1_
  26.7 1.6 %collective-permute-start.10 = (bf16[512,128]{1,0:T(8,128)(2,1)S(1)}, bf16[512,128]{1,0:T(8,128)(2,1)S(1)}, u32[]{:S(2)}, u32[]{:S(2)}) collective-permute-start(bf16[512,128]{1,0:T(8,128)(2,1)S(1)} %choose.1.refs_0_.refs_1_), channel_id=1, source_target_pairs={{4,0},{5,1},{6,2},{7,3},{0,4},{1,5},{2,6},{3,7},{12,8},{13,9},{14,... | collective-permute-start | bytes 393224 | tf_op jit(solution)/shard_map/ppermute | solution.py:29
  28.3 2.2 %own_slab.1.refs_0_ = bf16[2,1,64,256]{3,2,1,0:T(8,128)(2,1)} custom-call(bf16[512,128]{1,0:T(8,128)(2,1)S(1)} %choose.1.refs_0_.refs_1_, bf16[512,128]{1,0:T(8,128)(2,1)S(1)} %choose.1.refs_0_.refs_1_, bf16[512,128]{1,0:T(8,128)(2,1)S(1)} %get-tuple-element.27.pre_ref.refs_2_, bf16[27,256,256]{2,1,0:T(8,128)(2,1)S(1)} %get-tuple-element.23.refs_3_.conv_ref, ...), custom_call_target="tpu_custom_call" | custom-call | tf_op jit(solution)/shard_map/own_slab/pallas_call | solution.py:374
  30.4 0.0 collective-permute-start.12
  30.5 0.7 %part_weight_grads.2 = (f32[1728,256]{1,0:T(8,128)S(1)}, f32[64,256]{1,0:T(8,128)S(1)}) custom-call(bf16[512,128]{1,0:T(8,128)(2,1)S(1)} %choose.1.refs_0_.refs_1_, bf16[576,128]{1,0:T(8,128)(2,1)S(1)} %get-tuple-element.29.refs_0_.refs_1_.refs_2_, bf16[576,128]{1,0:T(8,128)(2,1)S(1)} %get-tuple-element.29.refs_0_.refs_1_.refs_2_, ...), custom_call_target="tpu_custom_call" | custom-call | tf_op jit(solution)/shard_map/part_weight_grads/pallas_call | solution.py:374
  31.1 0.6 %collective-permute-done.10.block_ref = bf16[512,128]{1,0:T(8,128)(2,1)S(1)} collective-permute-done((bf16[512,128]{1,0:T(8,128)(2,1)S(1)}, bf16[512,128]{1,0:T(8,128)(2,1)S(1)}, u32[]{:S(2)}, u32[]{:S(2)}) %collective-permute-start.10) | collective-permute-done | bytes 131104 | tf_op jit(solution)/shard_map/ppermute | solution.py:29
  31.8 0.1 collective-permute-start.11
  31.8 0.0 collective-permute-done.12.refs_0_
  31.8 1.0 %part_weight_grads.3 = (f32[1728,256]{1,0:T(8,128)S(1)}, f32[64,256]{1,0:T(8,128)S(1)}) custom-call(bf16[512,128]{1,0:T(8,128)(2,1)S(1)} %collective-permute-done.12.refs_0_, bf16[512,128]{1,0:T(8,128)(2,1)S(1)} %hand_on.1.refs_1_, bf16[576,128]{1,0:T(8,128)(2,1)S(1)} %collective-permute-done.3.refs_1_.refs_2_.refs_3_, ...), custom_call_target="tpu_custom_call" | custom-call | tf_op jit(solution)/shard_map/part_weight_grads/pallas_call | solution.py:374
  32.8 0.3 collective-permute-done.11.refs_0_
  33.2 1.8 %weight_grads.1 = (f32[1728,256]{1,0:T(8,128)}, f32[64,256]{1,0:T(8,128)}) custom-call(bf16[512,128]{1,0:T(8,128)(2,1)S(1)} %collective-permute-done.11.refs_0_, bf16[576,128]{1,0:T(8,128)(2,1)S(1)} %collective-permute-done.5.refs_3_.refs_1_.refs_2_, bf16[576,128]{1,0:T(8,128)(2,1)S(1)} %collective-permute-done.5.refs_3_.refs_1_.refs_2_, ...), custom_call_target="tpu_custom_call" | custom-call | tf_op jit(solution)/shard_map/weight_grads/pallas_call | solution.py:374
  (7 shorter events, 0.0 us)
Async XLA Ops:
  1.5 5.8 %collective-permute-start = (bf16[3,1,64,256]{3,2,1,0:T(8,128)(2,1)S(1)}, bf16[3,1,64,256]{3,2,1,0:T(8,128)(2,1)S(1)}, u32[]{:S(2)}, u32[]{:S(2)}) collective-permute-start(bf16[3,1,64,256]{3,2,1,0:T(8,128)(2,1)S(1)} %outgoing.1), channel_id=1, source_target_pairs={{1,0},{0,1},{3,2},{2,3},{5,4},{4,5},{7,6},{6,7},{9,8},{8,9},{11,10... | collective-permute-start | bytes 294920 | tf_op jit(solution)/shard_map/ppermute | solution.py:29
  7.5 4.3 %collective-permute-start.1 = (bf16[256,128]{1,0:T(8,128)(2,1)S(1)}, bf16[256,128]{1,0:T(8,128)(2,1)S(1)}, u32[]{:S(2)}, u32[]{:S(2)}) collective-permute-start(bf16[256,128]{1,0:T(8,128)(2,1)S(1)} %get-tuple-element.26), channel_id=1, source_target_pairs={{8,0},{0,8},{24,16},{16,24},{9,1},{1,9},{25,17},{17,25},{10,2},{2,... | collective-permute-start | bytes 196616 | tf_op jit(solution)/shard_map/ppermute | solution.py:452
  9.5 7.6 %collective-permute-start.3 = (bf16[576,128]{1,0:T(8,128)(2,1)S(1)}, bf16[576,128]{1,0:T(8,128)(2,1)S(1)}, u32[]{:S(2)}, u32[]{:S(2)}) collective-permute-start(bf16[576,128]{1,0:T(8,128)(2,1)S(1)} %get-tuple-element.30), channel_id=1, source_target_pairs={{2,0},{3,1},{0,2},{1,3},{6,4},{7,5},{4,6},{5,7},{10,8},{11,9},{8,1... | collective-permute-start | bytes 442376 | tf_op jit(solution)/shard_map/ppermute | solution.py:29
  9.6 7.5 %collective-permute-start.4 = (bf16[576,128]{1,0:T(8,128)(2,1)S(1)}, bf16[576,128]{1,0:T(8,128)(2,1)S(1)}, u32[]{:S(2)}, u32[]{:S(2)}) collective-permute-start(bf16[576,128]{1,0:T(8,128)(2,1)S(1)} %get-tuple-element.31), channel_id=1, source_target_pairs={{4,0},{5,1},{6,2},{7,3},{0,4},{1,5},{2,6},{3,7},{12,8},{13,9},{14,... | collective-permute-start | bytes 442376 | tf_op jit(solution)/shard_map/ppermute | solution.py:29
  11.2 7.4 %collective-permute-start.5 = (bf16[576,128]{1,0:T(8,128)(2,1)S(1)}, bf16[576,128]{1,0:T(8,128)(2,1)S(1)}, u32[]{:S(2)}, u32[]{:S(2)}) collective-permute-start(bf16[576,128]{1,0:T(8,128)(2,1)S(1)} %get-tuple-element.32), channel_id=1, source_target_pairs={{6,0},{7,1},{4,2},{5,3},{2,4},{3,5},{0,6},{1,7},{14,8},{15,9},{12,... | collective-permute-start | bytes 442376 | tf_op jit(solution)/shard_map/ppermute | solution.py:29
  11.8 8.3 %collective-permute-start.2 = (bf16[256,128]{1,0:T(8,128)(2,1)S(1)}, bf16[256,128]{1,0:T(8,128)(2,1)S(1)}, u32[]{:S(2)}, u32[]{:S(2)}) collective-permute-start(bf16[256,128]{1,0:T(8,128)(2,1)S(1)} %block.2), channel_id=1, source_target_pairs={{8,0},{16,8},{24,16},{0,24},{9,1},{17,9},{25,17},{1,25},{10,2},{18... | collective-permute-start | bytes 196616 | tf_op jit(solution)/shard_map/ppermute | solution.py:452
  18.6 5.0 %collective-permute-start.9 = (bf16[256,128]{1,0:T(8,128)(2,1)S(1)}, bf16[256,128]{1,0:T(8,128)(2,1)S(1)}, u32[]{:S(2)}, u32[]{:S(2)}) collective-permute-start(bf16[256,128]{1,0:T(8,128)(2,1)S(1)} %collect.1.refs_0_), channel_id=1, source_target_pairs={{1,0},{0,1},{3,2},{2,3},{5,4},{4,5},{7,6},{6,7},{9,8},{8,9},{11,10... | collective-permute-start | bytes 196616 | tf_op jit(solution)/shard_map/ppermute | solution.py:29
  20.1 5.2 %collective-permute-start.8 = (bf16[256,128]{1,0:T(8,128)(2,1)S(1)}, bf16[256,128]{1,0:T(8,128)(2,1)S(1)}, u32[]{:S(2)}, u32[]{:S(2)}) collective-permute-start(bf16[256,128]{1,0:T(8,128)(2,1)S(1)} %block.3.refs_3_), channel_id=1, source_target_pairs={{9,0},{8,1},{1,8},{0,9},{25,16},{24,17},{17,24},{16,25},{11,2},{10... | collective-permute-start | bytes 196616 | tf_op jit(solution)/shard_map/ppermute | solution.py:491
  22.4 4.3 %collective-permute-start.7 = (bf16[256,128]{1,0:T(8,128)(2,1)S(1)}, bf16[256,128]{1,0:T(8,128)(2,1)S(1)}, u32[]{:S(2)}, u32[]{:S(2)}) collective-permute-start(bf16[256,128]{1,0:T(8,128)(2,1)S(1)} %block.3.refs_3_), channel_id=1, source_target_pairs={{8,0},{0,8},{24,16},{16,24},{9,1},{1,9},{25,17},{17,25},{10,2},{2,... | collective-permute-start | bytes 196616 | tf_op jit(solution)/shard_map/ppermute | solution.py:452
  22.4 4.3 %collective-permute-start.6 = (bf16[256,128]{1,0:T(8,128)(2,1)S(1)}, bf16[256,128]{1,0:T(8,128)(2,1)S(1)}, u32[]{:S(2)}, u32[]{:S(2)}) collective-permute-start(bf16[256,128]{1,0:T(8,128)(2,1)S(1)} %early.1.refs_0_), channel_id=1, source_target_pairs={{1,0},{0,1},{3,2},{2,3},{5,4},{4,5},{7,6},{6,7},{9,8},{8,9},{11,10... | collective-permute-start | bytes 196616 | tf_op jit(solution)/shard_map/ppermute | solution.py:29
  26.7 5.0 %collective-permute-start.10 = (bf16[512,128]{1,0:T(8,128)(2,1)S(1)}, bf16[512,128]{1,0:T(8,128)(2,1)S(1)}, u32[]{:S(2)}, u32[]{:S(2)}) collective-permute-start(bf16[512,128]{1,0:T(8,128)(2,1)S(1)} %choose.1.refs_0_.refs_1_), channel_id=1, source_target_pairs={{4,0},{5,1},{6,2},{7,3},{0,4},{1,5},{2,6},{3,7},{12,8},{13,9},{14,... | collective-permute-start | bytes 393224 | tf_op jit(solution)/shard_map/ppermute | solution.py:29
  30.4 1.4 %collective-permute-start.12 = (bf16[512,128]{1,0:T(8,128)(2,1)S(1)}, bf16[512,128]{1,0:T(8,128)(2,1)S(1)}, u32[]{:S(2)}, u32[]{:S(2)}) collective-permute-start(bf16[512,128]{1,0:T(8,128)(2,1)S(1)} %choose.1.refs_0_.refs_1_), channel_id=1, source_target_pairs={{2,0},{3,1},{0,2},{1,3},{6,4},{7,5},{4,6},{5,7},{10,8},{11,9},{8,1... | collective-permute-start | bytes 393224 | tf_op jit(solution)/shard_map/ppermute | solution.py:29
  31.8 1.4 %collective-permute-start.11 = (bf16[512,128]{1,0:T(8,128)(2,1)S(1)}, bf16[512,128]{1,0:T(8,128)(2,1)S(1)}, u32[]{:S(2)}, u32[]{:S(2)}) collective-permute-start(bf16[512,128]{1,0:T(8,128)(2,1)S(1)} %hand_on.1.refs_1_), channel_id=1, source_target_pairs={{2,0},{3,1},{0,2},{1,3},{6,4},{7,5},{4,6},{5,7},{10,8},{11,9},{8,1... | collective-permute-start | bytes 393224 | tf_op jit(solution)/shard_map/ppermute | solution.py:29

commit v10 on v8

--- a/solution.py
+++ b/solution.py
@@ -47,11 +47,12 @@
         depth_off, row_off, col_off = (sign * off for off in tap)
         amount = -((depth_off * height + row_off) * width + col_off) % lanes
         if amount not in rolled:
-            rolled[amount] = pltpu.roll(block, amount, 1) if amount else block
+            moved_block = pltpu.roll(block, amount, 1) if amount else block
+            rolled[amount] = moved_block.astype(jnp.bfloat16)
         inside = (depth + depth_off >= 0) & (depth + depth_off < depth_all)
         inside &= (row + row_off >= 0) & (row + row_off < height)
         inside &= (col + col_off >= 0) & (col + col_off < width)
-        yield jnp.where(inside, rolled[amount], 0.0).astype(jnp.bfloat16)
+        yield jnp.where(inside, rolled[amount], jnp.zeros((), jnp.bfloat16))
 
 
 def pre_cotangent(grad, pre, proj):

time: 35.1 us -> 35.1 us (level)
  no operation moved by 1% of the time
where the time goes in v10:
time: 35.1 us; the launch traced here: 35 us
  starting transfers between devices  18.8 us (54%)
  Pallas kernels  10.4 us (30%)
  waiting for transfers between devices  5.05 us (14%)
  between operations  0.72 us (2%)
    pallas_call x16, Pallas kernels, kernel_call(): pl.pallas_call(body, out_shape=outs if single else tuple(outs), in_specs=...  10.4 us
    ppermute x9, starting transfers between devices, moved(): return lax.ppermute(block, ('dp', 'space'), pairs)  9.32 us
    ppermute x3, starting transfers between devices, shards(): lax.ppermute(results[-1], 'section', hop_pairs(section_count, step))  7.21 us
    ppermute x9, waiting for transfers between devices, moved(): return lax.ppermute(block, ('dp', 'space'), pairs)  3.14 us
    ppermute x1, starting transfers between devices, shards(): lax.ppermute(results[-1], ('section', 'space'), [(source * slabs + peer(i...  2.28 us
    ppermute x3, waiting for transfers between devices, shards(): lax.ppermute(results[-1], 'section', hop_pairs(section_count, step))  1.67 us
  transfers between devices with their start and end apart: 13, of which 7 were waited for; matrix products, arithmetic and copies ran while one was open for 0% of the time, Pallas kernels for 22%

profile of v10, /device:TPU:0, one launch (start us, length us, event | category | flops | bytes accessed | tf_op | source)
XLA Modules:
  0.0 35.0 jit_solution(8945230906825209159)
XLA Ops:
  0.6 0.9 %outgoing.1 = bf16[3,1,64,256]{3,2,1,0:T(8,128)(2,1)S(1)} custom-call(bf16[2,1,64,256]{3,2,1,0:T(8,128)(2,1)} %bitcast.15, bf16[2,1,64,256]{3,2,1,0:T(8,128)(2,1)} %bitcast.17), custom_call_target="tpu_custom_call" | custom-call | tf_op jit(solution)/shard_map/outgoing/pallas_call | solution.py:375
  1.5 3.0 %collective-permute-start = (bf16[3,1,64,256]{3,2,1,0:T(8,128)(2,1)S(1)}, bf16[3,1,64,256]{3,2,1,0:T(8,128)(2,1)S(1)}, u32[]{:S(2)}, u32[]{:S(2)}) collective-permute-start(bf16[3,1,64,256]{3,2,1,0:T(8,128)(2,1)S(1)} %outgoing.1), channel_id=1, source_target_pairs={{1,0},{0,1},{3,2},{2,3},{5,4},{4,5},{7,6},{6,7},{9,8},{8,9},{11,10... | collective-permute-start | bytes 294920 | tf_op jit(solution)/shard_map/ppermute | solution.py:29
  4.6 2.1 %prepare.1 = (bf16[1,1,64,256]{3,2,1,0:T(8,128)(2,1)S(1)}, bf16[2,1,64,256]{3,2,1,0:T(8,128)(2,1)S(1)}, bf16[256,128]{1,0:T(8,128)(2,1)S(1)}, bf16[27,256,256]{2,1,0:T(8,128)(2,1)S(1)}, bf16[256,256]{1,0:T(8,128)(2,1)S(1)}) custom-call(bf16[2,1,64,256]{3,2,1,0:T(8,128)(2,1)} %bitcast.16, bf16[2,1,64,256]{3,2,1,0:T(8,128)(2,1)} %bitcast.18, ...), custom_call_target="tpu_custom_call" | custom-call | tf_op jit(solution)/shard_map/prepare/pallas_call | solution.py:375
  6.7 0.6 %collective-permute-done.refs_2_ = bf16[3,1,64,256]{3,2,1,0:T(8,128)(2,1)S(1)} collective-permute-done((bf16[3,1,64,256]{3,2,1,0:T(8,128)(2,1)S(1)}, bf16[3,1,64,256]{3,2,1,0:T(8,128)(2,1)S(1)}, u32[]{:S(2)}, u32[]{:S(2)}) %collective-permute-start) | collective-permute-done | bytes 98336 | tf_op jit(solution)/shard_map/ppermute | solution.py:29
  7.3 0.2 first_block.1
  7.5 1.9 %collective-permute-start.1 = (bf16[256,128]{1,0:T(8,128)(2,1)S(1)}, bf16[256,128]{1,0:T(8,128)(2,1)S(1)}, u32[]{:S(2)}, u32[]{:S(2)}) collective-permute-start(bf16[256,128]{1,0:T(8,128)(2,1)S(1)} %get-tuple-element.26), channel_id=1, source_target_pairs={{8,0},{0,8},{24,16},{16,24},{9,1},{1,9},{25,17},{17,25},{10,2},{2,... | collective-permute-start | bytes 196616 | tf_op jit(solution)/shard_map/ppermute | solution.py:453
  9.5 0.1 pack.1
  9.5 0.1 collective-permute-start.3
  9.6 1.6 %collective-permute-start.4 = (bf16[576,128]{1,0:T(8,128)(2,1)S(1)}, bf16[576,128]{1,0:T(8,128)(2,1)S(1)}, u32[]{:S(2)}, u32[]{:S(2)}) collective-permute-start(bf16[576,128]{1,0:T(8,128)(2,1)S(1)} %get-tuple-element.31), channel_id=1, source_target_pairs={{4,0},{5,1},{6,2},{7,3},{0,4},{1,5},{2,6},{3,7},{12,8},{13,9},{14,... | collective-permute-start | bytes 442376 | tf_op jit(solution)/shard_map/ppermute | solution.py:29
  11.2 0.3 collective-permute-start.5
  11.5 0.4 %collective-permute-done.1.grad_ref.refs_1_ = bf16[256,128]{1,0:T(8,128)(2,1)S(1)} collective-permute-done((bf16[256,128]{1,0:T(8,128)(2,1)S(1)}, bf16[256,128]{1,0:T(8,128)(2,1)S(1)}, u32[]{:S(2)}, u32[]{:S(2)}) %collective-permute-start.1) | collective-permute-done | bytes 65568 | tf_op jit(solution)/shard_map/ppermute | solution.py:453
  11.8 5.3 %collective-permute-start.2 = (bf16[256,128]{1,0:T(8,128)(2,1)S(1)}, bf16[256,128]{1,0:T(8,128)(2,1)S(1)}, u32[]{:S(2)}, u32[]{:S(2)}) collective-permute-start(bf16[256,128]{1,0:T(8,128)(2,1)S(1)} %block.2), channel_id=1, source_target_pairs={{8,0},{16,8},{24,16},{0,24},{9,1},{17,9},{25,17},{1,25},{10,2},{18... | collective-permute-start | bytes 196616 | tf_op jit(solution)/shard_map/ppermute | solution.py:453
  17.1 0.0 collective-permute-done.3.refs_1_.refs_2_.refs_3_
  17.1 0.0 collective-permute-done.4.refs_2_.refs_4_.refs_5_
  17.1 1.5 %collective-permute-done.5.refs_3_.refs_1_.refs_2_ = bf16[576,128]{1,0:T(8,128)(2,1)S(1)} collective-permute-done((bf16[576,128]{1,0:T(8,128)(2,1)S(1)}, bf16[576,128]{1,0:T(8,128)(2,1)S(1)}, u32[]{:S(2)}, u32[]{:S(2)}) %collective-permute-start.5) | collective-permute-done | bytes 147488 | tf_op jit(solution)/shard_map/ppermute | solution.py:29
  18.6 1.5 %collective-permute-start.9 = (bf16[256,128]{1,0:T(8,128)(2,1)S(1)}, bf16[256,128]{1,0:T(8,128)(2,1)S(1)}, u32[]{:S(2)}, u32[]{:S(2)}) collective-permute-start(bf16[256,128]{1,0:T(8,128)(2,1)S(1)} %collect.1.refs_0_), channel_id=1, source_target_pairs={{1,0},{0,1},{3,2},{2,3},{5,4},{4,5},{7,6},{6,7},{9,8},{8,9},{11,10... | collective-permute-start | bytes 196616 | tf_op jit(solution)/shard_map/ppermute | solution.py:29
  20.1 0.0 collective-permute-done.2.grad_ref.refs_2_
  20.1 2.3 %collective-permute-start.8 = (bf16[256,128]{1,0:T(8,128)(2,1)S(1)}, bf16[256,128]{1,0:T(8,128)(2,1)S(1)}, u32[]{:S(2)}, u32[]{:S(2)}) collective-permute-start(bf16[256,128]{1,0:T(8,128)(2,1)S(1)} %block.3.refs_3_), channel_id=1, source_target_pairs={{9,0},{8,1},{1,8},{0,9},{25,16},{24,17},{17,24},{16,25},{11,2},{10... | collective-permute-start | bytes 196616 | tf_op jit(solution)/shard_map/ppermute | solution.py:492
  22.4 0.0 collective-permute-start.7
  22.4 1.2 %collective-permute-start.6 = (bf16[256,128]{1,0:T(8,128)(2,1)S(1)}, bf16[256,128]{1,0:T(8,128)(2,1)S(1)}, u32[]{:S(2)}, u32[]{:S(2)}) collective-permute-start(bf16[256,128]{1,0:T(8,128)(2,1)S(1)} %early.1.refs_0_), channel_id=1, source_target_pairs={{1,0},{0,1},{3,2},{2,3},{5,4},{4,5},{7,6},{6,7},{9,8},{8,9},{11,10... | collective-permute-start | bytes 196616 | tf_op jit(solution)/shard_map/ppermute | solution.py:29
  23.6 0.0 collective-permute-done.9.refs_1_
  23.6 1.5 %unfold.1.refs_2_.refs_3_.refs_6_ = bf16[2,1728,512]{2,1,0:T(8,128)(2,1)S(1)} custom-call(bf16[256,128]{1,0:T(8,128)(2,1)S(1)} %collect.1.refs_0_, bf16[256,128]{1,0:T(8,128)(2,1)S(1)} %collective-permute-done.9.refs_1_), custom_call_target="tpu_custom_call" | custom-call | tf_op jit(solution)/shard_map/unfold/pallas_call | solution.py:375
  25.1 0.2 collective-permute-done.8.refs_1_
  25.4 1.3 %collective-permute-done.7.refs_0_ = bf16[256,128]{1,0:T(8,128)(2,1)S(1)} collective-permute-done((bf16[256,128]{1,0:T(8,128)(2,1)S(1)}, bf16[256,128]{1,0:T(8,128)(2,1)S(1)}, u32[]{:S(2)}, u32[]{:S(2)}) %collective-permute-start.7) | collective-permute-done | bytes 65568 | tf_op jit(solution)/shard_map/ppermute | solution.py:453
  26.7 0.0 collective-permute-done.6.refs_1_
  26.7 1.6 %collective-permute-start.10 = (bf16[512,128]{1,0:T(8,128)(2,1)S(1)}, bf16[512,128]{1,0:T(8,128)(2,1)S(1)}, u32[]{:S(2)}, u32[]{:S(2)}) collective-permute-start(bf16[512,128]{1,0:T(8,128)(2,1)S(1)} %choose.1.refs_0_.refs_1_), channel_id=1, source_target_pairs={{4,0},{5,1},{6,2},{7,3},{0,4},{1,5},{2,6},{3,7},{12,8},{13,9},{14,... | collective-permute-start | bytes 393224 | tf_op jit(solution)/shard_map/ppermute | solution.py:29
  28.3 2.2 %own_slab.1.refs_0_ = bf16[2,1,64,256]{3,2,1,0:T(8,128)(2,1)} custom-call(bf16[512,128]{1,0:T(8,128)(2,1)S(1)} %choose.1.refs_0_.refs_1_, bf16[512,128]{1,0:T(8,128)(2,1)S(1)} %choose.1.refs_0_.refs_1_, bf16[512,128]{1,0:T(8,128)(2,1)S(1)} %get-tuple-element.27.pre_ref.refs_2_, bf16[27,256,256]{2,1,0:T(8,128)(2,1)S(1)} %get-tuple-element.23.refs_3_.conv_ref, ...), custom_call_target="tpu_custom_call" | custom-call | tf_op jit(solution)/shard_map/own_slab/pallas_call | solution.py:375
  30.5 0.0 collective-permute-start.12
  30.5 0.6 %part_weight_grads.2 = (f32[1728,256]{1,0:T(8,128)S(1)}, f32[64,256]{1,0:T(8,128)S(1)}) custom-call(bf16[512,128]{1,0:T(8,128)(2,1)S(1)} %choose.1.refs_0_.refs_1_, bf16[576,128]{1,0:T(8,128)(2,1)S(1)} %get-tuple-element.29.refs_0_.refs_1_.refs_2_, bf16[576,128]{1,0:T(8,128)(2,1)S(1)} %get-tuple-element.29.refs_0_.refs_1_.refs_2_, ...), custom_call_target="tpu_custom_call" | custom-call | tf_op jit(solution)/shard_map/part_weight_grads/pallas_call | solution.py:375
  31.1 0.6 %collective-permute-done.10.block_ref = bf16[512,128]{1,0:T(8,128)(2,1)S(1)} collective-permute-done((bf16[512,128]{1,0:T(8,128)(2,1)S(1)}, bf16[512,128]{1,0:T(8,128)(2,1)S(1)}, u32[]{:S(2)}, u32[]{:S(2)}) %collective-permute-start.10) | collective-permute-done | bytes 131104 | tf_op jit(solution)/shard_map/ppermute | solution.py:29
  31.8 0.1 collective-permute-start.11
  31.8 0.0 collective-permute-done.12.refs_0_
  31.9 1.0 %part_weight_grads.3 = (f32[1728,256]{1,0:T(8,128)S(1)}, f32[64,256]{1,0:T(8,128)S(1)}) custom-call(bf16[512,128]{1,0:T(8,128)(2,1)S(1)} %collective-permute-done.12.refs_0_, bf16[512,128]{1,0:T(8,128)(2,1)S(1)} %hand_on.1.refs_1_, bf16[576,128]{1,0:T(8,128)(2,1)S(1)} %collective-permute-done.3.refs_1_.refs_2_.refs_3_, ...), custom_call_target="tpu_custom_call" | custom-call | tf_op jit(solution)/shard_map/part_weight_grads/pallas_call | solution.py:375
  32.8 0.3 collective-permute-done.11.refs_0_
  33.2 1.8 %weight_grads.1 = (f32[1728,256]{1,0:T(8,128)}, f32[64,256]{1,0:T(8,128)}) custom-call(bf16[512,128]{1,0:T(8,128)(2,1)S(1)} %collective-permute-done.11.refs_0_, bf16[576,128]{1,0:T(8,128)(2,1)S(1)} %collective-permute-done.5.refs_3_.refs_1_.refs_2_, bf16[576,128]{1,0:T(8,128)(2,1)S(1)} %collective-permute-done.5.refs_3_.refs_1_.refs_2_, ...), custom_call_target="tpu_custom_call" | custom-call | tf_op jit(solution)/shard_map/weight_grads/pallas_call | solution.py:375
  (7 shorter events, 0.0 us)
Async XLA Ops:
  1.5 5.8 %collective-permute-start = (bf16[3,1,64,256]{3,2,1,0:T(8,128)(2,1)S(1)}, bf16[3,1,64,256]{3,2,1,0:T(8,128)(2,1)S(1)}, u32[]{:S(2)}, u32[]{:S(2)}) collective-permute-start(bf16[3,1,64,256]{3,2,1,0:T(8,128)(2,1)S(1)} %outgoing.1), channel_id=1, source_target_pairs={{1,0},{0,1},{3,2},{2,3},{5,4},{4,5},{7,6},{6,7},{9,8},{8,9},{11,10... | collective-permute-start | bytes 294920 | tf_op jit(solution)/shard_map/ppermute | solution.py:29
  7.5 4.3 %collective-permute-start.1 = (bf16[256,128]{1,0:T(8,128)(2,1)S(1)}, bf16[256,128]{1,0:T(8,128)(2,1)S(1)}, u32[]{:S(2)}, u32[]{:S(2)}) collective-permute-start(bf16[256,128]{1,0:T(8,128)(2,1)S(1)} %get-tuple-element.26), channel_id=1, source_target_pairs={{8,0},{0,8},{24,16},{16,24},{9,1},{1,9},{25,17},{17,25},{10,2},{2,... | collective-permute-start | bytes 196616 | tf_op jit(solution)/shard_map/ppermute | solution.py:453
  9.5 7.6 %collective-permute-start.3 = (bf16[576,128]{1,0:T(8,128)(2,1)S(1)}, bf16[576,128]{1,0:T(8,128)(2,1)S(1)}, u32[]{:S(2)}, u32[]{:S(2)}) collective-permute-start(bf16[576,128]{1,0:T(8,128)(2,1)S(1)} %get-tuple-element.30), channel_id=1, source_target_pairs={{2,0},{3,1},{0,2},{1,3},{6,4},{7,5},{4,6},{5,7},{10,8},{11,9},{8,1... | collective-permute-start | bytes 442376 | tf_op jit(solution)/shard_map/ppermute | solution.py:29
  9.6 7.5 %collective-permute-start.4 = (bf16[576,128]{1,0:T(8,128)(2,1)S(1)}, bf16[576,128]{1,0:T(8,128)(2,1)S(1)}, u32[]{:S(2)}, u32[]{:S(2)}) collective-permute-start(bf16[576,128]{1,0:T(8,128)(2,1)S(1)} %get-tuple-element.31), channel_id=1, source_target_pairs={{4,0},{5,1},{6,2},{7,3},{0,4},{1,5},{2,6},{3,7},{12,8},{13,9},{14,... | collective-permute-start | bytes 442376 | tf_op jit(solution)/shard_map/ppermute | solution.py:29
  11.2 7.4 %collective-permute-start.5 = (bf16[576,128]{1,0:T(8,128)(2,1)S(1)}, bf16[576,128]{1,0:T(8,128)(2,1)S(1)}, u32[]{:S(2)}, u32[]{:S(2)}) collective-permute-start(bf16[576,128]{1,0:T(8,128)(2,1)S(1)} %get-tuple-element.32), channel_id=1, source_target_pairs={{6,0},{7,1},{4,2},{5,3},{2,4},{3,5},{0,6},{1,7},{14,8},{15,9},{12,... | collective-permute-start | bytes 442376 | tf_op jit(solution)/shard_map/ppermute | solution.py:29
  11.8 8.3 %collective-permute-start.2 = (bf16[256,128]{1,0:T(8,128)(2,1)S(1)}, bf16[256,128]{1,0:T(8,128)(2,1)S(1)}, u32[]{:S(2)}, u32[]{:S(2)}) collective-permute-start(bf16[256,128]{1,0:T(8,128)(2,1)S(1)} %block.2), channel_id=1, source_target_pairs={{8,0},{16,8},{24,16},{0,24},{9,1},{17,9},{25,17},{1,25},{10,2},{18... | collective-permute-start | bytes 196616 | tf_op jit(solution)/shard_map/ppermute | solution.py:453
  18.6 5.0 %collective-permute-start.9 = (bf16[256,128]{1,0:T(8,128)(2,1)S(1)}, bf16[256,128]{1,0:T(8,128)(2,1)S(1)}, u32[]{:S(2)}, u32[]{:S(2)}) collective-permute-start(bf16[256,128]{1,0:T(8,128)(2,1)S(1)} %collect.1.refs_0_), channel_id=1, source_target_pairs={{1,0},{0,1},{3,2},{2,3},{5,4},{4,5},{7,6},{6,7},{9,8},{8,9},{11,10... | collective-permute-start | bytes 196616 | tf_op jit(solution)/shard_map/ppermute | solution.py:29
  20.1 5.2 %collective-permute-start.8 = (bf16[256,128]{1,0:T(8,128)(2,1)S(1)}, bf16[256,128]{1,0:T(8,128)(2,1)S(1)}, u32[]{:S(2)}, u32[]{:S(2)}) collective-permute-start(bf16[256,128]{1,0:T(8,128)(2,1)S(1)} %block.3.refs_3_), channel_id=1, source_target_pairs={{9,0},{8,1},{1,8},{0,9},{25,16},{24,17},{17,24},{16,25},{11,2},{10... | collective-permute-start | bytes 196616 | tf_op jit(solution)/shard_map/ppermute | solution.py:492
  22.4 4.3 %collective-permute-start.7 = (bf16[256,128]{1,0:T(8,128)(2,1)S(1)}, bf16[256,128]{1,0:T(8,128)(2,1)S(1)}, u32[]{:S(2)}, u32[]{:S(2)}) collective-permute-start(bf16[256,128]{1,0:T(8,128)(2,1)S(1)} %block.3.refs_3_), channel_id=1, source_target_pairs={{8,0},{0,8},{24,16},{16,24},{9,1},{1,9},{25,17},{17,25},{10,2},{2,... | collective-permute-start | bytes 196616 | tf_op jit(solution)/shard_map/ppermute | solution.py:453
  22.4 4.3 %collective-permute-start.6 = (bf16[256,128]{1,0:T(8,128)(2,1)S(1)}, bf16[256,128]{1,0:T(8,128)(2,1)S(1)}, u32[]{:S(2)}, u32[]{:S(2)}) collective-permute-start(bf16[256,128]{1,0:T(8,128)(2,1)S(1)} %early.1.refs_0_), channel_id=1, source_target_pairs={{1,0},{0,1},{3,2},{2,3},{5,4},{4,5},{7,6},{6,7},{9,8},{8,9},{11,10... | collective-permute-start | bytes 196616 | tf_op jit(solution)/shard_map/ppermute | solution.py:29
  26.7 5.0 %collective-permute-start.10 = (bf16[512,128]{1,0:T(8,128)(2,1)S(1)}, bf16[512,128]{1,0:T(8,128)(2,1)S(1)}, u32[]{:S(2)}, u32[]{:S(2)}) collective-permute-start(bf16[512,128]{1,0:T(8,128)(2,1)S(1)} %choose.1.refs_0_.refs_1_), channel_id=1, source_target_pairs={{4,0},{5,1},{6,2},{7,3},{0,4},{1,5},{2,6},{3,7},{12,8},{13,9},{14,... | collective-permute-start | bytes 393224 | tf_op jit(solution)/shard_map/ppermute | solution.py:29
  30.5 1.4 %collective-permute-start.12 = (bf16[512,128]{1,0:T(8,128)(2,1)S(1)}, bf16[512,128]{1,0:T(8,128)(2,1)S(1)}, u32[]{:S(2)}, u32[]{:S(2)}) collective-permute-start(bf16[512,128]{1,0:T(8,128)(2,1)S(1)} %choose.1.refs_0_.refs_1_), channel_id=1, source_target_pairs={{2,0},{3,1},{0,2},{1,3},{6,4},{7,5},{4,6},{5,7},{10,8},{11,9},{8,1... | collective-permute-start | bytes 393224 | tf_op jit(solution)/shard_map/ppermute | solution.py:29
  31.8 1.4 %collective-permute-start.11 = (bf16[512,128]{1,0:T(8,128)(2,1)S(1)}, bf16[512,128]{1,0:T(8,128)(2,1)S(1)}, u32[]{:S(2)}, u32[]{:S(2)}) collective-permute-start(bf16[512,128]{1,0:T(8,128)(2,1)S(1)} %hand_on.1.refs_1_), channel_id=1, source_target_pairs={{2,0},{3,1},{0,2},{1,3},{6,4},{7,5},{4,6},{5,7},{10,8},{11,9},{8,1... | collective-permute-start | bytes 393224 | tf_op jit(solution)/shard_map/ppermute | solution.py:29
